TPU v7x, 128 devices: a whole 4x4x4 slice. The times are simulated.
128 devices in a mesh: expert: 64 (over x, z, y_lo, core), dp: 2 (over y_hi).
Axes of the slice: x: 4, y: 4 (y_hi: 2, y_lo: 2; y = y_hi * 2 + y_lo), z: 4, core: 2. Of those that a mesh axis runs over, the one named last changes fastest.
Arguments:
- tokens: bfloat16 [16384, 6144], P(('expert', 'dp')), may hold values from -6 to 6
- cotangent: bfloat16 [16384, 6144], P(('expert', 'dp')), may hold values from -0.59765625 to 0.59765625
- gate_probs: float32 [16384, 2], P(('expert', 'dp')), may hold values from 0.2 to 1
- routes: int32 [16384, 2], P(('expert', 'dp')), may hold values from 0 to 63, all different within a row; in each aligned block of 128 rows (0 to 127, 128 to 255, ...) at most 6 rows name the same one
- placement: int32 [64], replicated, may hold values from 0 to 63, each once
- weights: bfloat16 [64, 6144, 384], P('expert'), may hold values from -1.1 to 1.1, as said below
- first_moment: bfloat16 [64, 6144, 384], P('expert', 'dp'), may hold values from -1.796875 to 1.796875
- second_moment: bfloat16 [64, 6144, 384], P('expert', 'dp'), may hold values from 0.0099487305 to 1
Outputs:
- mixed: bfloat16 [16384, 6144], P(('expert', 'dp'))
- token_grad: bfloat16 [16384, 6144], P(('expert', 'dp'))
- first_new: bfloat16 [64, 6144, 384], P('expert', 'dp')
- second_new: bfloat16 [64, 6144, 384], P('expert', 'dp')
- adam_step: bfloat16 [64, 6144, 384], P('expert', 'dp')
Inputs may be any that keep to these rules, and one draw needn't show every extreme that they name: `routes`: each row names 2 different experts; among the rows of one device no expert is named more than 6 times, and that count is reached. `placement`: a permutation of the experts. `weights`: gate and up columns spread about 1/sqrt(6144), down columns about 1/sqrt(128).
All inputs are finite; a program needn't handle non-finite values.
Results may differ from a plain program's by a relative error of at most 0.018.
Values may be sent and summed in bfloat16 or wider, within the bound.
No kernel may reach another device: no remote copies, remote signals or barrier semaphores. Data moves between devices by JAX's collectives and lax.ppermute only.
A program may use at most 192 MiB of HBM per device.

v0:
```python
import jax
import jax.numpy as jnp
from jax import lax
from jax.sharding import PartitionSpec as P


def expert_pass(weight, row_data, row_cot):
    hidden = weight.shape[1] // 3
    front_both = jnp.dot(row_data, weight[:, : 2 * hidden], preferred_element_type=jnp.float32)
    gate_pre = front_both[:, :hidden]
    upward = front_both[:, hidden:]
    sigmoid_gate = jax.nn.sigmoid(gate_pre)
    active = gate_pre * sigmoid_gate
    inner_act = (active * upward).astype(jnp.bfloat16)
    down_cols = weight[:, 2 * hidden :]
    output = lax.dot_general(
        inner_act, down_cols, (((1,), (1,)), ((), ())), preferred_element_type=jnp.float32
    ).astype(jnp.bfloat16)
    inner_grad = jnp.dot(row_cot, down_cols, preferred_element_type=jnp.float32)
    slope_term = sigmoid_gate * (1.0 + gate_pre * (1.0 - sigmoid_gate))
    pre_grad = jnp.concatenate(
        [inner_grad * upward * slope_term, inner_grad * active], axis=1
    ).astype(jnp.bfloat16)
    grad_front = lax.dot_general(
        row_data, pre_grad, (((0,), (0,)), ((), ())), preferred_element_type=jnp.float32
    )
    grad_down = lax.dot_general(
        row_cot, inner_act, (((0,), (0,)), ((), ())), preferred_element_type=jnp.float32
    )
    row_grad = lax.dot_general(
        pre_grad,
        weight[:, : 2 * hidden],
        (((1,), (1,)), ((), ())),
        preferred_element_type=jnp.float32,
    ).astype(jnp.bfloat16)
    return (output, row_grad, jnp.concatenate([grad_front, grad_down], axis=1))


def adamw(gradient, first_in, second_in, current):
    first_next = 0.9 * first_in.astype(jnp.float32) + 0.1 * gradient
    second_next = 0.95 * second_in.astype(jnp.float32) + 0.05 * gradient * gradient
    step_dir = first_next / (jnp.sqrt(second_next) + 1e-08) + 0.1 * current
    return (
        first_next.astype(jnp.bfloat16),
        second_next.astype(jnp.bfloat16),
        step_dir.astype(jnp.bfloat16),
    )


def relocate(array_one, array_two, array_three, new_order):
    spread_one, spread_two, spread_three = (
        lax.all_to_all(array_one, "expert", split_axis=1, concat_axis=0, tiled=True),
        lax.all_to_all(array_two, "expert", split_axis=1, concat_axis=0, tiled=True),
        lax.all_to_all(array_three, "expert", split_axis=1, concat_axis=0, tiled=True),
    )
    order_one = jnp.take(spread_one, new_order, axis=0)
    order_two = jnp.take(spread_two, new_order, axis=0)
    order_three = jnp.take(spread_three, new_order, axis=0)
    return (
        lax.all_to_all(order_one, "expert", split_axis=0, concat_axis=1, tiled=True),
        lax.all_to_all(order_two, "expert", split_axis=0, concat_axis=1, tiled=True),
        lax.all_to_all(order_three, "expert", split_axis=0, concat_axis=1, tiled=True),
    )


def local(tokens, cotangent, gate_probs, routes, placement, weights, first_moment, second_moment):
    expert_count = lax.axis_size("expert")
    tok_rows, model_width = tokens.shape
    top_count = routes.shape[1]
    capacity = max(2, (3 * tok_rows * top_count + 2 * expert_count - 1) // (2 * expert_count))
    assigned = tok_rows * top_count
    total_rows = expert_count * capacity
    expert_ids = routes.reshape(-1)
    labels = jnp.arange(expert_count, dtype=jnp.int32)
    onehot = (expert_ids[:, None] == labels[None, :]).astype(jnp.int32)
    earlier = jnp.sum((jnp.cumsum(onehot, axis=0) - onehot) * onehot, axis=1)
    inverse = jnp.sum(
        labels[None, :] * (placement[None, :] == labels[:, None]).astype(jnp.int32), axis=1
    )
    target = jnp.sum(onehot * placement[None, :], axis=1)
    weights, first_moment, second_moment = relocate(weights, first_moment, second_moment, inverse)
    slot_of = target * capacity + earlier
    filler = (
        jnp.full((total_rows,), assigned, jnp.int32)
        .at[slot_of]
        .set(jnp.arange(assigned, dtype=jnp.int32))
    )
    row_token = filler // top_count
    token_pad = jnp.concatenate([tokens, jnp.zeros((1, model_width), tokens.dtype)], axis=0)
    cot_pad = jnp.concatenate([cotangent, jnp.zeros((1, model_width), cotangent.dtype)], axis=0)
    probs_flat = gate_probs.reshape(-1)
    probs_pad = jnp.concatenate([probs_flat, jnp.zeros((1,), jnp.float32)])
    send_rows = jnp.take(token_pad, row_token, axis=0)
    slot_prob = jnp.take(probs_pad, filler)
    send_cot = (
        slot_prob[:, None] * jnp.take(cot_pad, row_token, axis=0).astype(jnp.float32)
    ).astype(jnp.bfloat16)
    recv_rows, recv_cot = (
        lax.all_to_all(send_rows, "expert", split_axis=0, concat_axis=0, tiled=True),
        lax.all_to_all(send_cot, "expert", split_axis=0, concat_axis=0, tiled=True),
    )
    expert_out, row_grad, gradient = expert_pass(weights[0], recv_rows, recv_cot)
    back_out, back_grad = (
        lax.all_to_all(expert_out, "expert", split_axis=0, concat_axis=0, tiled=True),
        lax.all_to_all(row_grad, "expert", split_axis=0, concat_axis=0, tiled=True),
    )
    picked_out = jnp.take(back_out, slot_of, axis=0).astype(jnp.float32) * probs_flat[:, None]
    mixed = jnp.sum(picked_out.reshape(tok_rows, top_count, model_width), axis=1).astype(
        jnp.bfloat16
    )
    picked_grad = jnp.take(back_grad, slot_of, axis=0).astype(jnp.float32)
    token_grad = jnp.sum(picked_grad.reshape(tok_rows, top_count, model_width), axis=1).astype(
        jnp.bfloat16
    )
    grad_share = lax.psum_scatter(
        gradient.astype(jnp.bfloat16), "dp", scatter_dimension=0, tiled=True
    ).astype(jnp.float32)
    half_rows = grad_share.shape[0]
    current = lax.dynamic_slice_in_dim(
        weights[0], lax.axis_index("dp") * half_rows, half_rows, 0
    ).astype(jnp.float32)
    first_new, second_new, adam_step = adamw(grad_share, first_moment[0], second_moment[0], current)
    first_new = first_new[None]
    second_new = second_new[None]
    adam_step = adam_step[None]
    return (mixed, token_grad, first_new, second_new, adam_step)


def solution(mesh):
    in_specs = (
        P(("expert", "dp"), None),
        P(("expert", "dp"), None),
        P(("expert", "dp"), None),
        P(("expert", "dp"), None),
        P(),
        P("expert", None, None),
        P("expert", "dp", None),
        P("expert", "dp", None),
    )
    out_specs = (
        P(("expert", "dp"), None),
        P(("expert", "dp"), None),
        P("expert", "dp", None),
        P("expert", "dp", None),
        P("expert", "dp", None),
    )
    return jax.shard_map(local, mesh=mesh, in_specs=in_specs, out_specs=out_specs, check_vma=False)
```

profile of v0, /device:TPU:6, one launch (start us, length us, event | category | flops | bytes accessed | tf_op | source)
XLA Modules:
  0.0 908.2 jit_solution(12697132800031591376)
XLA Ops:
  13.3 50.5 %reduce.5 = bf16[3072,384]{1,0:T(8,128)(2,1)S(1)} reduce(bf16[3072,1,384]{2,1,0:T(2,128)(2,1)} %bitcast.65, bf16[]{:T(256)} %broadcast.157), dimensions={1}, to_apply=%bitcast.54.reduce_sub_computation | reduce | bytes 4718594
  66.0 10.6 %all-to-all-start.6 = ((bf16[64,2,9216]{2,1,0:T(2,128)(2,1)}), bf16[64,2,9216]{2,1,0:T(2,128)(2,1)S(1)}, u32[]{:S(2)}, u32[]{:S(2)}) async-start(bf16[64,2,9216]{2,1,0:T(2,128)(2,1)} %reshape.240), calls=%async_computation.6 | async-start | bytes 4718592 | tf_op jit(solution)/shard_map/all_to_all | solution.py:53
  83.7 52.0 %reduce.4 = bf16[3072,384]{1,0:T(8,128)(2,1)} reduce(bf16[3072,1,384]{2,1,0:T(2,128)(2,1)} %bitcast.70, bf16[]{:T(256)} %broadcast.157), dimensions={1}, to_apply=%bitcast.53.reduce_sub_computation | reduce | bytes 4718594
  145.2 9.3 %all-to-all-start.8 = ((bf16[64,2,9216]{2,1,0:T(2,128)(2,1)}), bf16[64,2,9216]{2,1,0:T(2,128)(2,1)}, u32[]{:S(2)}, u32[]{:S(2)}) async-start(bf16[64,2,9216]{2,1,0:T(2,128)(2,1)} %reshape.242), calls=%async_computation.9 | async-start | bytes 4718592 | tf_op jit(solution)/shard_map/all_to_all | solution.py:54
  171.8 7.8 all_to_all.89
  211.1 63.0 %all-to-all-done.4 = bf16[64,6,6144]{2,1,0:T(8,128)(2,1)} async-done(((bf16[64,6,6144]{2,1,0:T(8,128)(2,1)}), bf16[64,6,6144]{2,1,0:T(8,128)(2,1)}, u32[]{:S(2)}, u32[]{:S(2)}) %all-to-all-start.4) | async-done | bytes 4718624 | tf_op jit(solution)/shard_map/all_to_all | solution.py:100
  274.1 8.9 all-to-all-start
  283.0 9.6 %copy.74 = bf16[1,6144,384]{2,0,1:T(2,128)(2,1)} copy(bf16[1,6144,384]{2,1,0:T(8,128)(2,1)} %param.19) | data formatting | bytes 9437184 | tf_op args[5]
  292.7 101.9 %reduce.3 = bf16[6144,384]{1,0:T(8,128)(2,1)} reduce(bf16[6144,1,384]{2,1,0:T(2,128)(2,1)} %bitcast.55, bf16[]{:T(256)} %broadcast.157), dimensions={1}, to_apply=%bitcast.52.reduce_sub_computation | reduce | bytes 9437186
  394.6 10.4 %reshape.238 = bf16[64,2,18432]{2,1,0:T(2,128)(2,1)} reshape(bf16[6144,384]{1,0:T(8,128)(2,1)} %reduce.3) | data formatting | bytes 9437184
  404.9 9.1 %all-to-all-start.1 = ((bf16[64,2,18432]{2,1,0:T(2,128)(2,1)}), bf16[64,2,18432]{2,1,0:T(2,128)(2,1)}, u32[]{:S(2)}, u32[]{:S(2)}) async-start(bf16[64,2,18432]{2,1,0:T(2,128)(2,1)} %reshape.238), calls=%async_computation.1 | async-start | bytes 9437184 | tf_op jit(solution)/shard_map/all_to_all | solution.py:52
  423.8 10.5 %reshape.243 = bf16[3072,1,384]{2,1,0:T(2,128)(2,1)} reshape(bf16[64,2,9216]{2,1,0:T(2,128)(2,1)} %all-to-all-done.8) | data formatting | bytes 4718592
  449.2 25.7 %all-to-all-done.1 = bf16[64,2,18432]{2,1,0:T(2,128)(2,1)} async-done(((bf16[64,2,18432]{2,1,0:T(2,128)(2,1)}), bf16[64,2,18432]{2,1,0:T(2,128)(2,1)}, u32[]{:S(2)}, u32[]{:S(2)}) %all-to-all-start.1) | async-done | bytes 4718624 | tf_op jit(solution)/shard_map/all_to_all | solution.py:52
  474.9 8.1 all-to-all-start.7
  483.0 20.2 %reshape.239 = bf16[6144,1,384]{2,1,0:T(2,128)(2,1)} reshape(bf16[64,2,18432]{2,1,0:T(2,128)(2,1)} %all-to-all-done.1) | data formatting | bytes 9437184
  520.6 66.9 %all_to_all.111 = bf16[64,96,384]{2,1,0:T(8,128)(2,1)} all-to-all(bf16[64,96,384]{2,1,0:T(8,128)(2,1)} %broadcast_select_fusion.1), channel_id=1, replica_groups=mesh['expert'=64,'dp'=2] {'expert'}, dimensions={0} | all-to-all | bytes 9437184 | tf_op jit(solution)/shard_map/all_to_all | solution.py:60
  587.5 7.7 all-to-all-start.9
  595.2 7.8 all_to_all.91
  603.1 7.9 all_to_all.82
  629.7 9.0 all-to-all-start.5
  653.9 7.9 all_to_all.86
  661.8 71.5 %all-to-all-done.5 = bf16[64,6,6144]{2,1,0:T(8,128)(2,1)} async-done(((bf16[64,6,6144]{2,1,0:T(8,128)(2,1)}), bf16[64,6,6144]{2,1,0:T(8,128)(2,1)}, u32[]{:S(2)}, u32[]{:S(2)}) %all-to-all-start.5) | async-done | bytes 4718624 | tf_op jit(solution)/shard_map/all_to_all | solution.py:105
  733.3 10.3 %all-to-all-start.3 = ((bf16[64,6,6144]{2,1,0:T(8,128)(2,1)}), bf16[64,6,6144]{2,1,0:T(8,128)(2,1)}, u32[]{:S(2)}, u32[]{:S(2)}) async-start(bf16[64,6,6144]{2,1,0:T(8,128)(2,1)} %all_to_all.86), calls=%async_computation.3 | async-start | bytes 12582912 | tf_op jit(solution)/shard_map/all_to_all | solution.py:104
  767.0 7.8 all_to_all.94
  774.8 8.4 gather_fusion.5
  791.5 9.7 %reduce = bf16[128,6144]{1,0:T(8,128)(2,1)} reduce(bf16[128,2,6144]{2,1,0:T(2,128)(2,1)S(1)} %reshape.142, bf16[]{:T(256)} %constant.53.clone.1), dimensions={1}, to_apply=%region_7.10.clone | reduce | flops 786432 | bytes 4718594 | tf_op jit(solution)/shard_map/reduce_sum | solution.py:112
  801.3 40.2 %all-to-all-done.3 = bf16[64,6,6144]{2,1,0:T(8,128)(2,1)} async-done(((bf16[64,6,6144]{2,1,0:T(8,128)(2,1)}), bf16[64,6,6144]{2,1,0:T(8,128)(2,1)}, u32[]{:S(2)}, u32[]{:S(2)}) %all-to-all-start.3) | async-done | bytes 4718624 | tf_op jit(solution)/shard_map/all_to_all | solution.py:104
  841.5 8.2 all_to_all.88
  849.7 8.4 gather_fusion.3
  862.0 8.3 reshape.141
  870.3 11.8 %reduce_sum.51 = bf16[128,6144]{1,0:T(8,128)(2,1)} reduce(f32[128,2,6144]{2,1,0:T(2,128)} %reshape.141, f32[]{:T(128)} %constant.76.clone.1), dimensions={1}, to_apply=%region_6.9 | reduce | flops 786432 | bytes 7864324 | tf_op jit(solution)/shard_map/reduce_sum | solution.py:108
  882.1 7.9 fusion.9
  (111 shorter events, 196.0 us)
Async XLA Ops:
  63.8 12.8 %copy-start.10 = (s32[128,2]{0,1:T(2,128)S(1)}, s32[128,2]{0,1:T(2,128)}, u32[]{:S(2)}) copy-start(s32[128,2]{0,1:T(2,128)} %param.17) | copy-start | bytes 3076
  63.8 14.0 %copy-start.11 = (f32[128,2]{0,1:T(2,128)S(1)}, f32[128,2]{0,1:T(2,128)}, u32[]{:S(2)}) copy-start(f32[128,2]{0,1:T(2,128)} %param.16) | copy-start | bytes 3076
  66.0 77.8 %all-to-all-start.6 = ((bf16[64,2,9216]{2,1,0:T(2,128)(2,1)}), bf16[64,2,9216]{2,1,0:T(2,128)(2,1)S(1)}, u32[]{:S(2)}, u32[]{:S(2)}) async-start(bf16[64,2,9216]{2,1,0:T(2,128)(2,1)} %reshape.240), calls=%async_computation.6 | async-start | bytes 4718592 | tf_op jit(solution)/shard_map/all_to_all | solution.py:53
  78.1 76.4 %copy-start.7 = (f32[256]{0:T(256)}, f32[256]{0:T(256)S(1)}, u32[]{:S(2)}) copy-start(f32[256]{0:T(256)S(1)} %mul.117) | copy-start | bytes 3076
  83.7 58.0 %copy-start.12 = (s32[64]{0:T(128)S(1)}, s32[64]{0:T(128)}, u32[]{:S(2)}) copy-start(s32[64]{0:T(128)} %param.18) | copy-start | bytes 772
  143.8 1.4 copy-start.1
  145.2 39.7 %all-to-all-start.8 = ((bf16[64,2,9216]{2,1,0:T(2,128)(2,1)}), bf16[64,2,9216]{2,1,0:T(2,128)(2,1)}, u32[]{:S(2)}, u32[]{:S(2)}) async-start(bf16[64,2,9216]{2,1,0:T(2,128)(2,1)} %reshape.242), calls=%async_computation.9 | async-start | bytes 4718592 | tf_op jit(solution)/shard_map/all_to_all | solution.py:54
  179.6 13.0 %copy-start.6 = (bf16[128,6144]{1,0:T(8,128)(2,1)S(1)}, bf16[128,6144]{1,0:T(8,128)(2,1)}, u32[]{:S(2)}) copy-start(bf16[128,6144]{1,0:T(8,128)(2,1)} %param.14) | copy-start | bytes 4718596
  184.9 89.2 %all-to-all-start.4 = ((bf16[64,6,6144]{2,1,0:T(8,128)(2,1)}), bf16[64,6,6144]{2,1,0:T(8,128)(2,1)}, u32[]{:S(2)}, u32[]{:S(2)}) async-start(bf16[64,6,6144]{2,1,0:T(8,128)(2,1)} %all_to_all.89), calls=%async_computation.4 | async-start | bytes 12582912 | tf_op jit(solution)/shard_map/all_to_all | solution.py:100
  274.1 130.8 %all-to-all-start = ((bf16[64,6,6144]{2,1,0:T(8,128)(2,1)}), bf16[64,6,6144]{2,1,0:T(8,128)(2,1)}, u32[]{:S(2)}, u32[]{:S(2)}) async-start(bf16[64,6,6144]{2,1,0:T(8,128)(2,1)} %all_to_all.80), calls=%async_computation | async-start | bytes 12582912 | tf_op jit(solution)/shard_map/all_to_all | solution.py:99
  404.9 9.3 %copy-start.2 = (bf16[64,2,9216]{2,1,0:T(2,128)(2,1)S(1)}, bf16[64,2,9216]{2,1,0:T(2,128)(2,1)}, u32[]{:S(2)}) copy-start(bf16[64,2,9216]{2,1,0:T(2,128)(2,1)} %copy-done.1) | copy-start | bytes 7077892
  404.9 69.9 %all-to-all-start.1 = ((bf16[64,2,18432]{2,1,0:T(2,128)(2,1)}), bf16[64,2,18432]{2,1,0:T(2,128)(2,1)}, u32[]{:S(2)}, u32[]{:S(2)}) async-start(bf16[64,2,18432]{2,1,0:T(2,128)(2,1)} %reshape.238), calls=%async_computation.1 | async-start | bytes 9437184 | tf_op jit(solution)/shard_map/all_to_all | solution.py:52
  440.7 4.1 copy-start.5
  474.9 45.8 %all-to-all-start.7 = ((bf16[64,48,384]{2,1,0:T(8,128)(2,1)}), bf16[64,48,384]{2,1,0:T(8,128)(2,1)S(1)}, u32[]{:S(2)}, u32[]{:S(2)}) async-start(bf16[64,48,384]{2,1,0:T(8,128)(2,1)} %get-tuple-element.46), calls=%async_computation.7 | async-start | bytes 4718592 | tf_op jit(solution)/shard_map/all_to_all | solution.py:61
  587.5 42.1 %all-to-all-start.9 = ((bf16[64,48,384]{2,1,0:T(8,128)(2,1)}), bf16[64,48,384]{2,1,0:T(8,128)(2,1)}, u32[]{:S(2)}, u32[]{:S(2)}) async-start(bf16[64,48,384]{2,1,0:T(8,128)(2,1)} %get-tuple-element.45), calls=%async_computation.10 | async-start | bytes 4718592 | tf_op jit(solution)/shard_map/all_to_all | solution.py:62
  603.1 13.2 %slice-start = ((s8[4718592]{0:T(1024)(128)(4,1)}), s8[524288]{0:T(1024)(128)(4,1)S(1)}, s32[]{:S(2)}) async-start(s8[4718592]{0:T(1024)(128)(4,1)} %bitcast.60), calls=%async_computation.12 | async-start | bytes 1048576
  610.9 5.3 slice-start.1
  610.9 5.9 copy-start
  629.7 103.6 %all-to-all-start.5 = ((bf16[64,6,6144]{2,1,0:T(8,128)(2,1)}), bf16[64,6,6144]{2,1,0:T(8,128)(2,1)}, u32[]{:S(2)}, u32[]{:S(2)}) async-start(bf16[64,6,6144]{2,1,0:T(8,128)(2,1)} %all_to_all.92), calls=%async_computation.5 | async-start | bytes 12582912 | tf_op jit(solution)/shard_map/all_to_all | solution.py:105
  638.7 243.5 %reduce-scatter.2.cloned.1.call-start = ((), (), s32[]{:S(2)}) async-start(), calls=%async_computation.11 | async-start | bytes 7077888 | tf_op jit(solution)/shard_map/reduce_scatter | solution.py:115
  733.3 108.2 %all-to-all-start.3 = ((bf16[64,6,6144]{2,1,0:T(8,128)(2,1)}), bf16[64,6,6144]{2,1,0:T(8,128)(2,1)}, u32[]{:S(2)}, u32[]{:S(2)}) async-start(bf16[64,6,6144]{2,1,0:T(8,128)(2,1)} %all_to_all.86), calls=%async_computation.3 | async-start | bytes 12582912 | tf_op jit(solution)/shard_map/all_to_all | solution.py:104
  774.8 8.4 copy-start.9
  849.7 8.4 copy-start.8
  870.3 11.8 %copy-start.3 = (bf16[3072,384]{0,1:T(8,128)(2,1)S(1)}, bf16[3072,384]{0,1:T(8,128)(2,1)}, u32[]{:S(2)}) copy-start(bf16[3072,384]{0,1:T(8,128)(2,1)} %copy.68) | copy-start | bytes 7077892
  890.0 8.7 copy-start.4
Sparse Core Ops, SparseCore 0:
  649.0 186.9 reduce-scatter.1
where the time goes:
time: 920 us; the launch traced here: 908 us
  other arithmetic  272 us (30%)
  local copies, waits for them, and re-layouts  245 us (27%)
  waiting for transfers between devices  206 us (22%)
  starting transfers between devices  81.1 us (9%)
  blocking collectives  66.9 us (7%)
  matrix products  22.9 us (2%)
  between operations  14.7 us (2%)
    unnamed x4, other arithmetic  204 us
    unnamed x49, local copies, waits for them, and re-layouts  107 us
    all_to_all x1, waiting for transfers between devices, local(): lax.all_to_all(row_grad, 'expert', split_axis=0, concat_axis=0, tiled=True)  71.5 us
    all_to_all x1, blocking collectives, relocate(): lax.all_to_all(order_one, 'expert', split_axis=0, concat_axis=1, tiled=True)  66.9 us
    all_to_all x1, waiting for transfers between devices, local(): lax.all_to_all(send_cot, 'expert', split_axis=0, concat_axis=0, tiled=True)  63 us
    all_to_all x1, waiting for transfers between devices, local(): lax.all_to_all(expert_out, 'expert', split_axis=0, concat_axis=0, tiled=T...  40.2 us
    all_to_all x1, waiting for transfers between devices, relocate(): lax.all_to_all(array_one, 'expert', split_axis=1, concat_axis=0, tiled=True)  25.7 us
  transfers between devices with their start and end apart: 10, of which 5 were waited for; matrix products, arithmetic and copies ran while one was open for 44% of the time, Pallas kernels for 0%

commit v1 on v0

v1 whole, which is shorter than its diff:
```python
import functools
import jax
import jax.numpy as jnp
from jax import lax
from jax.experimental import pallas as pl
from jax.experimental.pallas import tpu as pltpu
from jax.sharding import PartitionSpec as P

BF = jnp.bfloat16
F32 = jnp.float32
VMEM = 48 * 1024 * 1024
TILE = 512


def row_parts(rows, first, cap):
    per = 4 * cap
    r = lax.broadcasted_iota(jnp.int32, (rows, 128), 0) + first
    e = r // per
    q = r - e * per
    h = q // (2 * cap)
    q = q - h * (2 * cap)
    a = q // cap
    s = q - a * cap
    return e * cap + s, h, a


def dispatch_kernel(cap, slot_ref, prob_ref, t0, t1, c0, c1, out_ref, low, high, scale):
    rows = out_ref.shape[0]

    @pl.when(pl.program_id(0) == 0)
    def _():
        ident, h, a = row_parts(rows, 0, cap)
        hit0 = ident == slot_ref[0:1, :]
        hit1 = ident == slot_ref[1:2, :]
        hit = hit0 | hit1
        prob = jnp.where(hit0, prob_ref[0:1, :], 0.0) + jnp.where(hit1, prob_ref[1:2, :], 0.0)
        prob = jnp.sum(prob, axis=1, keepdims=True)
        scale[...] = jnp.where(a == 0, 1.0, prob)
        for ref, half in ((low, 0), (high, 1)):
            for kind in (0, 1):
                keep = hit & (h == half) & (a == kind)
                ref[:, kind * 128 : (kind + 1) * 128] = jnp.where(keep, 1.0, 0.0).astype(BF)

    x0 = jnp.concatenate([t0[...], c0[...]], axis=0)
    x1 = jnp.concatenate([t1[...], c1[...]], axis=0)
    step = rows // 4
    for i in range(4):
        part = slice(i * step, (i + 1) * step)
        acc = jnp.dot(low[part, :], x0, preferred_element_type=F32)
        acc = acc + jnp.dot(high[part, :], x1, preferred_element_type=F32)
        out_ref[part, :] = (acc * scale[part, 0:1]).astype(BF)


def dispatch(slots, probs, tokens, cotangent, experts, cap):
    tok, width = tokens.shape
    half = width // 2
    tiles = half // TILE
    rows = experts * cap * 4
    small = pl.BlockSpec((2, tok), lambda i: (0, 0))
    left = pl.BlockSpec((tok, TILE), lambda i: (0, i))
    right = pl.BlockSpec((tok, TILE), lambda i: (0, i + tiles))
    return pl.pallas_call(
        functools.partial(dispatch_kernel, cap),
        grid=(tiles,),
        in_specs=[small, small, left, right, left, right],
        out_specs=pl.BlockSpec((rows, TILE), lambda i: (0, i)),
        out_shape=jax.ShapeDtypeStruct((rows, half), BF),
        scratch_shapes=[
            pltpu.VMEM((rows, 2 * tok), BF),
            pltpu.VMEM((rows, 2 * tok), BF),
            pltpu.VMEM((rows, 128), F32),
        ],
        compiler_params=pltpu.CompilerParams(vmem_limit_bytes=VMEM),
        cost_estimate=pl.CostEstimate(
            flops=2 * rows * 2 * tok * width, bytes_accessed=16 * 1024 * 1024, transcendentals=0
        ),
        name="dispatch",
    )(slots, probs, tokens, tokens, cotangent, cotangent)


def order_matrix(group, cap, inverse):
    n = group * cap * 4
    i = lax.broadcasted_iota(jnp.int32, (n, n), 1 if inverse else 0)
    j = lax.broadcasted_iota(jnp.int32, (n, n), 0 if inverse else 1)
    hk = i // (group * cap)
    rest = i - hk * (group * cap)
    src = rest // cap
    slot = rest - src * cap
    return jnp.where(src * (4 * cap) + hk * cap + slot == j, 1.0, 0.0).astype(BF)


def expert_kernel(
    cap, group, tiles, rank_ref, recv_ref, w_ref, out_ref, mine_ref, theirs_ref,
    rows_x, rows_c, front, down, inner, pre, fore, back
):
    i = pl.program_id(0)
    n = group * cap
    span = 4 * n
    sets = recv_ref.shape[0] // span
    hidden = inner.shape[1]

    @pl.when(i == 0)
    def _():
        fore[...] = order_matrix(group, cap, False)
        back[...] = order_matrix(group, cap, True)
        front[...] = jnp.zeros_like(front)
        down[...] = jnp.zeros_like(down)

    @pl.when(i < tiles)
    def _():
        for g in range(sets):
            got = jnp.dot(
                fore[...], recv_ref[g * span : (g + 1) * span, :], preferred_element_type=F32
            ).astype(BF)
            at = slice(g * n, (g + 1) * n)
            for h in range(2):
                rows_x[i, h, at, :] = got[2 * h * n : (2 * h + 1) * n]
                rows_c[i, h, at, :] = got[(2 * h + 1) * n : (2 * h + 2) * n]
        for h in range(2):
            front[...] += jnp.dot(
                rows_x[i, h], w_ref[h, :, : 2 * hidden], preferred_element_type=F32
            )
            down[...] += jnp.dot(
                rows_c[i, h], w_ref[h, :, 2 * hidden :], preferred_element_type=F32
            )

    @pl.when(i == tiles - 1)
    def _():
        gate = front[:, :hidden]
        up = front[:, hidden:]
        sig = jax.nn.sigmoid(gate)
        active = gate * sig
        inner[...] = (active * up).astype(BF)
        grad = down[...]
        slope = sig * (1.0 + gate * (1.0 - sig))
        pre[:, :hidden] = (grad * up * slope).astype(BF)
        pre[:, hidden:] = (grad * active).astype(BF)

    @pl.when(i >= tiles)
    def _():
        c = i - tiles
        contract = (((1,), (1,)), ((), ()))
        lead = (((0,), (0,)), ((), ()))
        made = []
        for h in range(2):
            made.append(
                lax.dot_general(
                    inner[...], w_ref[h, :, 2 * hidden :], contract, preferred_element_type=F32
                ).astype(BF)
            )
            made.append(
                lax.dot_general(
                    pre[...], w_ref[h, :, : 2 * hidden], contract, preferred_element_type=F32
                ).astype(BF)
            )
        for g in range(sets):
            stack = jnp.concatenate([m[g * n : (g + 1) * n] for m in made], axis=0)
            out_ref[g * span : (g + 1) * span, :] = jnp.dot(
                back[...], stack, preferred_element_type=F32
            ).astype(BF)
        parts = []
        for h in range(2):
            parts.append(
                (
                    lax.dot_general(rows_x[c, h], pre[...], lead, preferred_element_type=F32),
                    lax.dot_general(rows_c[c, h], inner[...], lead, preferred_element_type=F32),
                )
            )
        first = rank_ref[0] == 0
        for k, at in ((0, slice(0, 2 * hidden)), (1, slice(2 * hidden, 3 * hidden))):
            mine_ref[:, at] = jnp.where(first, parts[0][k], parts[1][k]).astype(BF)
            theirs_ref[:, at] = jnp.where(first, parts[1][k], parts[0][k]).astype(BF)


def expert_call(rank, recv, weight, cap):
    total, half = recv.shape
    columns = weight.shape[1]
    hidden = columns // 3
    tiles = half // TILE
    rows = total // 4
    group = 8
    n = group * cap * 4
    late = lambda i: jnp.maximum(i - tiles, 0)
    return pl.pallas_call(
        functools.partial(expert_kernel, cap, group, tiles),
        grid=(2 * tiles,),
        in_specs=[
            pl.BlockSpec(memory_space=pltpu.SMEM),
            pl.BlockSpec((total, TILE), lambda i: (0, jnp.minimum(i, tiles - 1))),
            pl.BlockSpec((2, TILE, columns), lambda i: (0, lax.rem(i, tiles), 0)),
        ],
        out_specs=[
            pl.BlockSpec((total, TILE), lambda i: (0, late(i))),
            pl.BlockSpec((TILE, columns), lambda i: (late(i), 0)),
            pl.BlockSpec((TILE, columns), lambda i: (late(i), 0)),
        ],
        out_shape=[
            jax.ShapeDtypeStruct((total, half), BF),
            jax.ShapeDtypeStruct((half, columns), BF),
            jax.ShapeDtypeStruct((half, columns), BF),
        ],
        scratch_shapes=[
            pltpu.VMEM((tiles, 2, rows, TILE), BF),
            pltpu.VMEM((tiles, 2, rows, TILE), BF),
            pltpu.VMEM((rows, 2 * hidden), F32),
            pltpu.VMEM((rows, hidden), F32),
            pltpu.VMEM((rows, hidden), BF),
            pltpu.VMEM((rows, 2 * hidden), BF),
            pltpu.VMEM((n, n), BF),
            pltpu.VMEM((n, n), BF),
        ],
        compiler_params=pltpu.CompilerParams(vmem_limit_bytes=VMEM),
        cost_estimate=pl.CostEstimate(
            flops=10 * 10**9, bytes_accessed=34 * 1024 * 1024, transcendentals=rows * hidden
        ),
        name="expert_pass",
    )(rank, recv, weight.reshape(2, half, columns))


def combine_kernel(cap, tiles, slot_ref, prob_ref, back_ref, mixed_ref, grad_ref, pick):
    total = back_ref.shape[0]
    tok = mixed_ref.shape[0]
    i = pl.program_id(0)

    @pl.when(i == 0)
    def _():
        per = 4 * cap
        r = lax.broadcasted_iota(jnp.int32, (tok, total), 1)
        e = r // per
        q = r - e * per
        h = q // (2 * cap)
        q = q - h * (2 * cap)
        a = q // cap
        ident = e * cap + q - a * cap
        hit0 = ident == slot_ref[:, 0:1]
        hit1 = ident == slot_ref[:, 1:2]
        for half in range(2):
            out = (h == half) & (a == 0)
            pick[3 * half] = jnp.where(hit0 & out, 1.0, 0.0).astype(BF)
            pick[3 * half + 1] = jnp.where(hit1 & out, 1.0, 0.0).astype(BF)
            pick[3 * half + 2] = jnp.where(
                (hit0 | hit1) & (h == half) & (a == 1), 1.0, 0.0
            ).astype(BF)

    for half in range(2):
        at = pl.ds(pl.multiple_of(half * tiles * TILE + i * TILE, TILE), TILE)
        block = back_ref[...]
        one = jnp.dot(pick[3 * half], block, preferred_element_type=F32)
        two = jnp.dot(pick[3 * half + 1], block, preferred_element_type=F32)
        both = jnp.dot(pick[3 * half + 2], block, preferred_element_type=F32)
        mixed_ref[:, at] = (one * prob_ref[:, 0:1] + two * prob_ref[:, 1:2]).astype(BF)
        grad_ref[:, at] = both.astype(BF)


def combine(slots, probs, back, cap):
    total, half = back.shape
    tok = slots.shape[0]
    tiles = half // TILE
    whole = pl.BlockSpec((tok, 2 * half), lambda i: (0, 0))
    small = pl.BlockSpec((tok, 2), lambda i: (0, 0))
    shape = jax.ShapeDtypeStruct((tok, 2 * half), BF)
    return pl.pallas_call(
        functools.partial(combine_kernel, cap, tiles),
        grid=(tiles,),
        in_specs=[small, small, pl.BlockSpec((total, TILE), lambda i: (0, i))],
        out_specs=[whole, whole],
        out_shape=[shape, shape],
        scratch_shapes=[pltpu.VMEM((6, tok, total), BF)],
        compiler_params=pltpu.CompilerParams(vmem_limit_bytes=VMEM),
        cost_estimate=pl.CostEstimate(
            flops=2 * 6 * tok * total * half, bytes_accessed=13 * 1024 * 1024, transcendentals=0
        ),
        name="combine",
    )(slots, probs, back)


def moments_kernel(piece, mine, other, first, second, out):
    grad = mine[...].astype(F32) + other[...].astype(F32)
    m = (0.9 * first[...].astype(F32) + 0.1 * grad).astype(BF)
    v = (0.95 * second[...].astype(F32) + 0.05 * grad * grad).astype(BF)
    for j in range(mine.shape[0] // piece):
        out[2 * j * piece : (2 * j + 1) * piece, :] = m[j * piece : (j + 1) * piece]
        out[(2 * j + 1) * piece : (2 * j + 2) * piece, :] = v[j * piece : (j + 1) * piece]


def moments(mine, other, first, second, piece):
    rows, columns = mine.shape
    block = 8 * piece
    spec = pl.BlockSpec((block, columns), lambda i: (i, 0))
    return pl.pallas_call(
        functools.partial(moments_kernel, piece),
        grid=(rows // block,),
        in_specs=[spec] * 4,
        out_specs=pl.BlockSpec((2 * block, columns), lambda i: (i, 0)),
        out_shape=jax.ShapeDtypeStruct((2 * rows, columns), BF),
        compiler_params=pltpu.CompilerParams(vmem_limit_bytes=VMEM),
        cost_estimate=pl.CostEstimate(
            flops=10 * rows * columns, bytes_accessed=12 * rows * columns, transcendentals=0
        ),
        name="moments",
    )(mine, other, first, second)


def step_kernel(piece, both, weight, m_out, v_out, step_out):
    for j in range(weight.shape[0] // piece):
        at = slice(j * piece, (j + 1) * piece)
        m = both[2 * j * piece : (2 * j + 1) * piece, :]
        v = both[(2 * j + 1) * piece : (2 * j + 2) * piece, :]
        m_out[at, :] = m
        v_out[at, :] = v
        step = m.astype(F32) / (jnp.sqrt(v.astype(F32)) + 1e-08)
        step_out[at, :] = (step + 0.1 * weight[at, :].astype(F32)).astype(BF)


def final_step(both, weight, piece):
    rows, columns = weight.shape
    block = 8 * piece
    spec = pl.BlockSpec((block, columns), lambda i: (i, 0))
    shape = jax.ShapeDtypeStruct((rows, columns), BF)
    return pl.pallas_call(
        functools.partial(step_kernel, piece),
        grid=(rows // block,),
        in_specs=[pl.BlockSpec((2 * block, columns), lambda i: (i, 0)), spec],
        out_specs=[spec] * 3,
        out_shape=[shape] * 3,
        compiler_params=pltpu.CompilerParams(vmem_limit_bytes=VMEM),
        cost_estimate=pl.CostEstimate(
            flops=10 * rows * columns, bytes_accessed=12 * rows * columns, transcendentals=0
        ),
        name="final_step",
    )(both, weight)


def swap(array):
    return lax.all_to_all(array, "expert", split_axis=0, concat_axis=0, tiled=True)


def reorder(array, inverse):
    count = inverse.shape[0]
    pieces = array.reshape(count, array.shape[0] // count, array.shape[1])
    return jnp.take(pieces, inverse, axis=0, mode="clip").reshape(array.shape)


def local(tokens, cotangent, gate_probs, routes, placement, weights, first_moment, second_moment):
    experts = lax.axis_size("expert")
    tok, width = tokens.shape
    top = routes.shape[1]
    cap = max(2, (3 * tok * top + 2 * experts - 1) // (2 * experts))
    ids = routes.reshape(-1)
    labels = jnp.arange(experts, dtype=jnp.int32)
    onehot = (ids[:, None] == labels[None, :]).astype(jnp.int32)
    earlier = jnp.sum((jnp.cumsum(onehot, axis=0) - onehot) * onehot, axis=1)
    slots = (ids * cap + earlier).reshape(tok, top)
    inverse = jnp.sum(
        labels[None, :] * (placement[None, :] == labels[:, None]).astype(jnp.int32), axis=1
    )
    rank = lax.axis_index("dp")
    weight = weights[0]
    rows = weight.shape[0] // 2
    piece = rows // experts

    send = dispatch(slots.T, gate_probs.T, tokens, cotangent, experts, cap)
    recv = swap(send)
    half = lax.dynamic_slice_in_dim(weight, rank * rows, rows, 0)
    spread_w = swap(half)
    result, mine, theirs = expert_call(rank.reshape(1).astype(jnp.int32), recv, weight, cap)
    other = lax.ppermute(theirs, "dp", [(0, 1), (1, 0)])
    back = swap(result)
    mixed, token_grad = combine(slots, gate_probs, back, cap)
    state = moments(mine, other, first_moment[0], second_moment[0], piece)
    spread_state = swap(state)
    moved_w = swap(reorder(spread_w, inverse))
    moved_state = swap(reorder(spread_state, inverse))
    m, v, step = final_step(moved_state, moved_w, piece)
    return (mixed, token_grad, m[None], v[None], step[None])


def solution(mesh):
    in_specs = (
        P(("expert", "dp"), None),
        P(("expert", "dp"), None),
        P(("expert", "dp"), None),
        P(("expert", "dp"), None),
        P(),
        P("expert", None, None),
        P("expert", "dp", None),
        P("expert", "dp", None),
    )
    out_specs = (
        P(("expert", "dp"), None),
        P(("expert", "dp"), None),
        P("expert", "dp", None),
        P("expert", "dp", None),
        P("expert", "dp", None),
    )
    return jax.shard_map(local, mesh=mesh, in_specs=in_specs, out_specs=out_specs, check_vma=False)
```

time: 920 us -> 554 us (0.60); the launches traced: 908 us -> 553 us
  other arithmetic: 272 us -> 1.57 us
  local copies, waits for them, and re-layouts: 245 us -> 19.5 us
  waiting for transfers between devices: 206 us -> 349 us
  Pallas kernels: 0 us -> 58.9 us
  starting transfers between devices: 81.1 us -> 55.6 us
  matrix products: 22.9 us -> 0 us
  between operations: 14.7 us -> 0.74 us
    unnamed x4 -> x0, other arithmetic: 204 us -> none
    unnamed x49 -> x16, local copies, waits for them, and re-layouts: 107 us -> 7.49 us
    all_to_all x9 -> x5, waiting for transfers between devices: 206 us -> 291 us  [swap(): lax.all_to_all(array, 'expert', split_axis=0, concat_axis=0, tiled=True)]
    all_to_all x8 -> x0, local copies, waits for them, and re-layouts: 62.8 us -> none  [the longest x2 16.1 us: local(): lax.all_to_all(expert_out, 'expert', split_axis=0, concat_axis=0, tiled=T...]
    pallas_call x0 -> x5, Pallas kernels: none -> 58.9 us  [the longest x1 20.6 us: expert_call(): pl.pallas_call(functools.partial(expert_kernel, cap, group, tiles), grid=...]
    ppermute x0 -> x1, waiting for transfers between devices: none -> 58.1 us  [local(): other = lax.ppermute(theirs, 'dp', [(0, 1), (1, 0)])]
    gather x8 -> x2, local copies, waits for them, and re-layouts: 42.9 us -> 7.97 us  [reorder(): return jnp.take(pieces, inverse, axis=0, mode='clip').reshape(array.shape)]
    all_to_all x9 -> x5, starting transfers between devices: 80.9 us -> 52.7 us  [swap(): lax.all_to_all(array, 'expert', split_axis=0, concat_axis=0, tiled=True)]
  transfers between devices with their start and end apart: 10 -> 6, of which waited for: 5 -> 5; matrix products, arithmetic and copies ran while one was open for 44% -> 2% of each run, Pallas kernels for 0% -> 7%
where the time goes in v1:
time: 554 us; the launch traced here: 553 us
  waiting for transfers between devices  349 us (63%)
  blocking collectives  67.3 us (12%)
  Pallas kernels  58.9 us (11%)
  starting transfers between devices  55.6 us (10%)
  local copies, waits for them, and re-layouts  19.5 us (4%)
    all_to_all x5, waiting for transfers between devices, swap(): lax.all_to_all(array, 'expert', split_axis=0, concat_axis=0, tiled=True)  291 us
    all_to_all x1, blocking collectives, swap(): lax.all_to_all(array, 'expert', split_axis=0, concat_axis=0, tiled=True)  67.3 us
    ppermute x1, waiting for transfers between devices, local(): other = lax.ppermute(theirs, 'dp', [(0, 1), (1, 0)])  58.1 us
    all_to_all x5, starting transfers between devices, swap(): lax.all_to_all(array, 'expert', split_axis=0, concat_axis=0, tiled=True)  52.7 us
    pallas_call x1, Pallas kernels, expert_call(): pl.pallas_call(functools.partial(expert_kernel, cap, group, tiles), grid=...  20.6 us
    pallas_call x1, Pallas kernels, combine(): pl.pallas_call(functools.partial(combine_kernel, cap, tiles), grid=(tiles...  12 us
  transfers between devices with their start and end apart: 6, of which 5 were waited for; matrix products, arithmetic and copies ran while one was open for 2% of the time, Pallas kernels for 7%

profile of v1, /device:TPU:6, one launch (start us, length us, event | category | flops | bytes accessed | tf_op | source)
XLA Modules:
  0.0 552.6 jit_solution(14604031571839059923)
XLA Ops:
  0.6 0.7 broadcast_multiply_fusion
  1.3 0.8 copy.31
  2.1 0.1 eq.38
  2.2 0.1 eq.42
  2.5 0.6 reduce-window.6
  3.1 0.2 slice_reduce_fusion
  3.5 0.1 reduce_sum.21
  3.7 0.7 copy-done.2
  4.4 1.4 copy-done.4
  5.8 1.4 copy-done.5
  7.2 10.0 %dispatch.1 = bf16[1536,3072]{1,0:T(8,128)(2,1)} custom-call(s32[2,128]{1,0:T(2,128)S(1)} %copy.35.slot_ref, f32[2,128]{1,0:T(2,128)S(1)} %bitcast.38, bf16[128,6144]{1,0:T(8,128)(2,1)S(1)} %copy-done.4, bf16[128,6144]{1,0:T(8,128)(2,1)S(1)} %copy-done.4, bf16[128,6144]{1,0:T(8,128)(2,1)S(1)} %copy-done.5, bf16[128,6144]{1,0:T(8,128)(2,1)S(1)} %copy-done.5), custom_call_target="tpu_custom_call" | custom-call | flops 4831838208 | bytes 16777216 | tf_op jit(solution)/shard_map/dispatch/pallas_call | solution.py:62
  17.2 10.2 %all-to-all-start = ((bf16[64,24,3072]{2,1,0:T(8,128)(2,1)}), bf16[64,24,3072]{2,1,0:T(8,128)(2,1)}, u32[]{:S(2)}, u32[]{:S(2)}) async-start(bf16[64,24,3072]{2,1,0:T(8,128)(2,1)} %bitcast.41), calls=%async_computation | async-start | bytes 18874368 | tf_op jit(solution)/shard_map/all_to_all | solution.py:335
  27.4 3.3 constant_dynamic-slice_fusion
  30.7 119.6 %all-to-all-done = bf16[64,24,3072]{2,1,0:T(8,128)(2,1)} async-done(((bf16[64,24,3072]{2,1,0:T(8,128)(2,1)}), bf16[64,24,3072]{2,1,0:T(8,128)(2,1)}, u32[]{:S(2)}, u32[]{:S(2)}) %all-to-all-start) | async-done | bytes 9437216 | tf_op jit(solution)/shard_map/all_to_all | solution.py:335
  150.3 13.5 %all-to-all-start.4 = ((bf16[64,48,384]{2,1,0:T(8,128)(2,1)}), bf16[64,48,384]{2,1,0:T(8,128)(2,1)S(1)}, u32[]{:S(2)}, u32[]{:S(2)}) async-start(bf16[64,48,384]{2,1,0:T(8,128)(2,1)} %bitcast.13), calls=%async_computation.4 | async-start | bytes 4718592 | tf_op jit(solution)/shard_map/all_to_all | solution.py:335
  163.9 20.6 %expert_pass.1 = (bf16[1536,3072]{1,0:T(8,128)(2,1)}, bf16[3072,384]{1,0:T(8,128)(2,1)S(1)}, bf16[3072,384]{1,0:T(8,128)(2,1)}) custom-call(s32[1]{0:T(128)} %bitcast.1.rank_ref, bf16[1536,3072]{1,0:T(8,128)(2,1)} %bitcast.5.recv_ref, bf16[2,3072,384]{2,1,0:T(8,128)(2,1)} %bitcast.44), custom_call_target="tpu_custom_call" | custom-call | flops 10000000000 | bytes 35651584 | tf_op jit(solution)/shard_map/expert_pass/pallas_call | solution.py:184
  184.5 1.4 copy-done
  185.9 2.9 collective-permute-start
  188.9 5.5 all-to-all-done.4
  194.3 2.3 gather_fusion.1
  196.6 7.7 %all-to-all-start.5 = ((bf16[64,48,384]{2,1,0:T(8,128)(2,1)}), bf16[64,48,384]{2,1,0:T(8,128)(2,1)S(1)}, u32[]{:S(2)}, u32[]{:S(2)}) async-start(bf16[64,48,384]{2,1,0:T(8,128)(2,1)} %gather_fusion.1), calls=%async_computation.5 | async-start | bytes 4718592 | tf_op jit(solution)/shard_map/all_to_all | solution.py:335
  204.3 58.1 %collective-permute-done.other = bf16[3072,384]{1,0:T(8,128)(2,1)} collective-permute-done((bf16[3072,384]{1,0:T(8,128)(2,1)}, bf16[3072,384]{1,0:T(8,128)(2,1)}, u32[]{:S(2)}, u32[]{:S(2)}) %collective-permute-start) | collective-permute-done | bytes 2359328 | tf_op jit(solution)/shard_map/ppermute | solution.py:367
  262.4 1.7 copy-done.1
  264.0 8.1 %moments.1 = bf16[6144,384]{1,0:T(8,128)(2,1)} custom-call(bf16[3072,384]{1,0:T(8,128)(2,1)S(1)} %copy-done.1, bf16[3072,384]{1,0:T(8,128)(2,1)} %collective-permute-done.other, bf16[3072,384]{1,0:T(8,128)(2,1)} %bitcast.42, bf16[3072,384]{1,0:T(8,128)(2,1)} %bitcast.43), custom_call_target="tpu_custom_call" | custom-call | flops 11796480 | bytes 14155776 | tf_op jit(solution)/shard_map/moments/pallas_call | solution.py:290
  272.1 67.3 %all_to_all.56 = bf16[64,96,384]{2,1,0:T(8,128)(2,1)} all-to-all(bf16[64,96,384]{2,1,0:T(8,128)(2,1)} %bitcast.39), channel_id=1, replica_groups=mesh['expert'=64,'dp'=2] {'expert'}, dimensions={0} | all-to-all | bytes 9437184 | tf_op jit(solution)/shard_map/all_to_all | solution.py:335
  339.4 7.7 %all-to-all-start.1 = ((bf16[64,24,3072]{2,1,0:T(8,128)(2,1)}), bf16[64,24,3072]{2,1,0:T(8,128)(2,1)}, u32[]{:S(2)}, u32[]{:S(2)}) async-start(bf16[64,24,3072]{2,1,0:T(8,128)(2,1)} %bitcast.40), calls=%async_computation.1 | async-start | bytes 18874368 | tf_op jit(solution)/shard_map/all_to_all | solution.py:335
  347.1 5.7 %gather_fusion = bf16[64,96,384]{2,1,0:T(8,128)(2,1)} fusion(bf16[64,96,384]{2,1,0:T(8,128)(2,1)} %all_to_all.56, s32[1024]{0:T(1024)S(1)} %pad_clamp_fusion), kind=kCustom, calls=%fused_computation | custom fusion | bytes 9437440 | tf_op jit(solution)/shard_map/jit(_take)/gather | solution.py:341
  352.8 117.2 %all-to-all-done.1 = bf16[64,24,3072]{2,1,0:T(8,128)(2,1)} async-done(((bf16[64,24,3072]{2,1,0:T(8,128)(2,1)}), bf16[64,24,3072]{2,1,0:T(8,128)(2,1)}, u32[]{:S(2)}, u32[]{:S(2)}) %all-to-all-start.1) | async-done | bytes 9437216 | tf_op jit(solution)/shard_map/all_to_all | solution.py:335
  470.0 13.6 %all-to-all-start.3 = ((bf16[64,96,384]{2,1,0:T(8,128)(2,1)}), bf16[64,96,384]{2,1,0:T(8,128)(2,1)}, u32[]{:S(2)}, u32[]{:S(2)}) async-start(bf16[64,96,384]{2,1,0:T(8,128)(2,1)} %gather_fusion), calls=%async_computation.3 | async-start | bytes 9437184 | tf_op jit(solution)/shard_map/all_to_all | solution.py:335
  483.7 12.0 %combine.1 = (bf16[128,6144]{1,0:T(8,128)(2,1)}, bf16[128,6144]{1,0:T(8,128)(2,1)}) custom-call(s32[128,2]{1,0:T(8,128)S(1)} %add.7.slot_ref, f32[128,2]{1,0:T(8,128)S(1)} %copy.36.prob_ref, bf16[1536,3072]{1,0:T(8,128)(2,1)} %bitcast.8.back_ref), custom_call_target="tpu_custom_call" | custom-call | flops 7247757312 | bytes 13631488 | tf_op jit(solution)/shard_map/combine/pallas_call | solution.py:262
  495.7 48.6 %all-to-all-done.3 = bf16[64,96,384]{2,1,0:T(8,128)(2,1)} async-done(((bf16[64,96,384]{2,1,0:T(8,128)(2,1)}), bf16[64,96,384]{2,1,0:T(8,128)(2,1)}, u32[]{:S(2)}, u32[]{:S(2)}) %all-to-all-start.3) | async-done | bytes 4718624 | tf_op jit(solution)/shard_map/all_to_all | solution.py:335
  544.4 8.2 %final_step.1 = (bf16[3072,384]{1,0:T(8,128)(2,1)}, bf16[3072,384]{1,0:T(8,128)(2,1)}, bf16[3072,384]{1,0:T(8,128)(2,1)}) custom-call(bf16[6144,384]{1,0:T(8,128)(2,1)} %bitcast.12.both, bf16[3072,384]{1,0:T(8,128)(2,1)S(1)} %bitcast.36), custom_call_target="tpu_custom_call" | custom-call | flops 11796480 | bytes 14155776 | tf_op jit(solution)/shard_map/final_step/pallas_call | solution.py:320
  (20 shorter events, 0.6 us)
Async XLA Ops:
  3.7 0.7 copy-start.2
  4.4 1.4 copy-start.4
  5.8 1.4 copy-start.5
  17.2 133.1 %all-to-all-start = ((bf16[64,24,3072]{2,1,0:T(8,128)(2,1)}), bf16[64,24,3072]{2,1,0:T(8,128)(2,1)}, u32[]{:S(2)}, u32[]{:S(2)}) async-start(bf16[64,24,3072]{2,1,0:T(8,128)(2,1)} %bitcast.41), calls=%async_computation | async-start | bytes 18874368 | tf_op jit(solution)/shard_map/all_to_all | solution.py:335
  150.3 13.5 %copy-start.6 = (s32[64]{0:T(128)S(1)}, s32[64]{0:T(128)}, u32[]{:S(2)}) copy-start(s32[64]{0:T(128)} %param.12) | copy-start | bytes 772
  150.3 44.0 %all-to-all-start.4 = ((bf16[64,48,384]{2,1,0:T(8,128)(2,1)}), bf16[64,48,384]{2,1,0:T(8,128)(2,1)S(1)}, u32[]{:S(2)}, u32[]{:S(2)}) async-start(bf16[64,48,384]{2,1,0:T(8,128)(2,1)} %bitcast.13), calls=%async_computation.4 | async-start | bytes 4718592 | tf_op jit(solution)/shard_map/all_to_all | solution.py:335
  184.5 1.4 copy-start
  185.9 76.4 %collective-permute-start = (bf16[3072,384]{1,0:T(8,128)(2,1)}, bf16[3072,384]{1,0:T(8,128)(2,1)}, u32[]{:S(2)}, u32[]{:S(2)}) collective-permute-start(bf16[3072,384]{1,0:T(8,128)(2,1)} %get-tuple-element.17), channel_id=1, source_target_pairs={{0,1},{1,0},{2,3},{3,2},{4,5},{5,4},{6,7},{7,6},{8,9},{9,8},{10,11... | collective-permute-start | bytes 7077896 | tf_op jit(solution)/shard_map/ppermute | solution.py:367
  196.6 75.5 %all-to-all-start.5 = ((bf16[64,48,384]{2,1,0:T(8,128)(2,1)}), bf16[64,48,384]{2,1,0:T(8,128)(2,1)S(1)}, u32[]{:S(2)}, u32[]{:S(2)}) async-start(bf16[64,48,384]{2,1,0:T(8,128)(2,1)} %gather_fusion.1), calls=%async_computation.5 | async-start | bytes 4718592 | tf_op jit(solution)/shard_map/all_to_all | solution.py:335
  262.4 1.7 copy-start.1
  339.4 130.6 %all-to-all-start.1 = ((bf16[64,24,3072]{2,1,0:T(8,128)(2,1)}), bf16[64,24,3072]{2,1,0:T(8,128)(2,1)}, u32[]{:S(2)}, u32[]{:S(2)}) async-start(bf16[64,24,3072]{2,1,0:T(8,128)(2,1)} %bitcast.40), calls=%async_computation.1 | async-start | bytes 18874368 | tf_op jit(solution)/shard_map/all_to_all | solution.py:335
  352.8 130.8 %copy-start.3 = (f32[128,2]{0,1:T(2,128)S(1)}, f32[128,2]{0,1:T(2,128)}, u32[]{:S(2)}) copy-start(f32[128,2]{0,1:T(2,128)} %param.10) | copy-start | bytes 3076
  470.0 74.4 %all-to-all-start.3 = ((bf16[64,96,384]{2,1,0:T(8,128)(2,1)}), bf16[64,96,384]{2,1,0:T(8,128)(2,1)}, u32[]{:S(2)}, u32[]{:S(2)}) async-start(bf16[64,96,384]{2,1,0:T(8,128)(2,1)} %gather_fusion), calls=%async_computation.3 | async-start | bytes 9437184 | tf_op jit(solution)/shard_map/all_to_all | solution.py:335

commit v2 on v1

v2 whole, which is shorter than its diff:
```python
import functools
import jax
import jax.numpy as jnp
from jax import lax
from jax.experimental import pallas as pl
from jax.experimental.pallas import tpu as pltpu
from jax.sharding import PartitionSpec as P

BF = jnp.bfloat16
F32 = jnp.float32
VMEM = 48 * 1024 * 1024
TILE = 512


def row_parts(rows, first, cap):
    per = 4 * cap
    r = lax.broadcasted_iota(jnp.int32, (rows, 128), 0) + first
    e = r // per
    q = r - e * per
    h = q // (2 * cap)
    q = q - h * (2 * cap)
    a = q // cap
    s = q - a * cap
    return e * cap + s, h, a


def dispatch_kernel(cap, slot_ref, prob_ref, t0, t1, c0, c1, out_ref, low, high, scale):
    rows = out_ref.shape[0]

    @pl.when((pl.program_id(0) == 0) & (pl.program_id(1) == 0))
    def _():
        ident, h, a = row_parts(rows, 0, cap)
        hit0 = ident == slot_ref[0:1, :]
        hit1 = ident == slot_ref[1:2, :]
        hit = hit0 | hit1
        prob = jnp.where(hit0, prob_ref[0:1, :], 0.0) + jnp.where(hit1, prob_ref[1:2, :], 0.0)
        prob = jnp.sum(prob, axis=1, keepdims=True)
        scale[...] = jnp.where(a == 0, 1.0, prob)
        for ref, half in ((low, 0), (high, 1)):
            for kind in (0, 1):
                keep = hit & (h == half) & (a == kind)
                ref[:, kind * 128 : (kind + 1) * 128] = jnp.where(keep, 1.0, 0.0).astype(BF)

    x0 = jnp.concatenate([t0[...], c0[...]], axis=0)
    x1 = jnp.concatenate([t1[...], c1[...]], axis=0)
    step = rows // 4
    for i in range(4):
        part = slice(i * step, (i + 1) * step)
        acc = jnp.dot(low[part, :], x0, preferred_element_type=F32)
        acc = acc + jnp.dot(high[part, :], x1, preferred_element_type=F32)
        out_ref[part, :] = (acc * scale[part, 0:1]).astype(BF)


def dispatch(slots, probs, tokens, cotangent, experts, cap):
    tok, width = tokens.shape
    half = width // 4
    tiles = half // TILE
    rows = experts * cap * 4
    small = pl.BlockSpec((2, tok), lambda r, i: (0, 0))
    left = pl.BlockSpec((tok, TILE), lambda r, i: (0, 2 * r * tiles + i))
    right = pl.BlockSpec((tok, TILE), lambda r, i: (0, (2 * r + 1) * tiles + i))
    return pl.pallas_call(
        functools.partial(dispatch_kernel, cap),
        grid=(2, tiles),
        in_specs=[small, small, left, right, left, right],
        out_specs=pl.BlockSpec((rows, TILE), lambda r, i: (r, i)),
        out_shape=jax.ShapeDtypeStruct((2 * rows, half), BF),
        scratch_shapes=[
            pltpu.VMEM((rows, 2 * tok), BF),
            pltpu.VMEM((rows, 2 * tok), BF),
            pltpu.VMEM((rows, 128), F32),
        ],
        compiler_params=pltpu.CompilerParams(vmem_limit_bytes=VMEM),
        cost_estimate=pl.CostEstimate(
            flops=2 * rows * 2 * tok * width, bytes_accessed=16 * 1024 * 1024, transcendentals=0
        ),
        name="dispatch",
    )(slots, probs, tokens, tokens, cotangent, cotangent)


def order_matrix(group, cap, inverse):
    n = group * cap * 4
    i = lax.broadcasted_iota(jnp.int32, (n, n), 1 if inverse else 0)
    j = lax.broadcasted_iota(jnp.int32, (n, n), 0 if inverse else 1)
    hk = i // (group * cap)
    rest = i - hk * (group * cap)
    src = rest // cap
    slot = rest - src * cap
    return jnp.where(src * (4 * cap) + hk * cap + slot == j, 1.0, 0.0).astype(BF)


def front_kernel(cap, group, rank_ref, recv_ref, w_ref, x_ref, c_ref, sum_ref, send_ref, fore):
    i = pl.program_id(0)
    n = group * cap
    span = 4 * n
    sets = recv_ref.shape[0] // span
    hidden = sum_ref.shape[1] // 3

    @pl.when(i == 0)
    def _():
        fore[...] = order_matrix(group, cap, False)
        sum_ref[...] = jnp.zeros_like(sum_ref)

    for g in range(sets):
        got = jnp.dot(
            fore[...], recv_ref[g * span : (g + 1) * span, :], preferred_element_type=F32
        ).astype(BF)
        at = slice(g * n, (g + 1) * n)
        for h in range(2):
            x_ref[h, at, :] = got[2 * h * n : (2 * h + 1) * n]
            c_ref[h, at, :] = got[(2 * h + 1) * n : (2 * h + 2) * n]
    for h in range(2):
        sum_ref[:, : 2 * hidden] += jnp.dot(
            x_ref[h], w_ref[0, h, :, : 2 * hidden], preferred_element_type=F32
        )
        sum_ref[:, 2 * hidden :] += jnp.dot(
            c_ref[h], w_ref[0, h, :, 2 * hidden :], preferred_element_type=F32
        )

    @pl.when(i == pl.num_programs(0) - 1)
    def _():
        send_ref[...] = sum_ref[...].astype(BF)


GROUP = 8


def front_call(rank, recv, weight, cap):
    total, half = recv.shape
    columns = weight.shape[-1]
    tiles = half // TILE
    rows = total // 4
    n = GROUP * cap * 4
    held = pl.BlockSpec((2, rows, TILE), lambda i, r: (0, 0, i))
    small = pl.BlockSpec((rows, columns), lambda i, r: (0, 0))
    return pl.pallas_call(
        functools.partial(front_kernel, cap, GROUP),
        grid_spec=pltpu.PrefetchScalarGridSpec(
            num_scalar_prefetch=1,
            grid=(tiles,),
            in_specs=[
                pl.BlockSpec((total, TILE), lambda i, r: (0, i)),
                pl.BlockSpec((1, 2, TILE, columns), lambda i, r: (r[0], 0, i, 0)),
            ],
            out_specs=[held, held, small, small],
            scratch_shapes=[pltpu.VMEM((n, n), BF)],
        ),
        out_shape=[
            jax.ShapeDtypeStruct((2, rows, half), BF),
            jax.ShapeDtypeStruct((2, rows, half), BF),
            jax.ShapeDtypeStruct((rows, columns), F32),
            jax.ShapeDtypeStruct((rows, columns), BF),
        ],
        compiler_params=pltpu.CompilerParams(vmem_limit_bytes=VMEM),
        cost_estimate=pl.CostEstimate(
            flops=5 * 10**9, bytes_accessed=22 * 1024 * 1024, transcendentals=0
        ),
        name="expert_front",
    )(rank, recv, weight.reshape(2, 2, half, columns))


def rear_kernel(
    cap, group, piece, rank_ref, x_ref, c_ref, own_ref, other_ref, w_ref, first_ref, second_ref,
    out_ref, state_ref, inner, pre, back
):
    i = pl.program_id(0)
    n = group * cap
    span = 4 * n
    sets = out_ref.shape[0] // span
    hidden = inner.shape[1]

    @pl.when(i == 0)
    def _():
        back[...] = order_matrix(group, cap, True)
        total = own_ref[...] + other_ref[...].astype(F32)
        gate = total[:, :hidden]
        up = total[:, hidden : 2 * hidden]
        grad = total[:, 2 * hidden :]
        sig = jax.nn.sigmoid(gate)
        active = gate * sig
        inner[...] = (active * up).astype(BF)
        slope = sig * (1.0 + gate * (1.0 - sig))
        pre[:, :hidden] = (grad * up * slope).astype(BF)
        pre[:, hidden:] = (grad * active).astype(BF)

    contract = (((1,), (1,)), ((), ()))
    lead = (((0,), (0,)), ((), ()))
    made = []
    for h in range(2):
        made.append(
            lax.dot_general(
                inner[...], w_ref[0, h, :, 2 * hidden :], contract, preferred_element_type=F32
            ).astype(BF)
        )
        made.append(
            lax.dot_general(
                pre[...], w_ref[0, h, :, : 2 * hidden], contract, preferred_element_type=F32
            ).astype(BF)
        )
    for g in range(sets):
        stack = jnp.concatenate([m[g * n : (g + 1) * n] for m in made], axis=0)
        out_ref[g * span : (g + 1) * span, :] = jnp.dot(
            back[...], stack, preferred_element_type=F32
        ).astype(BF)
    for h in range(2):
        for source, factor, at in (
            (x_ref, pre, slice(0, 2 * hidden)),
            (c_ref, inner, slice(2 * hidden, 3 * hidden)),
        ):
            grad = lax.dot_general(source[h], factor[...], lead, preferred_element_type=F32)
            m = (0.9 * first_ref[h, :, at].astype(F32) + 0.1 * grad).astype(BF)
            v = (0.95 * second_ref[h, :, at].astype(F32) + 0.05 * grad * grad).astype(BF)
            for j in range(grad.shape[0] // piece):
                state_ref[h, j, :piece, at] = m[j * piece : (j + 1) * piece]
                state_ref[h, j, piece:, at] = v[j * piece : (j + 1) * piece]


def rear_call(rank, x, c, own, other, weight, first, second, cap, piece):
    half = x.shape[2]
    rows, columns = own.shape
    hidden = columns // 3
    tile = 8 * piece
    tiles = half // tile
    total = 4 * rows
    n = GROUP * cap * 4
    held = pl.BlockSpec((2, rows, tile), lambda i, r: (0, 0, i))
    small = pl.BlockSpec((rows, columns), lambda i, r: (0, 0))
    moment = pl.BlockSpec((2, tile, columns), lambda i, r: (0, i, 0))
    return pl.pallas_call(
        functools.partial(rear_kernel, cap, GROUP, piece),
        grid_spec=pltpu.PrefetchScalarGridSpec(
            num_scalar_prefetch=1,
            grid=(tiles,),
            in_specs=[
                held,
                held,
                small,
                small,
                pl.BlockSpec((1, 2, tile, columns), lambda i, r: (r[0], 0, i, 0)),
                moment,
                moment,
            ],
            out_specs=[
                pl.BlockSpec((total, tile), lambda i, r: (0, i)),
                pl.BlockSpec((2, 8, 2 * piece, columns), lambda i, r: (0, i, 0, 0)),
            ],
            scratch_shapes=[
                pltpu.VMEM((rows, hidden), BF),
                pltpu.VMEM((rows, 2 * hidden), BF),
                pltpu.VMEM((n, n), BF),
            ],
        ),
        out_shape=[
            jax.ShapeDtypeStruct((total, half), BF),
            jax.ShapeDtypeStruct((2, half // piece, 2 * piece, columns), BF),
        ],
        compiler_params=pltpu.CompilerParams(vmem_limit_bytes=VMEM),
        cost_estimate=pl.CostEstimate(
            flops=7 * 10**9, bytes_accessed=34 * 1024 * 1024, transcendentals=rows * hidden
        ),
        name="expert_rear",
    )(
        rank, x, c, own, other, weight.reshape(2, 2, half, columns),
        first.reshape(2, half, columns), second.reshape(2, half, columns),
    )


def combine_kernel(cap, tiles, slot_ref, prob_ref, back_ref, mixed_ref, grad_ref, pick):
    total = back_ref.shape[0]
    tok = mixed_ref.shape[0]
    part = pl.program_id(0)
    i = pl.program_id(1)

    @pl.when((part == 0) & (i == 0))
    def _():
        per = 4 * cap
        r = lax.broadcasted_iota(jnp.int32, (tok, total), 1)
        e = r // per
        q = r - e * per
        h = q // (2 * cap)
        q = q - h * (2 * cap)
        a = q // cap
        ident = e * cap + q - a * cap
        hit0 = ident == slot_ref[:, 0:1]
        hit1 = ident == slot_ref[:, 1:2]
        for half in range(2):
            out = (h == half) & (a == 0)
            pick[3 * half] = jnp.where(hit0 & out, 1.0, 0.0).astype(BF)
            pick[3 * half + 1] = jnp.where(hit1 & out, 1.0, 0.0).astype(BF)
            pick[3 * half + 2] = jnp.where(
                (hit0 | hit1) & (h == half) & (a == 1), 1.0, 0.0
            ).astype(BF)

    for half in range(2):
        at = pl.ds(pl.multiple_of(((2 * part + half) * tiles + i) * TILE, TILE), TILE)
        block = back_ref[...]
        one = jnp.dot(pick[3 * half], block, preferred_element_type=F32)
        two = jnp.dot(pick[3 * half + 1], block, preferred_element_type=F32)
        both = jnp.dot(pick[3 * half + 2], block, preferred_element_type=F32)
        mixed_ref[:, at] = (one * prob_ref[:, 0:1] + two * prob_ref[:, 1:2]).astype(BF)
        grad_ref[:, at] = both.astype(BF)


def combine(slots, probs, back, cap):
    total, half = back.shape
    total = total // 2
    tok = slots.shape[0]
    tiles = half // TILE
    whole = pl.BlockSpec((tok, 4 * half), lambda r, i: (0, 0))
    small = pl.BlockSpec((tok, 2), lambda r, i: (0, 0))
    shape = jax.ShapeDtypeStruct((tok, 4 * half), BF)
    return pl.pallas_call(
        functools.partial(combine_kernel, cap, tiles),
        grid=(2, tiles),
        in_specs=[small, small, pl.BlockSpec((total, TILE), lambda r, i: (r, i))],
        out_specs=[whole, whole],
        out_shape=[shape, shape],
        scratch_shapes=[pltpu.VMEM((6, tok, total), BF)],
        compiler_params=pltpu.CompilerParams(vmem_limit_bytes=VMEM),
        cost_estimate=pl.CostEstimate(
            flops=2 * 12 * tok * total * half, bytes_accessed=13 * 1024 * 1024, transcendentals=0
        ),
        name="combine",
    )(slots, probs, back)


def step_kernel(piece, both, weight, m_out, v_out, step_out):
    for j in range(weight.shape[0] // piece):
        at = slice(j * piece, (j + 1) * piece)
        m = both[2 * j * piece : (2 * j + 1) * piece, :]
        v = both[(2 * j + 1) * piece : (2 * j + 2) * piece, :]
        m_out[at, :] = m
        v_out[at, :] = v
        step = m.astype(F32) / (jnp.sqrt(v.astype(F32)) + 1e-08)
        step_out[at, :] = (step + 0.1 * weight[at, :].astype(F32)).astype(BF)


def final_step(both, weight, piece):
    rows, columns = weight.shape
    block = 8 * piece
    spec = pl.BlockSpec((block, columns), lambda i: (i, 0))
    shape = jax.ShapeDtypeStruct((rows, columns), BF)
    return pl.pallas_call(
        functools.partial(step_kernel, piece),
        grid=(rows // block,),
        in_specs=[pl.BlockSpec((2 * block, columns), lambda i: (i, 0)), spec],
        out_specs=[spec] * 3,
        out_shape=[shape] * 3,
        compiler_params=pltpu.CompilerParams(vmem_limit_bytes=VMEM),
        cost_estimate=pl.CostEstimate(
            flops=10 * rows * columns, bytes_accessed=12 * rows * columns, transcendentals=0
        ),
        name="final_step",
    )(both, weight)


def swap(array, axes="expert"):
    return lax.all_to_all(array, axes, split_axis=0, concat_axis=0, tiled=True)


def reorder(array, inverse):
    count = inverse.shape[0]
    pieces = array.reshape(count, array.shape[0] // count, array.shape[1])
    return jnp.take(pieces, inverse, axis=0, mode="clip").reshape(array.shape)


def local(tokens, cotangent, gate_probs, routes, placement, weights, first_moment, second_moment):
    experts = lax.axis_size("expert")
    tok, width = tokens.shape
    top = routes.shape[1]
    cap = max(2, (3 * tok * top + 2 * experts - 1) // (2 * experts))
    ids = routes.reshape(-1)
    labels = jnp.arange(experts, dtype=jnp.int32)
    onehot = (ids[:, None] == labels[None, :]).astype(jnp.int32)
    earlier = jnp.sum((jnp.cumsum(onehot, axis=0) - onehot) * onehot, axis=1)
    slots = (ids * cap + earlier).reshape(tok, top)
    inverse = jnp.sum(
        labels[None, :] * (placement[None, :] == labels[:, None]).astype(jnp.int32), axis=1
    )
    rank = lax.axis_index("dp")
    weight = weights[0]
    rows = weight.shape[0] // 2
    piece = rows // experts
    columns = weight.shape[1]
    both = ("dp", "expert")
    together = lax.optimization_barrier

    spread_w = swap(lax.dynamic_slice_in_dim(weight, rank * rows, rows, 0))
    send = dispatch(slots.T, gate_probs.T, tokens, cotangent, experts, cap)
    send, spread_w = together((send, spread_w))
    recv = swap(send, both)
    ready_w, recv = together((reorder(spread_w, inverse), recv))
    moved_w = swap(ready_w)
    place = rank.reshape(1).astype(jnp.int32)
    x, c, own, out = front_call(place, recv, weight, cap)
    other = lax.ppermute(out, "dp", [(0, 1), (1, 0)])
    result, state = rear_call(
        place, x, c, own, other, weight, first_moment[0], second_moment[0], cap, piece
    )
    state, moved_w = together((state, moved_w))
    spread_state = swap(state.reshape(2 * rows, columns))
    result, spread_state = together((result, spread_state))
    back = swap(result, both)
    ready_state, back = together((reorder(spread_state, inverse), back))
    moved_state = swap(ready_state)
    mixed, token_grad = combine(slots, gate_probs, back, cap)
    m, v, step = final_step(moved_state, moved_w, piece)
    return (mixed, token_grad, m[None], v[None], step[None])


def solution(mesh):
    in_specs = (
        P(("expert", "dp"), None),
        P(("expert", "dp"), None),
        P(("expert", "dp"), None),
        P(("expert", "dp"), None),
        P(),
        P("expert", None, None),
        P("expert", "dp", None),
        P("expert", "dp", None),
    )
    out_specs = (
        P(("expert", "dp"), None),
        P(("expert", "dp"), None),
        P("expert", "dp", None),
        P("expert", "dp", None),
        P("expert", "dp", None),
    )
    return jax.shard_map(local, mesh=mesh, in_specs=in_specs, out_specs=out_specs, check_vma=False)
```

time: 554 us -> 529 us (0.955)
  waiting for transfers between devices: 349 us -> 305 us
  starting transfers between devices: 55.6 us -> 81.8 us
    ppermute x1, waiting for transfers between devices: 58.1 us -> 26.1 us  [local(): other = lax.ppermute(out, 'dp', [(0, 1), (1, 0)])]
    all_to_all x5, starting transfers between devices: 52.7 us -> 80.4 us  [swap(): return lax.all_to_all(array, axes, split_axis=0, concat_axis=0, tiled=True)]
    all_to_all x5, waiting for transfers between devices: 291 us -> 279 us  [swap(): return lax.all_to_all(array, axes, split_axis=0, concat_axis=0, tiled=True)]
    unnamed x16 -> x14, local copies, waits for them, and re-layouts: 7.49 us -> 1.67 us
  transfers between devices with their start and end apart: 6 -> 6, of which waited for: 5 -> 5; matrix products, arithmetic and copies ran while one was open for 2% -> 2% of each run, Pallas kernels for 7% -> 9%
where the time goes in v2:
time: 529 us; the launch traced here: 528 us
  waiting for transfers between devices  305 us (58%)
  starting transfers between devices  81.8 us (15%)
  blocking collectives  67.6 us (13%)
  Pallas kernels  56.9 us (11%)
  local copies, waits for them, and re-layouts  15.4 us (3%)
    all_to_all x5, waiting for transfers between devices, swap(): return lax.all_to_all(array, axes, split_axis=0, concat_axis=0, tiled=True)  279 us
    all_to_all x5, starting transfers between devices, swap(): return lax.all_to_all(array, axes, split_axis=0, concat_axis=0, tiled=True)  80.4 us
    all_to_all x1, blocking collectives, swap(): return lax.all_to_all(array, axes, split_axis=0, concat_axis=0, tiled=True)  67.6 us
    ppermute x1, waiting for transfers between devices, local(): other = lax.ppermute(out, 'dp', [(0, 1), (1, 0)])  26.1 us
    pallas_call x1, Pallas kernels, rear_call(): pl.pallas_call(functools.partial(rear_kernel, cap, GROUP, piece), grid_sp...  14.4 us
    pallas_call x1, Pallas kernels, front_call(): pl.pallas_call(functools.partial(front_kernel, cap, GROUP), grid_spec=plt...  12.3 us
    pallas_call x1, Pallas kernels, combine(): pl.pallas_call(functools.partial(combine_kernel, cap, tiles), grid=(2, ti...  12.1 us
  transfers between devices with their start and end apart: 6, of which 5 were waited for; matrix products, arithmetic and copies ran while one was open for 2% of the time, Pallas kernels for 9%

profile of v2, /device:TPU:6, one launch (start us, length us, event | category | flops | bytes accessed | tf_op | source)
XLA Modules:
  0.0 528.0 jit_solution(11614804223725458286)
XLA Ops:
  0.6 3.3 constant_dynamic-slice_fusion
  4.0 10.3 %all-to-all-start = ((bf16[64,48,384]{2,1,0:T(8,128)(2,1)}), bf16[64,48,384]{2,1,0:T(8,128)(2,1)}, u32[]{:S(2)}, u32[]{:S(2)}) async-start(bf16[64,48,384]{2,1,0:T(8,128)(2,1)} %bitcast.50), calls=%async_computation | async-start | bytes 4718592 | tf_op jit(solution)/shard_map/all_to_all | solution.py:358
  14.3 0.1 copy.31
  14.4 0.1 eq.42
  14.6 0.1 eq.38
  14.7 0.6 reduce-window.6
  15.3 0.2 slice_reduce_fusion
  15.5 0.1 fusion.2
  15.7 0.1 reduce_sum.21
  15.8 0.1 copy.34
  15.9 0.1 copy.35.slot_ref
  16.0 1.4 copy-done.3
  17.4 10.0 %dispatch.1 = bf16[3072,1536]{1,0:T(8,128)(2,1)} custom-call(s32[2,128]{1,0:T(2,128)S(1)} %copy.35.slot_ref, f32[2,128]{1,0:T(2,128)S(1)} %bitcast.46, bf16[128,6144]{1,0:T(8,128)(2,1)S(1)} %copy-done.2, bf16[128,6144]{1,0:T(8,128)(2,1)S(1)} %copy-done.2, bf16[128,6144]{1,0:T(8,128)(2,1)S(1)} %copy-done.3, bf16[128,6144]{1,0:T(8,128)(2,1)S(1)} %copy-done.3), custom_call_target="tpu_custom_call" | custom-call | flops 4831838208 | bytes 16777216 | tf_op jit(solution)/shard_map/dispatch/pallas_call | solution.py:62
  27.4 17.3 %all-to-all-done = bf16[64,48,384]{2,1,0:T(8,128)(2,1)} async-done(((bf16[64,48,384]{2,1,0:T(8,128)(2,1)}), bf16[64,48,384]{2,1,0:T(8,128)(2,1)}, u32[]{:S(2)}, u32[]{:S(2)}) %all-to-all-start) | async-done | bytes 2359328 | tf_op jit(solution)/shard_map/all_to_all | solution.py:358
  44.7 9.1 %all-to-all-start.1 = ((bf16[128,24,1536]{2,1,0:T(8,128)(2,1)}), bf16[128,24,1536]{2,1,0:T(8,128)(2,1)}, u32[]{:S(2)}, u32[]{:S(2)}) async-start(bf16[128,24,1536]{2,1,0:T(8,128)(2,1)} %bitcast.49), calls=%async_computation.1 | async-start | bytes 18874368 | tf_op jit(solution)/shard_map/all_to_all | solution.py:358
  53.9 0.1 select_reduce_fusion
  54.0 3.9 gather_fusion
  57.9 107.1 %all-to-all-done.1 = bf16[128,24,1536]{2,1,0:T(8,128)(2,1)} async-done(((bf16[128,24,1536]{2,1,0:T(8,128)(2,1)}), bf16[128,24,1536]{2,1,0:T(8,128)(2,1)}, u32[]{:S(2)}, u32[]{:S(2)}) %all-to-all-start.1) | async-done | bytes 9437216 | tf_op jit(solution)/shard_map/all_to_all | solution.py:358
  165.0 25.7 %all-to-all-start.2 = ((bf16[64,48,384]{2,1,0:T(8,128)(2,1)}), bf16[64,48,384]{2,1,0:T(8,128)(2,1)S(1)}, u32[]{:S(2)}, u32[]{:S(2)}) async-start(bf16[64,48,384]{2,1,0:T(8,128)(2,1)} %gather_fusion), calls=%async_computation.2 | async-start | bytes 4718592 | tf_op jit(solution)/shard_map/all_to_all | solution.py:358
  190.8 12.3 %expert_front.1 = (bf16[2,768,1536]{2,1,0:T(8,128)(2,1)}, bf16[2,768,1536]{2,1,0:T(8,128)(2,1)}, f32[768,384]{1,0:T(8,128)S(1)}, bf16[768,384]{1,0:T(8,128)(2,1)S(1)}) custom-call(s32[1]{0:T(128)} %bitcast.1.rank_ref, bf16[3072,1536]{1,0:T(8,128)(2,1)} %bitcast.9.recv_ref, bf16[2,2,1536,384]{3,2,1,0:T(8,128)(2,1)} %bitcast.52), custom_call_target="tpu_custom_call" | custom-call | flops 5000000000 | bytes 23068672 | tf_op jit(solution)/shard_map/expert_front/pallas_call | solution.py:136
  203.0 1.3 collective-permute-start
  204.4 26.1 %collective-permute-done.other_ref = bf16[768,384]{1,0:T(8,128)(2,1)S(1)} collective-permute-done((bf16[768,384]{1,0:T(8,128)(2,1)S(1)}, bf16[768,384]{1,0:T(8,128)(2,1)S(1)}, u32[]{:S(2)}, u32[]{:S(2)}) %collective-permute-start) | collective-permute-done | bytes 589856 | tf_op jit(solution)/shard_map/ppermute | solution.py:396
  230.5 14.4 %expert_rear.1 = (bf16[3072,1536]{1,0:T(8,128)(2,1)}, bf16[2,32,96,384]{3,2,1,0:T(8,128)(2,1)}) custom-call(s32[1]{0:T(128)} %bitcast.1.rank_ref, bf16[2,768,1536]{2,1,0:T(8,128)(2,1)} %get-tuple-element.29.x_ref, bf16[2,768,1536]{2,1,0:T(8,128)(2,1)} %get-tuple-element.30.c_ref, f32[768,384]{1,0:T(8,128)S(1)} %get-tuple-element.31.own_ref, ...), custom_call_target="tpu_custom_call" | custom-call | flops 7000000000 | bytes 35651584 | tf_op jit(solution)/shard_map/expert_rear/pallas_call | solution.py:229
  244.8 67.6 %all_to_all.71 = bf16[64,96,384]{2,1,0:T(8,128)(2,1)} all-to-all(bf16[64,96,384]{2,1,0:T(8,128)(2,1)} %bitcast.51), channel_id=1, replica_groups=mesh['expert'=64,'dp'=2] {'expert'}, dimensions={0} | all-to-all | bytes 9437184 | tf_op jit(solution)/shard_map/all_to_all | solution.py:358
  312.4 9.4 %all-to-all-start.4 = ((bf16[128,24,1536]{2,1,0:T(8,128)(2,1)}), bf16[128,24,1536]{2,1,0:T(8,128)(2,1)}, u32[]{:S(2)}, u32[]{:S(2)}) async-start(bf16[128,24,1536]{2,1,0:T(8,128)(2,1)} %bitcast.48), calls=%async_computation.4 | async-start | bytes 18874368 | tf_op jit(solution)/shard_map/all_to_all | solution.py:358
  321.8 5.7 %gather_fusion.1 = bf16[64,96,384]{2,1,0:T(8,128)(2,1)} fusion(bf16[64,96,384]{2,1,0:T(8,128)(2,1)} %all_to_all.71, s32[1024]{0:T(1024)S(1)} %pad_clamp_fusion), kind=kCustom, calls=%fused_computation.1 | custom fusion | bytes 9437440 | tf_op jit(solution)/shard_map/jit(_take)/gather | solution.py:364
  327.5 105.5 %all-to-all-done.4 = bf16[128,24,1536]{2,1,0:T(8,128)(2,1)} async-done(((bf16[128,24,1536]{2,1,0:T(8,128)(2,1)}), bf16[128,24,1536]{2,1,0:T(8,128)(2,1)}, u32[]{:S(2)}, u32[]{:S(2)}) %all-to-all-start.4) | async-done | bytes 9437216 | tf_op jit(solution)/shard_map/all_to_all | solution.py:358
  433.0 25.9 %all-to-all-start.5 = ((bf16[64,96,384]{2,1,0:T(8,128)(2,1)}), bf16[64,96,384]{2,1,0:T(8,128)(2,1)}, u32[]{:S(2)}, u32[]{:S(2)}) async-start(bf16[64,96,384]{2,1,0:T(8,128)(2,1)} %gather_fusion.1), calls=%async_computation.5 | async-start | bytes 9437184 | tf_op jit(solution)/shard_map/all_to_all | solution.py:358
  458.9 0.1 copy.36.prob_ref
  459.0 12.1 %combine.1 = (bf16[128,6144]{1,0:T(8,128)(2,1)}, bf16[128,6144]{1,0:T(8,128)(2,1)}) custom-call(s32[128,2]{1,0:T(8,128)S(1)} %add.7.slot_ref, f32[128,2]{1,0:T(8,128)S(1)} %copy.36.prob_ref, bf16[3072,1536]{1,0:T(8,128)(2,1)} %bitcast.20.back_ref), custom_call_target="tpu_custom_call" | custom-call | flops 7247757312 | bytes 13631488 | tf_op jit(solution)/shard_map/combine/pallas_call | solution.py:312
  471.1 48.6 %all-to-all-done.5 = bf16[64,96,384]{2,1,0:T(8,128)(2,1)} async-done(((bf16[64,96,384]{2,1,0:T(8,128)(2,1)}), bf16[64,96,384]{2,1,0:T(8,128)(2,1)}, u32[]{:S(2)}, u32[]{:S(2)}) %all-to-all-start.5) | async-done | bytes 4718624 | tf_op jit(solution)/shard_map/all_to_all | solution.py:358
  519.7 8.3 %final_step.1 = (bf16[3072,384]{1,0:T(8,128)(2,1)}, bf16[3072,384]{1,0:T(8,128)(2,1)}, bf16[3072,384]{1,0:T(8,128)(2,1)}) custom-call(bf16[6144,384]{1,0:T(8,128)(2,1)} %bitcast.22.both, bf16[3072,384]{1,0:T(8,128)(2,1)S(1)} %bitcast.44), custom_call_target="tpu_custom_call" | custom-call | flops 11796480 | bytes 14155776 | tf_op jit(solution)/shard_map/final_step/pallas_call | solution.py:343
  (18 shorter events, 0.1 us)
Async XLA Ops:
  3.9 10.3 %copy-start.4 = (s32[128,2]{0,1:T(2,128)S(1)}, s32[128,2]{0,1:T(2,128)}, u32[]{:S(2)}) copy-start(s32[128,2]{0,1:T(2,128)} %param.11) | copy-start | bytes 3076
  3.9 12.1 %copy-start = (f32[128,2]{0,1:T(2,128)S(1)}, f32[128,2]{0,1:T(2,128)}, u32[]{:S(2)}) copy-start(f32[128,2]{0,1:T(2,128)} %param.10) | copy-start | bytes 3076
  4.0 12.1 %copy-start.2 = (bf16[128,6144]{1,0:T(8,128)(2,1)S(1)}, bf16[128,6144]{1,0:T(8,128)(2,1)}, u32[]{:S(2)}) copy-start(bf16[128,6144]{1,0:T(8,128)(2,1)} %t1.1) | copy-start | bytes 4718596
  4.0 40.8 %all-to-all-start = ((bf16[64,48,384]{2,1,0:T(8,128)(2,1)}), bf16[64,48,384]{2,1,0:T(8,128)(2,1)}, u32[]{:S(2)}, u32[]{:S(2)}) async-start(bf16[64,48,384]{2,1,0:T(8,128)(2,1)} %bitcast.50), calls=%async_computation | async-start | bytes 4718592 | tf_op jit(solution)/shard_map/all_to_all | solution.py:358
  16.0 1.4 copy-start.3
  44.7 9.1 %copy-start.5 = (s32[64]{0:T(128)S(1)}, s32[64]{0:T(128)}, u32[]{:S(2)}) copy-start(s32[64]{0:T(128)} %param.12) | copy-start | bytes 772
  44.7 120.3 %all-to-all-start.1 = ((bf16[128,24,1536]{2,1,0:T(8,128)(2,1)}), bf16[128,24,1536]{2,1,0:T(8,128)(2,1)}, u32[]{:S(2)}, u32[]{:S(2)}) async-start(bf16[128,24,1536]{2,1,0:T(8,128)(2,1)} %bitcast.49), calls=%async_computation.1 | async-start | bytes 18874368 | tf_op jit(solution)/shard_map/all_to_all | solution.py:358
  165.0 79.8 %all-to-all-start.2 = ((bf16[64,48,384]{2,1,0:T(8,128)(2,1)}), bf16[64,48,384]{2,1,0:T(8,128)(2,1)S(1)}, u32[]{:S(2)}, u32[]{:S(2)}) async-start(bf16[64,48,384]{2,1,0:T(8,128)(2,1)} %gather_fusion), calls=%async_computation.2 | async-start | bytes 4718592 | tf_op jit(solution)/shard_map/all_to_all | solution.py:358
  190.7 39.7 %copy-start.1 = (bf16[1,3072,384]{2,1,0:T(8,128)(2,1)S(1)}, bf16[1,3072,384]{2,1,0:T(8,128)(2,1)}, u32[]{:S(2)}) copy-start(bf16[1,3072,384]{2,1,0:T(8,128)(2,1)} %param.14) | copy-start | bytes 7077892
  203.0 27.4 %collective-permute-start = (bf16[768,384]{1,0:T(8,128)(2,1)S(1)}, bf16[768,384]{1,0:T(8,128)(2,1)S(1)}, u32[]{:S(2)}, u32[]{:S(2)}) collective-permute-start(bf16[768,384]{1,0:T(8,128)(2,1)S(1)} %get-tuple-element.32), channel_id=1, source_target_pairs={{0,1},{1,0},{2,3},{3,2},{4,5},{5,4},{6,7},{7,6},{8,9},{9,8},{10,11... | collective-permute-start | bytes 1769480 | tf_op jit(solution)/shard_map/ppermute | solution.py:396
  312.4 120.6 %all-to-all-start.4 = ((bf16[128,24,1536]{2,1,0:T(8,128)(2,1)}), bf16[128,24,1536]{2,1,0:T(8,128)(2,1)}, u32[]{:S(2)}, u32[]{:S(2)}) async-start(bf16[128,24,1536]{2,1,0:T(8,128)(2,1)} %bitcast.48), calls=%async_computation.4 | async-start | bytes 18874368 | tf_op jit(solution)/shard_map/all_to_all | solution.py:358
  433.0 86.7 %all-to-all-start.5 = ((bf16[64,96,384]{2,1,0:T(8,128)(2,1)}), bf16[64,96,384]{2,1,0:T(8,128)(2,1)}, u32[]{:S(2)}, u32[]{:S(2)}) async-start(bf16[64,96,384]{2,1,0:T(8,128)(2,1)} %gather_fusion.1), calls=%async_computation.5 | async-start | bytes 9437184 | tf_op jit(solution)/shard_map/all_to_all | solution.py:358

commit v3 on v2

v3 whole, which is shorter than its diff:
```python
import functools
import jax
import jax.numpy as jnp
from jax import lax
from jax.experimental import pallas as pl
from jax.experimental.pallas import tpu as pltpu
from jax.sharding import PartitionSpec as P

BF = jnp.bfloat16
F32 = jnp.float32
MIB = 1024 * 1024
DISPATCH_VMEM, FRONT_VMEM, REAR_VMEM, COMBINE_VMEM = 56 * MIB, 48 * MIB, 56 * MIB, 40 * MIB
TILE = 512


def row_parts(shape, axis, cap):
    per = 4 * cap
    r = lax.broadcasted_iota(jnp.int32, shape, axis)
    e = r // per
    q = r - e * per
    h = q // (2 * cap)
    q = q - h * (2 * cap)
    a = q // cap
    return e * cap + q - a * cap, h, a


def dispatch_kernel(cap, experts, route_ref, prob_ref, t0, t1, c0, c1, out_ref, low, high, scale):
    per = 4 * cap
    rows = experts * per

    @pl.when((pl.program_id(0) == 0) & (pl.program_id(1) == 0))
    def _():
        tok = route_ref.shape[1]
        label = lax.broadcasted_iota(jnp.int32, (experts, tok), 0)
        one0 = jnp.where(label == route_ref[0:1, :], 1.0, 0.0)
        one1 = jnp.where(label == route_ref[1:2, :], 1.0, 0.0)
        before = lax.broadcasted_iota(jnp.int32, (tok, tok), 0) < lax.broadcasted_iota(
            jnp.int32, (tok, tok), 1
        )
        count = jnp.dot(
            (one0 + one1).astype(BF),
            jnp.where(before, 1.0, 0.0).astype(BF),
            preferred_element_type=F32,
        )
        earlier0 = jnp.sum(one0 * count, axis=0, keepdims=True).astype(jnp.int32)
        earlier1 = jnp.sum(one1 * count, axis=0, keepdims=True).astype(jnp.int32)
        ident, h, a = row_parts((rows, tok), 0, cap)
        hit0 = ident == route_ref[0:1, :] * cap + earlier0
        hit1 = ident == route_ref[1:2, :] * cap + earlier1
        hit = hit0 | hit1
        prob = jnp.where(hit0, prob_ref[0:1, :], 0.0) + jnp.where(hit1, prob_ref[1:2, :], 0.0)
        prob = jnp.sum(prob, axis=1, keepdims=True)
        scale[...] = jnp.where(a == 0, 1.0, prob)
        for ref, half in ((low, 0), (high, 1)):
            for kind in (0, 1):
                keep = hit & (h == half) & (a == kind)
                ref[:, kind * tok : (kind + 1) * tok] = jnp.where(keep, 1.0, 0.0).astype(BF)

    x0 = jnp.concatenate([t0[...], c0[...]], axis=0)
    x1 = jnp.concatenate([t1[...], c1[...]], axis=0)
    step = rows // 4
    for i in range(4):
        part = slice(i * step, (i + 1) * step)
        acc = jnp.dot(low[part, :], x0, preferred_element_type=F32)
        acc = acc + jnp.dot(high[part, :], x1, preferred_element_type=F32)
        acc = acc * scale[part, 0:1]
        for j in range(step // per):
            out_ref[i * (step // per) + j, 0] = acc[j * per : (j + 1) * per].astype(BF)


def dispatch(routes, probs, tokens, cotangent, experts, cap):
    tok, width = tokens.shape
    half = width // 4
    tiles = half // TILE
    per = 4 * cap
    rows = experts * per
    small = pl.BlockSpec((2, tok), lambda r, i: (0, 0))
    left = pl.BlockSpec((tok, TILE), lambda r, i: (0, 2 * r * tiles + i))
    right = pl.BlockSpec((tok, TILE), lambda r, i: (0, (2 * r + 1) * tiles + i))
    return pl.pallas_call(
        functools.partial(dispatch_kernel, cap, experts),
        grid=(2, tiles),
        in_specs=[small, small, left, right, left, right],
        out_specs=pl.BlockSpec((experts, 1, per, TILE), lambda r, i: (0, r, 0, i)),
        out_shape=jax.ShapeDtypeStruct((experts, 2, per, half), BF),
        scratch_shapes=[
            pltpu.VMEM((rows, 2 * tok), BF),
            pltpu.VMEM((rows, 2 * tok), BF),
            pltpu.VMEM((rows, 128), F32),
        ],
        compiler_params=pltpu.CompilerParams(vmem_limit_bytes=DISPATCH_VMEM),
        cost_estimate=pl.CostEstimate(
            flops=2 * rows * 2 * tok * width, bytes_accessed=16 * MIB, transcendentals=0
        ),
        name="dispatch",
    )(routes, probs, tokens, tokens, cotangent, cotangent)


def order_matrix(group, cap, inverse):
    n = group * cap * 4
    i = lax.broadcasted_iota(jnp.int32, (n, n), 1 if inverse else 0)
    j = lax.broadcasted_iota(jnp.int32, (n, n), 0 if inverse else 1)
    hk = i // (group * cap)
    rest = i - hk * (group * cap)
    src = rest // cap
    slot = rest - src * cap
    return jnp.where(src * (4 * cap) + hk * cap + slot == j, 1.0, 0.0).astype(BF)


def front_kernel(cap, group, rank_ref, recv_ref, w_ref, x_ref, c_ref, sum_ref, send_ref, fore):
    i = pl.program_id(0)
    n = group * cap
    span = 4 * n
    sets = recv_ref.shape[0] // span
    hidden = sum_ref.shape[1] // 3

    @pl.when(i == 0)
    def _():
        fore[...] = order_matrix(group, cap, False)
        sum_ref[...] = jnp.zeros_like(sum_ref)

    for g in range(sets):
        got = jnp.dot(
            fore[...], recv_ref[g * span : (g + 1) * span, :], preferred_element_type=F32
        ).astype(BF)
        at = slice(g * n, (g + 1) * n)
        for h in range(2):
            x_ref[h, at, :] = got[2 * h * n : (2 * h + 1) * n]
            c_ref[h, at, :] = got[(2 * h + 1) * n : (2 * h + 2) * n]
    for h in range(2):
        sum_ref[:, : 2 * hidden] += jnp.dot(
            x_ref[h], w_ref[0, h, :, : 2 * hidden], preferred_element_type=F32
        )
        sum_ref[:, 2 * hidden :] += jnp.dot(
            c_ref[h], w_ref[0, h, :, 2 * hidden :], preferred_element_type=F32
        )

    @pl.when(i == pl.num_programs(0) - 1)
    def _():
        send_ref[...] = sum_ref[...].astype(BF)


GROUP = 8


def front_call(rank, recv, weight, cap):
    total, half = recv.shape
    columns = weight.shape[-1]
    tiles = half // TILE
    rows = total // 4
    n = GROUP * cap * 4
    held = pl.BlockSpec((2, rows, TILE), lambda i, r: (0, 0, i))
    small = pl.BlockSpec((rows, columns), lambda i, r: (0, 0))
    return pl.pallas_call(
        functools.partial(front_kernel, cap, GROUP),
        grid_spec=pltpu.PrefetchScalarGridSpec(
            num_scalar_prefetch=1,
            grid=(tiles,),
            in_specs=[
                pl.BlockSpec((total, TILE), lambda i, r: (0, i)),
                pl.BlockSpec((1, 2, TILE, columns), lambda i, r: (r[0], 0, i, 0)),
            ],
            out_specs=[held, held, small, small],
            scratch_shapes=[pltpu.VMEM((n, n), BF)],
        ),
        out_shape=[
            jax.ShapeDtypeStruct((2, rows, half), BF),
            jax.ShapeDtypeStruct((2, rows, half), BF),
            jax.ShapeDtypeStruct((rows, columns), F32),
            jax.ShapeDtypeStruct((rows, columns), BF),
        ],
        compiler_params=pltpu.CompilerParams(vmem_limit_bytes=FRONT_VMEM),
        cost_estimate=pl.CostEstimate(
            flops=5 * 10**9, bytes_accessed=22 * 1024 * 1024, transcendentals=0
        ),
        name="expert_front",
    )(rank, recv, weight.reshape(2, 2, half, columns))


def rear_kernel(
    cap, group, piece, rank_ref, x_ref, c_ref, own_ref, other_ref, w_ref, first_ref, second_ref,
    out_ref, state_ref, inner, pre, back
):
    i = pl.program_id(0)
    n = group * cap
    span = 4 * n
    sets = out_ref.shape[0] // span
    hidden = inner.shape[1]

    @pl.when(i == 0)
    def _():
        back[...] = order_matrix(group, cap, True)
        total = own_ref[...] + other_ref[...].astype(F32)
        gate = total[:, :hidden]
        up = total[:, hidden : 2 * hidden]
        grad = total[:, 2 * hidden :]
        sig = jax.nn.sigmoid(gate)
        active = gate * sig
        inner[...] = (active * up).astype(BF)
        slope = sig * (1.0 + gate * (1.0 - sig))
        pre[:, :hidden] = (grad * up * slope).astype(BF)
        pre[:, hidden:] = (grad * active).astype(BF)

    contract = (((1,), (1,)), ((), ()))
    lead = (((0,), (0,)), ((), ()))
    made = []
    for h in range(2):
        made.append(
            lax.dot_general(
                inner[...], w_ref[0, h, :, 2 * hidden :], contract, preferred_element_type=F32
            ).astype(BF)
        )
        made.append(
            lax.dot_general(
                pre[...], w_ref[0, h, :, : 2 * hidden], contract, preferred_element_type=F32
            ).astype(BF)
        )
    for g in range(sets):
        stack = jnp.concatenate([m[g * n : (g + 1) * n] for m in made], axis=0)
        out_ref[g * span : (g + 1) * span, :] = jnp.dot(
            back[...], stack, preferred_element_type=F32
        ).astype(BF)
    for h in range(2):
        for source, factor, at in (
            (x_ref, pre, slice(0, 2 * hidden)),
            (c_ref, inner, slice(2 * hidden, 3 * hidden)),
        ):
            grad = lax.dot_general(source[h], factor[...], lead, preferred_element_type=F32)
            m = 0.9 * first_ref[h, :, at].astype(F32) + 0.1 * grad
            v = 0.95 * second_ref[h, :, at].astype(F32) + 0.05 * grad * grad
            step = m / (jnp.sqrt(v) + 1e-08) + 0.1 * w_ref[0, h, :, at].astype(F32)
            for k, value in enumerate((m, v, step)):
                value = value.astype(BF)
                for j in range(grad.shape[0] // piece):
                    state_ref[h, j, k * piece : (k + 1) * piece, at] = value[
                        j * piece : (j + 1) * piece
                    ]


def rear_call(rank, x, c, own, other, weight, first, second, cap, piece):
    half = x.shape[2]
    rows, columns = own.shape
    hidden = columns // 3
    tile = 8 * piece
    tiles = half // tile
    total = 4 * rows
    n = GROUP * cap * 4
    held = pl.BlockSpec((2, rows, tile), lambda i, r: (0, 0, i))
    small = pl.BlockSpec((rows, columns), lambda i, r: (0, 0))
    moment = pl.BlockSpec((2, tile, columns), lambda i, r: (0, i, 0))
    return pl.pallas_call(
        functools.partial(rear_kernel, cap, GROUP, piece),
        grid_spec=pltpu.PrefetchScalarGridSpec(
            num_scalar_prefetch=1,
            grid=(tiles,),
            in_specs=[
                held,
                held,
                small,
                small,
                pl.BlockSpec((1, 2, tile, columns), lambda i, r: (r[0], 0, i, 0)),
                moment,
                moment,
            ],
            out_specs=[
                pl.BlockSpec((total, tile), lambda i, r: (0, i)),
                pl.BlockSpec((2, 8, 3 * piece, columns), lambda i, r: (0, i, 0, 0)),
            ],
            scratch_shapes=[
                pltpu.VMEM((rows, hidden), BF),
                pltpu.VMEM((rows, 2 * hidden), BF),
                pltpu.VMEM((n, n), BF),
            ],
        ),
        out_shape=[
            jax.ShapeDtypeStruct((total, half), BF),
            jax.ShapeDtypeStruct((2, half // piece, 3 * piece, columns), BF),
        ],
        compiler_params=pltpu.CompilerParams(vmem_limit_bytes=REAR_VMEM),
        cost_estimate=pl.CostEstimate(
            flops=7 * 10**9, bytes_accessed=36 * 1024 * 1024, transcendentals=rows * hidden
        ),
        name="expert_rear",
    )(
        rank, x, c, own, other, weight.reshape(2, 2, half, columns),
        first.reshape(2, half, columns), second.reshape(2, half, columns),
    )


def combine_kernel(cap, tiles, meta_ref, back_ref, mixed_ref, grad_ref, pick):
    total = back_ref.shape[0]
    tok = mixed_ref.shape[0]
    i = pl.program_id(0)

    @pl.when(i == 0)
    def _():
        ident, part, a = row_parts((tok, total), 1, cap)
        index = ident // cap
        ident = index // 2 * cap + ident - index * cap
        chunk = (index - index // 2 * 2) * 2 + part
        hit0 = ident == meta_ref[:, 0:1].astype(jnp.int32)
        hit1 = ident == meta_ref[:, 1:2].astype(jnp.int32)
        for k in range(4):
            here = chunk == k
            out = here & (a == 0)
            pick[3 * k] = jnp.where(hit0 & out, 1.0, 0.0).astype(BF)
            pick[3 * k + 1] = jnp.where(hit1 & out, 1.0, 0.0).astype(BF)
            pick[3 * k + 2] = jnp.where((hit0 | hit1) & here & (a == 1), 1.0, 0.0).astype(BF)

    block = back_ref[...]
    for k in range(4):
        at = pl.ds(pl.multiple_of((k * tiles + i) * TILE, TILE), TILE)
        one = jnp.dot(pick[3 * k], block, preferred_element_type=F32)
        two = jnp.dot(pick[3 * k + 1], block, preferred_element_type=F32)
        both = jnp.dot(pick[3 * k + 2], block, preferred_element_type=F32)
        mixed_ref[:, at] = (one * meta_ref[:, 2:3] + two * meta_ref[:, 3:4]).astype(BF)
        grad_ref[:, at] = both.astype(BF)


def combine(meta, back, cap):
    total, half = back.shape
    tok = meta.shape[0]
    tiles = half // TILE
    whole = pl.BlockSpec((tok, 4 * half), lambda i: (0, 0))
    shape = jax.ShapeDtypeStruct((tok, 4 * half), BF)
    return pl.pallas_call(
        functools.partial(combine_kernel, cap, tiles),
        grid=(tiles,),
        in_specs=[
            pl.BlockSpec((tok, 4), lambda i: (0, 0)),
            pl.BlockSpec((total, TILE), lambda i: (0, i)),
        ],
        out_specs=[whole, whole],
        out_shape=[shape, shape],
        scratch_shapes=[pltpu.VMEM((12, tok, total), BF)],
        compiler_params=pltpu.CompilerParams(vmem_limit_bytes=COMBINE_VMEM),
        cost_estimate=pl.CostEstimate(
            flops=2 * 12 * tok * total * half, bytes_accessed=13 * MIB, transcendentals=0
        ),
        name="combine",
    )(meta, back)


def reorder_kernel(order_ref, source, out):
    def body(j, carry):
        out[j] = source[order_ref[j]]
        return carry

    lax.fori_loop(0, out.shape[0], body, 0)


def reorder(array, inverse, count):
    shape = (count, array.shape[0] // count, array.shape[1])
    whole = pl.BlockSpec(memory_space=pltpu.VMEM)
    return pl.pallas_call(
        reorder_kernel,
        in_specs=[pl.BlockSpec(memory_space=pltpu.SMEM), whole],
        out_specs=whole,
        out_shape=jax.ShapeDtypeStruct(shape, BF),
        compiler_params=pltpu.CompilerParams(vmem_limit_bytes=4 * MIB),
        cost_estimate=pl.CostEstimate(
            flops=0, bytes_accessed=4 * array.size, transcendentals=0
        ),
        name="reorder",
    )(inverse, array.reshape(shape))


def swap(array, axes="expert"):
    return lax.all_to_all(array, axes, split_axis=0, concat_axis=0, tiled=True)


def slot_table(routes, experts, cap):
    ids = routes.reshape(-1)
    labels = jnp.arange(experts, dtype=jnp.int32)
    onehot = (ids[:, None] == labels[None, :]).astype(jnp.int32)
    earlier = jnp.sum((jnp.cumsum(onehot, axis=0) - onehot) * onehot, axis=1)
    return (ids * cap + earlier).reshape(routes.shape)


def local(tokens, cotangent, gate_probs, routes, placement, weights, first_moment, second_moment):
    experts = lax.axis_size("expert")
    tok, width = tokens.shape
    top = routes.shape[1]
    cap = max(2, (3 * tok * top + 2 * experts - 1) // (2 * experts))
    labels = jnp.arange(experts, dtype=jnp.int32)
    inverse = jnp.sum(
        labels[None, :] * (placement[None, :] == labels[:, None]).astype(jnp.int32), axis=1
    )
    inverse = jnp.minimum(inverse, experts - 1)
    rank = lax.axis_index("dp")
    weight = weights[0]
    rows = weight.shape[0] // 2
    piece = rows // experts
    columns = weight.shape[1]
    both = ("expert", "dp")
    together = lax.optimization_barrier

    place = rank.reshape(1).astype(jnp.int32)
    send = dispatch(routes.T, gate_probs.T, tokens, cotangent, experts, cap)
    send, routes, probs, inverse, place = together((send, routes, gate_probs, inverse, place))
    slots = slot_table(routes, experts, cap)
    meta = jnp.concatenate([slots.astype(F32), probs], axis=1)
    send, meta = together((send, meta))
    recv = swap(send.reshape(-1, width // 4), both)
    recv, meta, inverse, place = together((recv, meta, inverse, place))
    x, c, own, out = front_call(place, recv, weight, cap)
    other = lax.ppermute(out, "dp", [(0, 1), (1, 0)])
    result, state = rear_call(
        place, x, c, own, other, weight, first_moment[0], second_moment[0], cap, piece
    )
    result, state, meta, inverse = together((result, state, meta, inverse))
    spread = swap(state.reshape(3 * rows, columns))
    spread, result, meta, inverse = together((spread, result, meta, inverse))
    ready = reorder(spread, inverse, experts).reshape(3 * rows, columns)
    ready, result, meta = together((ready, result, meta))
    back = swap(result, both)
    ready, back, meta = together((ready, back, meta))
    moved = swap(ready).reshape(experts, 3, piece, columns)
    mixed, token_grad = combine(meta, back, cap)
    m, v, step = (moved[:, k].reshape(1, rows, columns) for k in range(3))
    return (mixed, token_grad, m, v, step)


def solution(mesh):
    in_specs = (
        P(("expert", "dp"), None),
        P(("expert", "dp"), None),
        P(("expert", "dp"), None),
        P(("expert", "dp"), None),
        P(),
        P("expert", None, None),
        P("expert", "dp", None),
        P("expert", "dp", None),
    )
    out_specs = (
        P(("expert", "dp"), None),
        P(("expert", "dp"), None),
        P("expert", "dp", None),
        P("expert", "dp", None),
        P("expert", "dp", None),
    )
    return jax.shard_map(local, mesh=mesh, in_specs=in_specs, out_specs=out_specs, check_vma=False)
```

time: 529 us -> 501 us (0.947)
  blocking collectives: 67.6 us -> 330 us
  waiting for transfers between devices: 305 us -> 82.9 us
  starting transfers between devices: 81.8 us -> 8.4 us
  Pallas kernels: 56.9 us -> 62.3 us
    all_to_all x1 -> x3, blocking collectives: 67.6 us -> 330 us  [swap(): return lax.all_to_all(array, axes, split_axis=0, concat_axis=0, tiled=True)]
    all_to_all x5 -> x1, waiting for transfers between devices: 279 us -> 67.4 us  [swap(): return lax.all_to_all(array, axes, split_axis=0, concat_axis=0, tiled=True)]
    all_to_all x5 -> x1, starting transfers between devices: 80.4 us -> 7.66 us  [swap(): return lax.all_to_all(array, axes, split_axis=0, concat_axis=0, tiled=True)]
    ppermute x1, waiting for transfers between devices: 26.1 us -> 15.5 us  [local(): other = lax.ppermute(out, 'dp', [(0, 1), (1, 0)])]
    gather x2 -> x0, local copies, waits for them, and re-layouts: 9.64 us -> none  [reorder(): return jnp.take(pieces, inverse, axis=0, mode='clip').reshape(array.shape)]
    slice x1 -> x2, local copies, waits for them, and re-layouts: 0.18 us -> 6.49 us  [the longest x1 6.3 us: local(): m, v, step = (moved[:, k].reshape(1, rows, columns) for k in range(3))]
  transfers between devices with their start and end apart: 6 -> 2, of which waited for: 5 -> 2; matrix products, arithmetic and copies ran while one was open for 2% -> 0% of each run, Pallas kernels for 9% -> 4%
where the time goes in v3:
time: 501 us; the launch traced here: 499 us
  blocking collectives  330 us (66%)
  waiting for transfers between devices  82.9 us (17%)
  Pallas kernels  62.3 us (12%)
  local copies, waits for them, and re-layouts  12.7 us (3%)
  starting transfers between devices  8.4 us (2%)
    all_to_all x3, blocking collectives, swap(): return lax.all_to_all(array, axes, split_axis=0, concat_axis=0, tiled=True)  330 us
    all_to_all x1, waiting for transfers between devices, swap(): return lax.all_to_all(array, axes, split_axis=0, concat_axis=0, tiled=True)  67.4 us
    pallas_call x1, Pallas kernels, combine(): pl.pallas_call(functools.partial(combine_kernel, cap, tiles), grid=(tiles...  20.4 us
    pallas_call x1, Pallas kernels, rear_call(): pl.pallas_call(functools.partial(rear_kernel, cap, GROUP, piece), grid_sp...  16.4 us
    ppermute x1, waiting for transfers between devices, local(): other = lax.ppermute(out, 'dp', [(0, 1), (1, 0)])  15.5 us
    pallas_call x1, Pallas kernels, front_call(): pl.pallas_call(functools.partial(front_kernel, cap, GROUP), grid_spec=plt...  12 us
    pallas_call x1, Pallas kernels, dispatch(): pl.pallas_call(functools.partial(dispatch_kernel, cap, experts), grid=(2,...  11.8 us
  transfers between devices with their start and end apart: 2, of which 2 were waited for; matrix products, arithmetic and copies ran while one was open for 0% of the time, Pallas kernels for 4%

profile of v3, /device:TPU:6, one launch (start us, length us, event | category | flops | bytes accessed | tf_op | source)
XLA Modules:
  0.0 498.5 jit_solution(7664783516389150614)
XLA Ops:
  0.6 0.8 select_reduce_fusion
  1.4 0.0 copy-start.3
  1.4 0.0 copy-start.4
  1.4 11.8 %dispatch.1 = bf16[64,2,24,1536]{3,2,1,0:T(8,128)(2,1)} custom-call(s32[2,128]{1,0:T(2,128)} %bitcast.48, f32[2,128]{1,0:T(2,128)} %bitcast.49, bf16[128,6144]{1,0:T(8,128)(2,1)} %t1.1, bf16[128,6144]{1,0:T(8,128)(2,1)} %t1.1, bf16[128,6144]{1,0:T(8,128)(2,1)} %c1.1, bf16[128,6144]{1,0:T(8,128)(2,1)} %c1.1), custom_call_target="tpu_custom_call" | custom-call | flops 4831838208 | bytes 16777216 | tf_op jit(solution)/shard_map/dispatch/pallas_call | solution.py:80
  13.3 0.0 copy-done.3
  13.3 0.1 copy.36
  13.4 0.1 eq.45
  13.5 0.1 eq.41
  13.7 0.6 reduce-window.6
  14.3 0.2 slice_reduce_fusion
  14.5 0.1 fusion.2
  14.6 0.1 reduce_sum.22
  14.8 0.1 copy.39
  14.8 0.0 copy-done.4
  14.9 120.5 %all_to_all.45 = bf16[128,24,1536]{2,1,0:T(8,128)(2,1)} all-to-all(bf16[128,24,1536]{2,1,0:T(8,128)(2,1)} %bitcast.39), channel_id=1, replica_groups=mesh['expert'=64,'dp'=2] {'expert','dp'}, dimensions={0} | all-to-all | bytes 18874368 | tf_op jit(solution)/shard_map/all_to_all | solution.py:369
  135.4 12.0 %expert_front.1 = (bf16[2,768,1536]{2,1,0:T(8,128)(2,1)}, bf16[2,768,1536]{2,1,0:T(8,128)(2,1)}, f32[768,384]{1,0:T(8,128)S(1)}, bf16[768,384]{1,0:T(8,128)(2,1)S(1)}) custom-call(s32[1]{0:T(128)} %bitcast.2.rank_ref, bf16[3072,1536]{1,0:T(8,128)(2,1)} %bitcast.43, bf16[2,2,1536,384]{3,2,1,0:T(8,128)(2,1)} %bitcast.50), custom_call_target="tpu_custom_call" | custom-call | flops 5000000000 | bytes 23068672 | tf_op jit(solution)/shard_map/expert_front/pallas_call | solution.py:154
  147.5 1.0 copy-done.2
  148.5 0.7 collective-permute-start
  149.2 15.5 %collective-permute-done.other_ref = bf16[768,384]{1,0:T(8,128)(2,1)S(1)} collective-permute-done((bf16[768,384]{1,0:T(8,128)(2,1)S(1)}, bf16[768,384]{1,0:T(8,128)(2,1)S(1)}, u32[]{:S(2)}, u32[]{:S(2)}) %collective-permute-start) | collective-permute-done | bytes 589856 | tf_op jit(solution)/shard_map/ppermute | solution.py:407
  164.7 0.8 copy-done.5
  165.5 16.4 %expert_rear.1 = (bf16[3072,1536]{1,0:T(8,128)(2,1)}, bf16[2,32,144,384]{3,2,1,0:T(8,128)(2,1)}) custom-call(s32[1]{0:T(128)} %bitcast.2.rank_ref, bf16[2,768,1536]{2,1,0:T(8,128)(2,1)} %get-tuple-element.47.x_ref, bf16[2,768,1536]{2,1,0:T(8,128)(2,1)} %get-tuple-element.48.c_ref, f32[768,384]{1,0:T(8,128)} %copy-done.2, bf16[768,384]{1,0:T(8,128)(2,1)} %copy-done.5, ...), custom_call_target="tpu_custom_call" | custom-call | flops 7000000000 | bytes 37748736 | tf_op jit(solution)/shard_map/expert_rear/pallas_call | solution.py:251
  181.9 92.7 %all_to_all.46 = bf16[64,144,384]{2,1,0:T(8,128)(2,1)S(1)} all-to-all(bf16[64,144,384]{2,1,0:T(8,128)(2,1)} %bitcast.44), channel_id=1, replica_groups=mesh['expert'=64,'dp'=2] {'expert'}, dimensions={0} | all-to-all | bytes 14155776 | tf_op jit(solution)/shard_map/all_to_all | solution.py:369
  274.7 1.7 reorder.1
  276.3 0.0 copy-start
  276.3 0.0 slice-done
  276.4 116.6 %all_to_all.47 = bf16[128,24,1536]{2,1,0:T(8,128)(2,1)} all-to-all(bf16[128,24,1536]{2,1,0:T(8,128)(2,1)S(1)} %bitcast.42), channel_id=1, replica_groups=mesh['expert'=64,'dp'=2] {'expert','dp'}, dimensions={0} | all-to-all | bytes 18874368 | tf_op jit(solution)/shard_map/all_to_all | solution.py:369
  393.0 7.7 %all-to-all-start.3 = ((bf16[64,144,384]{2,1,0:T(8,128)(2,1)}), bf16[64,144,384]{2,1,0:T(8,128)(2,1)}, u32[]{:S(2)}, u32[]{:S(2)}) async-start(bf16[64,144,384]{2,1,0:T(8,128)(2,1)} %copy-done), calls=%async_computation.3 | async-start | bytes 14155776 | tf_op jit(solution)/shard_map/all_to_all | solution.py:369
  400.6 0.1 copy.40.meta_ref
  400.8 3.7 copy-done.1
  404.4 20.4 %combine.1 = (bf16[128,6144]{1,0:T(8,128)(2,1)}, bf16[128,6144]{1,0:T(8,128)(2,1)}) custom-call(f32[128,4]{1,0:T(8,128)S(1)} %copy.40.meta_ref, bf16[3072,1536]{1,0:T(8,128)(2,1)S(1)} %bitcast.38), custom_call_target="tpu_custom_call" | custom-call | flops 14495514624 | bytes 13631488 | tf_op jit(solution)/shard_map/combine/pallas_call | solution.py:326
  424.8 67.4 %all-to-all-done.3 = bf16[64,144,384]{2,1,0:T(8,128)(2,1)} async-done(((bf16[64,144,384]{2,1,0:T(8,128)(2,1)}), bf16[64,144,384]{2,1,0:T(8,128)(2,1)}, u32[]{:S(2)}, u32[]{:S(2)}) %all-to-all-start.3) | async-done | bytes 7077920 | tf_op jit(solution)/shard_map/all_to_all | solution.py:369
  492.2 6.3 %fusion.4 = (bf16[64,1,48,384]{3,2,1,0:T(8,128)(2,1)}, bf16[64,1,48,384]{3,2,1,0:T(8,128)(2,1)}, bf16[64,1,48,384]{3,2,1,0:T(8,128)(2,1)}) fusion(bf16[64,3,48,384]{3,2,1,0:T(8,128)(2,1)} %bitcast.16), kind=kLoop, calls=%fused_computation.14 | loop fusion | bytes 14155776 | tf_op jit(solution)/shard_map/slice | solution.py:420
  (16 shorter events, 0.1 us)
Async XLA Ops:
  1.4 11.9 %copy-start.3 = (s32[128,2]{0,1:T(2,128)S(1)}, s32[128,2]{0,1:T(2,128)}, u32[]{:S(2)}) copy-start(s32[128,2]{0,1:T(2,128)} %param.11) | copy-start | bytes 3076
  1.4 13.4 %copy-start.4 = (f32[128,2]{0,1:T(2,128)S(1)}, f32[128,2]{0,1:T(2,128)}, u32[]{:S(2)}) copy-start(f32[128,2]{0,1:T(2,128)} %param.10) | copy-start | bytes 3076
  147.5 1.0 copy-start.2
  148.5 16.2 %collective-permute-start = (bf16[768,384]{1,0:T(8,128)(2,1)S(1)}, bf16[768,384]{1,0:T(8,128)(2,1)S(1)}, u32[]{:S(2)}, u32[]{:S(2)}) collective-permute-start(bf16[768,384]{1,0:T(8,128)(2,1)S(1)} %get-tuple-element.50), channel_id=1, source_target_pairs={{0,1},{1,0},{2,3},{3,2},{4,5},{5,4},{6,7},{7,6},{8,9},{9,8},{10,11... | collective-permute-start | bytes 1769480 | tf_op jit(solution)/shard_map/ppermute | solution.py:407
  164.7 0.8 copy-start.5
  181.9 94.4 %slice-start = ((s8[9437184]{0:T(1024)(128)(4,1)}), s8[4194304]{0:T(1024)(128)(4,1)S(1)}, s32[]{:S(2)}) async-start(s8[9437184]{0:T(1024)(128)(4,1)} %bitcast.40), calls=%async_computation.4 | async-start | bytes 8388608
  181.9 94.4 %slice-start.1 = ((s8[9437184]{0:T(1024)(128)(4,1)}), s8[4194304]{0:T(1024)(128)(4,1)S(1)}, s32[]{:S(2)}) async-start(s8[9437184]{0:T(1024)(128)(4,1)} %bitcast.40), calls=%async_computation.5 | async-start | bytes 8388608
  274.7 1.7 slice-start.2
  276.3 116.7 %copy-start = (bf16[64,144,384]{2,1,0:T(8,128)(2,1)}, bf16[64,144,384]{2,1,0:T(8,128)(2,1)S(1)}, u32[]{:S(2)}) copy-start(bf16[64,144,384]{2,1,0:T(8,128)(2,1)S(1)} %reorder.1) | copy-start | bytes 21233668
  393.0 99.2 %all-to-all-start.3 = ((bf16[64,144,384]{2,1,0:T(8,128)(2,1)}), bf16[64,144,384]{2,1,0:T(8,128)(2,1)}, u32[]{:S(2)}, u32[]{:S(2)}) async-start(bf16[64,144,384]{2,1,0:T(8,128)(2,1)} %copy-done), calls=%async_computation.3 | async-start | bytes 14155776 | tf_op jit(solution)/shard_map/all_to_all | solution.py:369
  400.8 3.7 copy-start.1

commit v4 on v0

v4 whole, which is shorter than its diff:
```python
import functools
import jax
import jax.numpy as jnp
from jax import lax
from jax.experimental import pallas as pl
from jax.experimental.pallas import tpu as pltpu
from jax.sharding import PartitionSpec as P

BF = jnp.bfloat16
F32 = jnp.float32
MIB = 1024 * 1024
DISPATCH_VMEM, FRONT_VMEM, SORT_VMEM = 60 * MIB, 12 * MIB, 12 * MIB
REAR_VMEM, COMBINE_VMEM = 16 * MIB, 24 * MIB
TILE = 512


def slots_of(route, experts, cap):
    tok = route.shape[1]
    label = lax.broadcasted_iota(jnp.int32, (experts, tok), 0)
    one0 = jnp.where(label == route[0:1, :], 1.0, 0.0)
    one1 = jnp.where(label == route[1:2, :], 1.0, 0.0)
    before = lax.broadcasted_iota(jnp.int32, (tok, tok), 0) < lax.broadcasted_iota(
        jnp.int32, (tok, tok), 1
    )
    count = jnp.dot(
        (one0 + one1).astype(BF),
        jnp.where(before, 1.0, 0.0).astype(BF),
        preferred_element_type=F32,
    )
    earlier0 = jnp.sum(one0 * count, axis=0, keepdims=True).astype(jnp.int32)
    earlier1 = jnp.sum(one1 * count, axis=0, keepdims=True).astype(jnp.int32)
    return route[0:1, :] * cap + earlier0, route[1:2, :] * cap + earlier1


def dispatch_kernel(
    cap, experts, route_ref, prob_ref, token_ref, cot_ref, out_ref, rows_in, low, high, scale,
    route, probs, stage, sem, out_sem
):
    tok, width = token_ref.shape
    per = 4 * cap
    small = [
        pltpu.make_async_copy(route_ref, route, sem.at[2]),
        pltpu.make_async_copy(prob_ref, probs, sem.at[3]),
    ]
    loads = [
        pltpu.make_async_copy(token_ref, rows_in.at[pl.ds(0, tok), :], sem.at[0]),
        pltpu.make_async_copy(cot_ref, rows_in.at[pl.ds(tok, tok), :], sem.at[1]),
    ]
    for load in small + loads:
        load.start()
    for load in small:
        load.wait()
    slot0, slot1 = slots_of(route[...], experts, cap)
    reach = 2 * per // 3
    shape = (experts, reach, tok)
    for half, ref in ((0, low), (1, high)):
        at = lax.broadcasted_iota(jnp.int32, shape, 1) + half * (reach // 2 - 2 * cap)
        ok = (at >= 0) & (at < 2 * cap)
        a = jnp.where(at >= cap, 1, 0)
        ident = lax.broadcasted_iota(jnp.int32, shape, 0) * cap + at - cap * a
        ident = jnp.where(ok, ident, -1).reshape(experts * reach, tok)
        a = a.reshape(experts * reach, tok)
        hit0 = ident == slot0
        hit1 = ident == slot1
        hit = hit0 | hit1
        for kind in (0, 1):
            ref[:, kind * tok : (kind + 1) * tok] = jnp.where(
                hit & (a == kind), 1.0, 0.0
            ).astype(BF)
        prob = jnp.where(hit0, probs[0:1, :], 0.0) + jnp.where(hit1, probs[1:2, :], 0.0)
        prob = jnp.sum(prob, axis=1, keepdims=True)
        scale[half] = jnp.where(a == 0, 1.0, prob)
    for load in loads:
        load.wait()
    half_width = width // 4
    lot = 16

    tiles = half_width // TILE
    sends = [
        pltpu.make_async_copy(
            stage.at[i], out_ref.at[:, :, :, pl.ds(i * TILE, TILE)], out_sem.at[i]
        )
        for i in range(tiles)
    ]
    for i in range(tiles):
        for r in range(2):
            first, second = (
                rows_in[:, (2 * r + h) * half_width + i * TILE :][:, :TILE] for h in range(2)
            )

            def body(g, carry):
                part = pl.ds(pl.multiple_of(g * lot * reach, lot * reach), lot * reach)
                y0 = jnp.dot(low[part, :], first, preferred_element_type=F32)
                y1 = jnp.dot(high[part, :], second, preferred_element_type=F32)
                y0 = y0 * scale[0, part, 0:1]
                y1 = y1 * scale[1, part, 0:1]
                mid = reach // 2
                for j in range(lot):
                    base = j * reach
                    made = [
                        y0[base : base + mid],
                        y0[base + mid : base + reach] + y1[base : base + mid],
                        y1[base + mid : base + reach],
                    ]
                    stage[i, g * lot + j, r] = jnp.concatenate(made, axis=0).astype(BF)
                return carry

            lax.fori_loop(0, experts // lot, body, 0)
        sends[i].start()
    for send in sends:
        send.wait()


def dispatch(routes, probs, tokens, cotangent, experts, cap):
    tok, width = tokens.shape
    half = width // 4
    per = 4 * cap
    rows = experts * per * 2 // 3
    anywhere = pl.BlockSpec(memory_space=pltpu.HBM)
    return pl.pallas_call(
        functools.partial(dispatch_kernel, cap, experts),
        in_specs=[anywhere] * 4,
        out_specs=anywhere,
        out_shape=jax.ShapeDtypeStruct((experts, 2, per, half), BF),
        scratch_shapes=[
            pltpu.VMEM((2 * tok, width), BF),
            pltpu.VMEM((rows, 2 * tok), BF),
            pltpu.VMEM((rows, 2 * tok), BF),
            pltpu.VMEM((2, rows, 128), F32),
            pltpu.VMEM((2, tok), jnp.int32),
            pltpu.VMEM((2, tok), F32),
            pltpu.VMEM((half // TILE, experts, 2, per, TILE), BF),
            pltpu.SemaphoreType.DMA((4,)),
            pltpu.SemaphoreType.DMA((half // TILE,)),
        ],
        compiler_params=pltpu.CompilerParams(vmem_limit_bytes=DISPATCH_VMEM),
        cost_estimate=pl.CostEstimate(
            flops=3 * 10**9, bytes_accessed=13 * MIB, transcendentals=0
        ),
        name="dispatch",
    )(routes, probs, tokens, cotangent)


def order_matrix(group, cap, inverse):
    n = group * cap * 4
    i = lax.broadcasted_iota(jnp.int32, (n, n), 1 if inverse else 0)
    j = lax.broadcasted_iota(jnp.int32, (n, n), 0 if inverse else 1)
    hk = i // (group * cap)
    rest = i - hk * (group * cap)
    src = rest // cap
    slot = rest - src * cap
    return jnp.where(src * (4 * cap) + hk * cap + slot == j, 1.0, 0.0).astype(BF)


def unmix(fore, recv_ref, first, columns, group, cap):
    n = group * cap
    span = 4 * n
    made = [[] for _ in range(4)]
    for g in range(first.stop // span - first.start // span):
        rows = slice(first.start + g * span, first.start + (g + 1) * span)
        got = jnp.dot(
            fore, recv_ref[rows, columns], preferred_element_type=F32
        ).astype(BF)
        for k in range(4):
            made[k].append(got[k * n : (k + 1) * n])
    return made


def front_kernel(cap, group, part, rank_ref, recv_ref, w_ref, sum_ref, send_ref):
    total = recv_ref.shape[0] // 2
    columns = sum_ref.shape[1]
    front = columns // 3 * 2
    rank = rank_ref[0]
    fore = order_matrix(group, cap, False)
    sum_ref[...] = jnp.zeros_like(sum_ref)

    def body(i, carry):
        at = pl.ds(pl.multiple_of(i * TILE, TILE), TILE)
        made = unmix(fore, recv_ref, slice(part * total, (part + 1) * total), at, group, cap)
        for h in range(2):
            x = jnp.concatenate(made[2 * h], axis=0)
            c = jnp.concatenate(made[2 * h + 1], axis=0)
            w = w_ref[rank, h, at, :]
            sum_ref[:, :front] += jnp.dot(x, w[:, :front], preferred_element_type=F32)
            sum_ref[:, front:] += jnp.dot(c, w[:, front:], preferred_element_type=F32)
        return carry

    lax.fori_loop(0, recv_ref.shape[1] // TILE, body, 0)
    send_ref[...] = sum_ref[...].astype(BF)


def sort_kernel(cap, group, recv_ref, x_ref, c_ref):
    n = group * cap
    fore = order_matrix(group, cap, False)

    def body(i, carry):
        at = pl.ds(pl.multiple_of(i * TILE, TILE), TILE)
        made = unmix(fore, recv_ref, slice(0, recv_ref.shape[0]), at, group, cap)
        for g in range(len(made[0])):
            rows = slice(g * n, (g + 1) * n)
            for h in range(2):
                x_ref[h, rows, at] = made[2 * h][g]
                c_ref[h, rows, at] = made[2 * h + 1][g]
        return carry

    lax.fori_loop(0, recv_ref.shape[1] // TILE, body, 0)


GROUP = 8
PIECES = 8


def held():
    return pl.BlockSpec(memory_space=pltpu.VMEM)


def scalars():
    return pl.BlockSpec(memory_space=pltpu.SMEM)


def front_call(rank, recv, weight, cap, part):
    total, half = recv.shape
    columns = weight.shape[-1]
    rows = total // 8
    return pl.pallas_call(
        functools.partial(front_kernel, cap, GROUP, part),
        in_specs=[scalars(), held(), held()],
        out_specs=[held(), held()],
        out_shape=[
            jax.ShapeDtypeStruct((rows, columns), F32),
            jax.ShapeDtypeStruct((rows, columns), BF),
        ],
        compiler_params=pltpu.CompilerParams(vmem_limit_bytes=FRONT_VMEM),
        cost_estimate=pl.CostEstimate(
            flops=2 * 10**9, bytes_accessed=7 * MIB, transcendentals=0
        ),
        name="expert_front",
    )(rank, recv, weight)


def sort_call(recv, cap):
    total, half = recv.shape
    rows = total // 4
    return pl.pallas_call(
        functools.partial(sort_kernel, cap, GROUP),
        in_specs=[held()],
        out_specs=[held(), held()],
        out_shape=[jax.ShapeDtypeStruct((2, rows, half), BF)] * 2,
        compiler_params=pltpu.CompilerParams(vmem_limit_bytes=SORT_VMEM),
        cost_estimate=pl.CostEstimate(
            flops=2 * 10**9, bytes_accessed=19 * MIB, transcendentals=0
        ),
        name="sort_rows",
    )(recv)


def rear_kernel(
    cap, group, piece, rank_ref, x_ref, c_ref, own0, own1, other0, other1, w_ref, first_ref,
    second_ref, out_ref, state_ref, inner, pre
):
    n = group * cap
    span = 4 * n
    sets = out_ref.shape[0] // span
    hidden = inner.shape[1]
    tile = PIECES * piece
    rank = rank_ref[0]
    back = order_matrix(group, cap, True)
    total = jnp.concatenate(
        [own0[...] + other0[...].astype(F32), own1[...] + other1[...].astype(F32)], axis=0
    )
    gate = total[:, :hidden]
    up = total[:, hidden : 2 * hidden]
    grad = total[:, 2 * hidden :]
    sig = jax.nn.sigmoid(gate)
    active = gate * sig
    inner[...] = (active * up).astype(BF)
    slope = sig * (1.0 + gate * (1.0 - sig))
    pre[:, :hidden] = (grad * up * slope).astype(BF)
    pre[:, hidden:] = (grad * active).astype(BF)
    contract = (((1,), (1,)), ((), ()))
    lead = (((0,), (0,)), ((), ()))

    def body(i, carry):
        cols = pl.ds(pl.multiple_of(i * tile, tile), tile)
        made = []
        for h in range(2):
            for factor, at in (
                (inner, slice(2 * hidden, 3 * hidden)),
                (pre, slice(0, 2 * hidden)),
            ):
                made.append(
                    lax.dot_general(
                        factor[...], w_ref[rank, h, cols, at], contract,
                        preferred_element_type=F32,
                    ).astype(BF)
                )
        for g in range(sets):
            stack = jnp.concatenate([m[g * n : (g + 1) * n] for m in made], axis=0)
            out_ref[g * span : (g + 1) * span, cols] = jnp.dot(
                back, stack, preferred_element_type=F32
            ).astype(BF)
        for h in range(2):
            for source, factor, at in (
                (x_ref, pre, slice(0, 2 * hidden)),
                (c_ref, inner, slice(2 * hidden, 3 * hidden)),
            ):
                grad = lax.dot_general(
                    source[h, :, cols], factor[...], lead, preferred_element_type=F32
                )
                m = 0.9 * first_ref[h, cols, at].astype(F32) + 0.1 * grad
                v = 0.95 * second_ref[h, cols, at].astype(F32) + 0.05 * grad * grad
                step = m / (jnp.sqrt(v) + 1e-08) + 0.1 * w_ref[rank, h, cols, at].astype(F32)
                for k, value in enumerate((m, v, step)):
                    value = value.astype(BF)
                    for j in range(PIECES):
                        state_ref[h, i * PIECES + j, k * piece : (k + 1) * piece, at] = value[
                            j * piece : (j + 1) * piece
                        ]
        return carry

    lax.fori_loop(0, out_ref.shape[1] // tile, body, 0)


def rear_call(rank, x, c, own, other, weight, first, second, cap, piece):
    rows, half = x.shape[1:]
    columns = weight.shape[-1]
    hidden = columns // 3
    total = 4 * rows
    return pl.pallas_call(
        functools.partial(rear_kernel, cap, GROUP, piece),
        in_specs=[scalars()] + [held()] * 9,
        out_specs=[held(), held()],
        scratch_shapes=[pltpu.VMEM((rows, hidden), BF), pltpu.VMEM((rows, 2 * hidden), BF)],
        out_shape=[
            jax.ShapeDtypeStruct((total, half), BF),
            jax.ShapeDtypeStruct((2, half // piece, 3 * piece, columns), BF),
        ],
        compiler_params=pltpu.CompilerParams(vmem_limit_bytes=REAR_VMEM),
        cost_estimate=pl.CostEstimate(
            flops=7 * 10**9, bytes_accessed=36 * MIB, transcendentals=rows * hidden
        ),
        name="expert_rear",
    )(
        rank, x, c, *own, *other, weight,
        first.reshape(2, half, columns), second.reshape(2, half, columns),
    )


def column(row):
    n = row.shape[1]
    same = lax.broadcasted_iota(jnp.int32, (n, n), 0) == lax.broadcasted_iota(
        jnp.int32, (n, n), 1
    )
    return jnp.sum(jnp.where(same, row, jnp.zeros_like(row)), axis=1, keepdims=True)


def combine_kernel(
    cap, group, experts, route_ref, prob_ref, back_ref, mixed_ref, grad_ref, stage, pick, both
):
    total, half = back_ref.shape
    tok = mixed_ref.shape[0]
    n = group * cap
    rows = total // 4
    fore = order_matrix(group, cap, False)
    slot0, slot1 = slots_of(route_ref[...], experts, cap)
    prob0, prob1 = column(prob_ref[0:1, :]), column(prob_ref[1:2, :])
    r = lax.broadcasted_iota(jnp.int32, (tok, rows), 1)
    source = r // cap
    expert = source // 2
    ident = expert * cap + r - source * cap
    part = source - 2 * expert
    hit0 = ident == column(slot0)
    hit1 = ident == column(slot1)
    for k in range(2):
        here = part == k
        at = 2 * k * tok
        pick[at : at + tok, :] = jnp.where(hit0 & here, 1.0, 0.0).astype(BF)
        pick[at + tok : at + 2 * tok, :] = jnp.where(hit1 & here, 1.0, 0.0).astype(BF)
        both[k * tok : (k + 1) * tok, :] = jnp.where((hit0 | hit1) & here, 1.0, 0.0).astype(BF)

    def body(i, carry):
        at = pl.ds(pl.multiple_of(i * TILE, TILE), TILE)
        made = unmix(fore, back_ref, slice(0, total), at, group, cap)
        for k in range(4):
            for g in range(len(made[k])):
                stage[k, g * n : (g + 1) * n, :] = made[k][g]
        for h in range(2):
            out = jnp.dot(pick[...], stage[2 * h], preferred_element_type=F32)
            grad = jnp.dot(both[...], stage[2 * h + 1], preferred_element_type=F32)
            for k in range(2):
                to = pl.ds(pl.multiple_of((2 * k + h) * half + i * TILE, TILE), TILE)
                one = out[2 * k * tok : (2 * k + 1) * tok]
                two = out[(2 * k + 1) * tok : (2 * k + 2) * tok]
                mixed_ref[:, to] = (one * prob0 + two * prob1).astype(BF)
                grad_ref[:, to] = grad[k * tok : (k + 1) * tok].astype(BF)
        return carry

    lax.fori_loop(0, half // TILE, body, 0)


def combine(routes, probs, back, experts, cap):
    total, half = back.shape
    tok = routes.shape[1]
    shape = jax.ShapeDtypeStruct((tok, 4 * half), BF)
    return pl.pallas_call(
        functools.partial(combine_kernel, cap, GROUP, experts),
        in_specs=[held()] * 3,
        out_specs=[held(), held()],
        out_shape=[shape, shape],
        scratch_shapes=[
            pltpu.VMEM((4, total // 4, TILE), BF),
            pltpu.VMEM((4 * tok, total // 4), BF),
            pltpu.VMEM((2 * tok, total // 4), BF),
        ],
        compiler_params=pltpu.CompilerParams(vmem_limit_bytes=COMBINE_VMEM),
        cost_estimate=pl.CostEstimate(
            flops=6 * 10**9, bytes_accessed=13 * MIB, transcendentals=0
        ),
        name="combine",
    )(routes, probs, back)


def reorder_kernel(order_ref, source, out):
    def body(j, carry):
        out[j] = source[order_ref[j]]
        return carry

    lax.fori_loop(0, out.shape[0], body, 0)


def reorder(array, inverse, count):
    shape = (count, array.shape[0] // count, array.shape[1])
    whole = pl.BlockSpec(memory_space=pltpu.VMEM)
    return pl.pallas_call(
        reorder_kernel,
        in_specs=[pl.BlockSpec(memory_space=pltpu.SMEM), whole],
        out_specs=whole,
        out_shape=jax.ShapeDtypeStruct(shape, BF),
        compiler_params=pltpu.CompilerParams(vmem_limit_bytes=4 * MIB),
        cost_estimate=pl.CostEstimate(
            flops=0, bytes_accessed=4 * array.size, transcendentals=0
        ),
        name="reorder",
    )(inverse, array.reshape(shape))


def swap(array, axes="expert"):
    return lax.all_to_all(array, axes, split_axis=0, concat_axis=0, tiled=True)


def split_kernel(source, *refs):
    outs, sem = refs[:3], refs[3]
    piece = outs[0].shape[1]
    copies = [
        pltpu.make_async_copy(source.at[:, pl.ds(k * piece, piece), :], out, sem.at[k])
        for k, out in enumerate(outs)
    ]
    for copy in copies:
        copy.start()
    for copy in copies:
        copy.wait()


def split(moved):
    count, rows, columns = moved.shape
    return pl.pallas_call(
        split_kernel,
        in_specs=[held()],
        out_specs=[pl.BlockSpec(memory_space=pl.ANY)] * 3,
        out_shape=[jax.ShapeDtypeStruct((count, rows // 3, columns), BF)] * 3,
        scratch_shapes=[pltpu.SemaphoreType.DMA((3,))],
        compiler_params=pltpu.CompilerParams(vmem_limit_bytes=4 * MIB),
        cost_estimate=pl.CostEstimate(flops=0, bytes_accessed=4 * moved.size, transcendentals=0),
        name="split",
    )(moved)


def local(tokens, cotangent, gate_probs, routes, placement, weights, first_moment, second_moment):
    experts = lax.axis_size("expert")
    tok, width = tokens.shape
    top = routes.shape[1]
    cap = max(2, (3 * tok * top + 2 * experts - 1) // (2 * experts))
    rank = lax.axis_index("dp")
    weight = weights[0]
    rows = weight.shape[0] // 2
    piece = rows // experts
    columns = weight.shape[1]
    both = ("expert", "dp")
    together = lax.optimization_barrier

    place = rank.reshape(1).astype(jnp.int32)
    labels = jnp.arange(experts, dtype=jnp.int32)
    inverse = jnp.sum(
        labels[None, :] * (placement[None, :] == labels[:, None]).astype(jnp.int32), axis=1
    )
    inverse = jnp.minimum(inverse, experts - 1)
    send = dispatch(routes.T, gate_probs.T, tokens, cotangent, experts, cap)
    send, inverse, place = together((send, inverse, place))
    recv = swap(send.reshape(-1, width // 4), both)
    weight = weight.reshape(2, 2, rows // 2, columns)
    recv, inverse, place = together((recv, inverse, place))
    own0, out0 = front_call(place, recv, weight, cap, 0)
    own1, out1 = front_call(place, recv, weight, cap, 1)
    other = [lax.ppermute(out, "dp", [(0, 1), (1, 0)]) for out in (out0, out1)]
    recv, own1 = together((recv, own1))
    x, c = sort_call(recv, cap)
    result, state = rear_call(
        place, x, c, [own0, own1], other, weight, first_moment[0], second_moment[0], cap, piece
    )
    result, state, inverse = together((result, state, inverse))
    spread = swap(state.reshape(3 * rows, columns))
    spread, result, inverse = together((spread, result, inverse))
    ready = reorder(spread, inverse, experts).reshape(3 * rows, columns)
    ready, result = together((ready, result))
    back = swap(result, both)
    mixed, token_grad = combine(routes.T, gate_probs.T, back, experts, cap)
    ready, mixed, token_grad = together((ready, mixed, token_grad))
    moved = swap(ready).reshape(experts, 3 * piece, columns)
    m, v, step = (array.reshape(1, rows, columns) for array in split(moved))
    return (mixed, token_grad, m, v, step)


def solution(mesh):
    in_specs = (
        P(("expert", "dp"), None),
        P(("expert", "dp"), None),
        P(("expert", "dp"), None),
        P(("expert", "dp"), None),
        P(),
        P("expert", None, None),
        P("expert", "dp", None),
        P("expert", "dp", None),
    )
    out_specs = (
        P(("expert", "dp"), None),
        P(("expert", "dp"), None),
        P("expert", "dp", None),
        P("expert", "dp", None),
        P("expert", "dp", None),
    )
    return jax.shard_map(local, mesh=mesh, in_specs=in_specs, out_specs=out_specs, check_vma=False)
```

time: 920 us -> 485 us (0.53); the launches traced: 908 us -> 484 us
  blocking collectives: 66.9 us -> 421 us
  other arithmetic: 272 us -> 0.77 us
  local copies, waits for them, and re-layouts: 245 us -> 2.05 us
  waiting for transfers between devices: 206 us -> 9.63 us
  starting transfers between devices: 81.1 us -> 3.61 us
  Pallas kernels: 0 us -> 45.9 us
  matrix products: 22.9 us -> 0 us
  between operations: 14.7 us -> 0.89 us
    all_to_all x1 -> x4, blocking collectives: 66.9 us -> 421 us  [swap(): return lax.all_to_all(array, axes, split_axis=0, concat_axis=0, tiled=True)]
    all_to_all x9 -> x0, waiting for transfers between devices: 206 us -> none  [the longest x1 71.5 us: local(): lax.all_to_all(row_grad, 'expert', split_axis=0, concat_axis=0, tiled=True)]
    unnamed x4 -> x1, other arithmetic: 204 us -> 0.01 us
    unnamed x49 -> x16, local copies, waits for them, and re-layouts: 107 us -> 2.05 us
    all_to_all x9 -> x0, starting transfers between devices: 80.9 us -> none  [the longest x1 10.6 us: relocate(): lax.all_to_all(array_two, 'expert', split_axis=1, concat_axis=0, tiled=True)]
    all_to_all x8 -> x0, local copies, waits for them, and re-layouts: 62.8 us -> none  [the longest x2 16.1 us: local(): lax.all_to_all(expert_out, 'expert', split_axis=0, concat_axis=0, tiled=T...]
    pallas_call x0 -> x8, Pallas kernels: none -> 45.9 us  [the longest x1 12.1 us: rear_call(): pl.pallas_call(functools.partial(rear_kernel, cap, GROUP, piece), in_spec...]
    gather x8 -> x0, local copies, waits for them, and re-layouts: 42.9 us -> none  [the longest x1 8.43 us: local(): picked_grad = jnp.take(back_grad, slot_of, axis=0).astype(jnp.float32)]
  transfers between devices with their start and end apart: 10 -> 2, of which waited for: 5 -> 2; matrix products, arithmetic and copies ran while one was open for 44% -> 0% of each run, Pallas kernels for 0% -> 1%
where the time goes in v4:
time: 485 us; the launch traced here: 484 us
  blocking collectives  421 us (87%)
  Pallas kernels  45.9 us (9%)
  waiting for transfers between devices  9.63 us (2%)
    all_to_all x4, blocking collectives, swap(): return lax.all_to_all(array, axes, split_axis=0, concat_axis=0, tiled=True)  421 us
    pallas_call x1, Pallas kernels, rear_call(): pl.pallas_call(functools.partial(rear_kernel, cap, GROUP, piece), in_spec...  12.1 us
    pallas_call x1, Pallas kernels, dispatch(): pl.pallas_call(functools.partial(dispatch_kernel, cap, experts), in_specs...  11.2 us
  transfers between devices with their start and end apart: 2, of which 2 were waited for; matrix products, arithmetic and copies ran while one was open for 0% of the time, Pallas kernels for 1%

profile of v4, /device:TPU:6, one launch (start us, length us, event | category | flops | bytes accessed | tf_op | source)
XLA Modules:
  0.0 484.3 jit_solution(15311577790387400043)
XLA Ops:
  0.6 0.8 select_reduce_fusion
  1.4 0.0 slice-start
  1.4 11.2 %dispatch.1 = bf16[64,2,24,1536]{3,2,1,0:T(8,128)(2,1)} custom-call(s32[2,128]{1,0:T(2,128)} %bitcast.29, f32[2,128]{1,0:T(2,128)} %bitcast.31, bf16[128,6144]{1,0:T(8,128)(2,1)} %token_ref.1, bf16[128,6144]{1,0:T(8,128)(2,1)} %cot_ref.1), custom_call_target="tpu_custom_call" | custom-call | flops 3000000000 | bytes 13631488 | tf_op jit(solution)/shard_map/dispatch/pallas_call | solution.py:120
  12.7 0.0 slice-start.1
  12.7 120.4 %all_to_all.44 = bf16[128,24,1536]{2,1,0:T(8,128)(2,1)S(1)} all-to-all(bf16[128,24,1536]{2,1,0:T(8,128)(2,1)} %bitcast.35), channel_id=1, replica_groups=mesh['expert'=64,'dp'=2] {'expert','dp'}, dimensions={0} | all-to-all | bytes 18874368 | tf_op jit(solution)/shard_map/all_to_all | solution.py:448
  133.1 0.0 slice-done
  133.1 0.0 slice-done.1
  133.1 3.1 expert_front.3
  136.3 3.1 expert_front.2
  139.4 0.9 collective-permute-start
  140.2 2.8 collective-permute-start.1
  143.0 0.0 copy-start.4
  143.0 0.0 copy-start.5
  143.0 3.1 sort_rows.1
  146.1 4.9 %collective-permute-done.other0 = bf16[384,384]{1,0:T(8,128)(2,1)S(1)} collective-permute-done((bf16[384,384]{1,0:T(8,128)(2,1)S(1)}, bf16[384,384]{1,0:T(8,128)(2,1)S(1)}, u32[]{:S(2)}, u32[]{:S(2)}) %collective-permute-start) | collective-permute-done | bytes 294944 | tf_op jit(solution)/shard_map/ppermute | solution.py:504
  150.9 4.8 collective-permute-done.1.other1
  155.7 0.0 copy-done.4
  155.7 0.0 copy-done.5
  155.7 12.1 %expert_rear.1 = (bf16[3072,1536]{1,0:T(8,128)(2,1)S(1)}, bf16[2,32,144,384]{3,2,1,0:T(8,128)(2,1)S(1)}) custom-call(s32[1]{0:T(128)} %bitcast.2.rank_ref, bf16[2,768,1536]{2,1,0:T(8,128)(2,1)S(1)} %get-tuple-element.44.x_ref, bf16[2,768,1536]{2,1,0:T(8,128)(2,1)S(1)} %get-tuple-element.45.c_ref, f32[384,384]{1,0:T(8,128)S(1)} %get-tuple-element.46.own0, ...), custom_call_target="tpu_custom_call" | custom-call | flops 7000000000 | bytes 37748736 | tf_op jit(solution)/shard_map/expert_rear/pallas_call | solution.py:329
  167.9 0.0 copy-start
  167.9 92.2 %all_to_all.45 = bf16[64,144,384]{2,1,0:T(8,128)(2,1)S(1)} all-to-all(bf16[64,144,384]{2,1,0:T(8,128)(2,1)S(1)} %bitcast.28), channel_id=1, replica_groups=mesh['expert'=64,'dp'=2] {'expert'}, dimensions={0} | all-to-all | bytes 14155776 | tf_op jit(solution)/shard_map/all_to_all | solution.py:448
  260.1 0.0 copy-done
  260.1 0.0 copy-start.1
  260.1 1.7 reorder.1
  261.8 2.0 copy-done.1
  263.8 0.0 copy-start.2
  263.8 116.5 %all_to_all.46 = bf16[128,24,1536]{2,1,0:T(8,128)(2,1)S(1)} all-to-all(bf16[128,24,1536]{2,1,0:T(8,128)(2,1)S(1)} %bitcast.26), channel_id=1, replica_groups=mesh['expert'=64,'dp'=2] {'expert','dp'}, dimensions={0} | all-to-all | bytes 18874368 | tf_op jit(solution)/shard_map/all_to_all | solution.py:448
  380.3 0.0 copy-done.2
  380.3 0.0 copy-done.3
  380.3 8.6 %combine.1 = (bf16[128,6144]{1,0:T(8,128)(2,1)}, bf16[128,6144]{1,0:T(8,128)(2,1)}) custom-call(s32[2,128]{1,0:T(2,128)S(1)} %bitcast.30, f32[2,128]{1,0:T(2,128)S(1)} %bitcast.32, bf16[3072,1536]{1,0:T(8,128)(2,1)S(1)} %bitcast.27), custom_call_target="tpu_custom_call" | custom-call | flops 6000000000 | bytes 13631488 | tf_op jit(solution)/shard_map/combine/pallas_call | solution.py:405
  388.9 92.2 %all_to_all.47.source = bf16[64,144,384]{2,1,0:T(8,128)(2,1)S(1)} all-to-all(bf16[64,144,384]{2,1,0:T(8,128)(2,1)S(1)} %reorder.1), channel_id=1, replica_groups=mesh['expert'=64,'dp'=2] {'expert'}, dimensions={0} | all-to-all | bytes 14155776 | tf_op jit(solution)/shard_map/all_to_all | solution.py:448
  481.1 3.0 split.1
  (3 shorter events, 0.0 us)
Async XLA Ops:
  1.4 131.7 %slice-start = ((s8[4718592]{0:T(1024)(128)(4,1)}), s8[524288]{0:T(1024)(128)(4,1)S(1)}, s32[]{:S(2)}) async-start(s8[4718592]{0:T(1024)(128)(4,1)} %bitcast.21), calls=%async_computation.4 | async-start | bytes 1048576
  12.7 120.4 %slice-start.1 = ((s8[4718592]{0:T(1024)(128)(4,1)}), s8[4194304]{0:T(1024)(128)(4,1)S(1)}, s32[]{:S(2)}) async-start(s8[4718592]{0:T(1024)(128)(4,1)} %bitcast.21), calls=%async_computation.5 | async-start | bytes 8388608
  139.4 11.5 %collective-permute-start = (bf16[384,384]{1,0:T(8,128)(2,1)S(1)}, bf16[384,384]{1,0:T(8,128)(2,1)S(1)}, u32[]{:S(2)}, u32[]{:S(2)}) collective-permute-start(bf16[384,384]{1,0:T(8,128)(2,1)S(1)} %get-tuple-element.48), channel_id=1, source_target_pairs={{0,1},{1,0},{2,3},{3,2},{4,5},{5,4},{6,7},{7,6},{8,9},{9,8},{10,11... | collective-permute-start | bytes 884744 | tf_op jit(solution)/shard_map/ppermute | solution.py:504
  140.2 15.5 %collective-permute-start.1 = (bf16[384,384]{1,0:T(8,128)(2,1)S(1)}, bf16[384,384]{1,0:T(8,128)(2,1)S(1)}, u32[]{:S(2)}, u32[]{:S(2)}) collective-permute-start(bf16[384,384]{1,0:T(8,128)(2,1)S(1)} %get-tuple-element.49), channel_id=1, source_target_pairs={{0,1},{1,0},{2,3},{3,2},{4,5},{5,4},{6,7},{7,6},{8,9},{9,8},{10,11... | collective-permute-start | bytes 884744 | tf_op jit(solution)/shard_map/ppermute | solution.py:504
  143.0 12.7 %copy-start.4 = (bf16[1,3072,384]{2,1,0:T(8,128)(2,1)S(1)}, bf16[1,3072,384]{2,1,0:T(8,128)(2,1)}, u32[]{:S(2)}) copy-start(bf16[1,3072,384]{2,1,0:T(8,128)(2,1)} %param.14) | copy-start | bytes 7077892
  143.0 12.7 %copy-start.5 = (bf16[1,3072,384]{2,1,0:T(8,128)(2,1)S(1)}, bf16[1,3072,384]{2,1,0:T(8,128)(2,1)}, u32[]{:S(2)}) copy-start(bf16[1,3072,384]{2,1,0:T(8,128)(2,1)} %param.15) | copy-start | bytes 7077892
  167.9 92.3 %copy-start = (bf16[3072,1536]{1,0:T(8,128)(2,1)}, bf16[3072,1536]{1,0:T(8,128)(2,1)S(1)}, u32[]{:S(2)}) copy-start(bf16[3072,1536]{1,0:T(8,128)(2,1)S(1)} %get-tuple-element.60) | copy-start | bytes 28311556
  260.1 3.7 copy-start.1
  263.8 116.5 %copy-start.2 = (s32[128,2]{0,1:T(2,128)S(1)}, s32[128,2]{0,1:T(2,128)}, u32[]{:S(2)}) copy-start(s32[128,2]{0,1:T(2,128)} %param.11) | copy-start | bytes 3076
  263.8 116.5 %copy-start.3 = (f32[128,2]{0,1:T(2,128)S(1)}, f32[128,2]{0,1:T(2,128)}, u32[]{:S(2)}) copy-start(f32[128,2]{0,1:T(2,128)} %param.10) | copy-start | bytes 3076

commit v5 on v4

--- a/solution.py
+++ b/solution.py
@@ -10,7 +10,7 @@
 F32 = jnp.float32
 MIB = 1024 * 1024
 DISPATCH_VMEM, FRONT_VMEM, SORT_VMEM = 60 * MIB, 12 * MIB, 12 * MIB
-REAR_VMEM, COMBINE_VMEM = 16 * MIB, 24 * MIB
+REAR_VMEM, COMBINE_VMEM = 12 * MIB, 16 * MIB
 TILE = 512
 
 
@@ -207,7 +207,6 @@
 
 
 GROUP = 8
-PIECES = 8
 
 
 def held():
@@ -256,13 +255,13 @@
 
 def rear_kernel(
     cap, group, piece, rank_ref, x_ref, c_ref, own0, own1, other0, other1, w_ref, first_ref,
-    second_ref, out_ref, state_ref, inner, pre
+    second_ref, out_ref, inner, pre
 ):
     n = group * cap
-    span = 4 * n
-    sets = out_ref.shape[0] // span
+    per = 4 * cap
+    sets = out_ref.shape[0] // group
+    tiles, tile = out_ref.shape[1] - 3, out_ref.shape[3]
     hidden = inner.shape[1]
-    tile = PIECES * piece
     rank = rank_ref[0]
     back = order_matrix(group, cap, True)
     total = jnp.concatenate(
@@ -296,9 +295,9 @@
                 )
         for g in range(sets):
             stack = jnp.concatenate([m[g * n : (g + 1) * n] for m in made], axis=0)
-            out_ref[g * span : (g + 1) * span, cols] = jnp.dot(
-                back, stack, preferred_element_type=F32
-            ).astype(BF)
+            mixed = jnp.dot(back, stack, preferred_element_type=F32)
+            for j in range(group):
+                out_ref[g * group + j, i] = mixed[j * per : (j + 1) * per].astype(BF)
         for h in range(2):
             for source, factor, at in (
                 (x_ref, pre, slice(0, 2 * hidden)),
@@ -310,31 +309,29 @@
                 m = 0.9 * first_ref[h, cols, at].astype(F32) + 0.1 * grad
                 v = 0.95 * second_ref[h, cols, at].astype(F32) + 0.05 * grad * grad
                 step = m / (jnp.sqrt(v) + 1e-08) + 0.1 * w_ref[rank, h, cols, at].astype(F32)
+                count = tile // piece
                 for k, value in enumerate((m, v, step)):
-                    value = value.astype(BF)
-                    for j in range(PIECES):
-                        state_ref[h, i * PIECES + j, k * piece : (k + 1) * piece, at] = value[
+                    for j in range(count):
+                        out_ref[(h * tiles + i) * count + j, tiles + k, :, at] = value[
                             j * piece : (j + 1) * piece
-                        ]
+                        ].astype(BF)
         return carry
 
-    lax.fori_loop(0, out_ref.shape[1] // tile, body, 0)
+    lax.fori_loop(0, tiles, body, 0)
 
 
 def rear_call(rank, x, c, own, other, weight, first, second, cap, piece):
     rows, half = x.shape[1:]
     columns = weight.shape[-1]
     hidden = columns // 3
-    total = 4 * rows
+    tile = 3 * hidden
+    tiles = half // tile
     return pl.pallas_call(
         functools.partial(rear_kernel, cap, GROUP, piece),
         in_specs=[scalars()] + [held()] * 9,
-        out_specs=[held(), held()],
+        out_specs=held(),
         scratch_shapes=[pltpu.VMEM((rows, hidden), BF), pltpu.VMEM((rows, 2 * hidden), BF)],
-        out_shape=[
-            jax.ShapeDtypeStruct((total, half), BF),
-            jax.ShapeDtypeStruct((2, half // piece, 3 * piece, columns), BF),
-        ],
+        out_shape=jax.ShapeDtypeStruct((rows // cap, tiles + 3, piece, tile), BF),
         compiler_params=pltpu.CompilerParams(vmem_limit_bytes=REAR_VMEM),
         cost_estimate=pl.CostEstimate(
             flops=7 * 10**9, bytes_accessed=36 * MIB, transcendentals=rows * hidden
@@ -357,10 +354,11 @@
 def combine_kernel(
     cap, group, experts, route_ref, prob_ref, back_ref, mixed_ref, grad_ref, stage, pick, both
 ):
-    total, half = back_ref.shape
-    tok = mixed_ref.shape[0]
+    sources, _, per, tile = back_ref.shape
+    tok, width = mixed_ref.shape
+    half = width // 4
     n = group * cap
-    rows = total // 4
+    rows = sources * cap
     fore = order_matrix(group, cap, False)
     slot0, slot1 = slots_of(route_ref[...], experts, cap)
     prob0, prob1 = column(prob_ref[0:1, :]), column(prob_ref[1:2, :])
@@ -379,38 +377,39 @@
         both[k * tok : (k + 1) * tok, :] = jnp.where((hit0 | hit1) & here, 1.0, 0.0).astype(BF)
 
     def body(i, carry):
-        at = pl.ds(pl.multiple_of(i * TILE, TILE), TILE)
-        made = unmix(fore, back_ref, slice(0, total), at, group, cap)
-        for k in range(4):
-            for g in range(len(made[k])):
-                stage[k, g * n : (g + 1) * n, :] = made[k][g]
+        for g in range(sources // group):
+            block = back_ref[g * group : (g + 1) * group, i].reshape(group * per, tile)
+            got = jnp.dot(fore, block, preferred_element_type=F32).astype(BF)
+            for k in range(4):
+                stage[k, g * n : (g + 1) * n, :] = got[k * n : (k + 1) * n]
         for h in range(2):
             out = jnp.dot(pick[...], stage[2 * h], preferred_element_type=F32)
             grad = jnp.dot(both[...], stage[2 * h + 1], preferred_element_type=F32)
             for k in range(2):
-                to = pl.ds(pl.multiple_of((2 * k + h) * half + i * TILE, TILE), TILE)
+                to = pl.ds(pl.multiple_of((2 * k + h) * half + i * tile, tile), tile)
                 one = out[2 * k * tok : (2 * k + 1) * tok]
                 two = out[(2 * k + 1) * tok : (2 * k + 2) * tok]
                 mixed_ref[:, to] = (one * prob0 + two * prob1).astype(BF)
                 grad_ref[:, to] = grad[k * tok : (k + 1) * tok].astype(BF)
         return carry
 
-    lax.fori_loop(0, half // TILE, body, 0)
+    lax.fori_loop(0, half // tile, body, 0)
 
 
 def combine(routes, probs, back, experts, cap):
-    total, half = back.shape
+    sources, slabs, _, tile = back.shape
+    rows = sources * cap
     tok = routes.shape[1]
-    shape = jax.ShapeDtypeStruct((tok, 4 * half), BF)
+    shape = jax.ShapeDtypeStruct((tok, 4 * (slabs - 3) * tile), BF)
     return pl.pallas_call(
         functools.partial(combine_kernel, cap, GROUP, experts),
         in_specs=[held()] * 3,
         out_specs=[held(), held()],
         out_shape=[shape, shape],
         scratch_shapes=[
-            pltpu.VMEM((4, total // 4, TILE), BF),
-            pltpu.VMEM((4 * tok, total // 4), BF),
-            pltpu.VMEM((2 * tok, total // 4), BF),
+            pltpu.VMEM((4, rows, tile), BF),
+            pltpu.VMEM((4 * tok, rows), BF),
+            pltpu.VMEM((2 * tok, rows), BF),
         ],
         compiler_params=pltpu.CompilerParams(vmem_limit_bytes=COMBINE_VMEM),
         cost_estimate=pl.CostEstimate(
@@ -422,37 +421,36 @@
 
 def reorder_kernel(order_ref, source, out):
     def body(j, carry):
-        out[j] = source[order_ref[j]]
+        for r in range(2):
+            out[2 * j + r] = source[2 * order_ref[j] + r, -3:]
         return carry
 
-    lax.fori_loop(0, out.shape[0], body, 0)
-
-
-def reorder(array, inverse, count):
-    shape = (count, array.shape[0] // count, array.shape[1])
-    whole = pl.BlockSpec(memory_space=pltpu.VMEM)
+    lax.fori_loop(0, out.shape[0] // 2, body, 0)
+
+
+def reorder(array, inverse):
+    sources, _, piece, columns = array.shape
     return pl.pallas_call(
         reorder_kernel,
-        in_specs=[pl.BlockSpec(memory_space=pltpu.SMEM), whole],
-        out_specs=whole,
-        out_shape=jax.ShapeDtypeStruct(shape, BF),
+        in_specs=[scalars(), held()],
+        out_specs=held(),
+        out_shape=jax.ShapeDtypeStruct((sources, 3, piece, columns), BF),
         compiler_params=pltpu.CompilerParams(vmem_limit_bytes=4 * MIB),
         cost_estimate=pl.CostEstimate(
-            flops=0, bytes_accessed=4 * array.size, transcendentals=0
+            flops=0, bytes_accessed=12 * sources * piece * columns, transcendentals=0
         ),
         name="reorder",
-    )(inverse, array.reshape(shape))
-
-
-def swap(array, axes="expert"):
+    )(inverse, array)
+
+
+def swap(array, axes):
     return lax.all_to_all(array, axes, split_axis=0, concat_axis=0, tiled=True)
 
 
 def split_kernel(source, *refs):
     outs, sem = refs[:3], refs[3]
-    piece = outs[0].shape[1]
     copies = [
-        pltpu.make_async_copy(source.at[:, pl.ds(k * piece, piece), :], out, sem.at[k])
+        pltpu.make_async_copy(source.at[:, k], out, sem.at[k])
         for k, out in enumerate(outs)
     ]
     for copy in copies:
@@ -462,12 +460,12 @@
 
 
 def split(moved):
-    count, rows, columns = moved.shape
+    count, _, piece, columns = moved.shape
     return pl.pallas_call(
         split_kernel,
         in_specs=[held()],
         out_specs=[pl.BlockSpec(memory_space=pl.ANY)] * 3,
-        out_shape=[jax.ShapeDtypeStruct((count, rows // 3, columns), BF)] * 3,
+        out_shape=[jax.ShapeDtypeStruct((count, piece, columns), BF)] * 3,
         scratch_shapes=[pltpu.SemaphoreType.DMA((3,))],
         compiler_params=pltpu.CompilerParams(vmem_limit_bytes=4 * MIB),
         cost_estimate=pl.CostEstimate(flops=0, bytes_accessed=4 * moved.size, transcendentals=0),
@@ -483,7 +481,7 @@
     rank = lax.axis_index("dp")
     weight = weights[0]
     rows = weight.shape[0] // 2
-    piece = rows // experts
+    piece = rows // (2 * experts)
     columns = weight.shape[1]
     both = ("expert", "dp")
     together = lax.optimization_barrier
@@ -504,18 +502,15 @@
     other = [lax.ppermute(out, "dp", [(0, 1), (1, 0)]) for out in (out0, out1)]
     recv, own1 = together((recv, own1))
     x, c = sort_call(recv, cap)
-    result, state = rear_call(
+    sent = rear_call(
         place, x, c, [own0, own1], other, weight, first_moment[0], second_moment[0], cap, piece
     )
-    result, state, inverse = together((result, state, inverse))
-    spread = swap(state.reshape(3 * rows, columns))
-    spread, result, inverse = together((spread, result, inverse))
-    ready = reorder(spread, inverse, experts).reshape(3 * rows, columns)
-    ready, result = together((ready, result))
-    back = swap(result, both)
+    sent, inverse = together((sent, inverse))
+    back = swap(sent.reshape(-1, columns), both).reshape(sent.shape)
+    ready = reorder(back, inverse)
     mixed, token_grad = combine(routes.T, gate_probs.T, back, experts, cap)
     ready, mixed, token_grad = together((ready, mixed, token_grad))
-    moved = swap(ready).reshape(experts, 3 * piece, columns)
+    moved = swap(ready.reshape(-1, columns), both).reshape(ready.shape)
     m, v, step = (array.reshape(1, rows, columns) for array in split(moved))
     return (mixed, token_grad, m, v, step)
 

time: 485 us -> 471 us (0.971)
  blocking collectives: 421 us -> 407 us
    all_to_all x4 -> x3, blocking collectives: 421 us -> 407 us  [swap(): return lax.all_to_all(array, axes, split_axis=0, concat_axis=0, tiled=True)]
where the time goes in v5:
time: 471 us; the launch traced here: 470 us
  blocking collectives  407 us (86%)
  Pallas kernels  48.1 us (10%)
  waiting for transfers between devices  9.63 us (2%)
    all_to_all x3, blocking collectives, swap(): return lax.all_to_all(array, axes, split_axis=0, concat_axis=0, tiled=True)  407 us
    pallas_call x1, Pallas kernels, rear_call(): pl.pallas_call(functools.partial(rear_kernel, cap, GROUP, piece), in_spec...  12.1 us
    pallas_call x1, Pallas kernels, dispatch(): pl.pallas_call(functools.partial(dispatch_kernel, cap, experts), in_specs...  11.2 us
    pallas_call x1, Pallas kernels, combine(): pl.pallas_call(functools.partial(combine_kernel, cap, GROUP, experts), in...  10.8 us
    ppermute x2, waiting for transfers between devices, local(): other = [lax.ppermute(out, 'dp', [(0, 1), (1, 0)]) for out in (out0, out1)]  9.63 us
  transfers between devices with their start and end apart: 2, of which 2 were waited for; matrix products, arithmetic and copies ran while one was open for 0% of the time, Pallas kernels for 1%

profile of v5, /device:TPU:6, one launch (start us, length us, event | category | flops | bytes accessed | tf_op | source)
XLA Modules:
  0.0 469.6 jit_solution(8542705243407770261)
XLA Ops:
  0.6 0.8 select_reduce_fusion
  1.4 0.0 slice-start
  1.4 11.2 %dispatch.1 = bf16[64,2,24,1536]{3,2,1,0:T(8,128)(2,1)} custom-call(s32[2,128]{1,0:T(2,128)} %bitcast.30, f32[2,128]{1,0:T(2,128)} %bitcast.32, bf16[128,6144]{1,0:T(8,128)(2,1)} %token_ref.1, bf16[128,6144]{1,0:T(8,128)(2,1)} %cot_ref.1), custom_call_target="tpu_custom_call" | custom-call | flops 3000000000 | bytes 13631488 | tf_op jit(solution)/shard_map/dispatch/pallas_call | solution.py:120
  12.7 0.0 slice-start.1
  12.7 120.4 %all_to_all.30 = bf16[128,24,1536]{2,1,0:T(8,128)(2,1)S(1)} all-to-all(bf16[128,24,1536]{2,1,0:T(8,128)(2,1)} %bitcast.34), channel_id=1, replica_groups=mesh['expert'=64,'dp'=2] {'expert','dp'}, dimensions={0} | all-to-all | bytes 18874368 | tf_op jit(solution)/shard_map/all_to_all | solution.py:447
  133.1 0.0 slice-done
  133.1 0.0 slice-done.1
  133.1 3.1 expert_front.3
  136.3 3.1 expert_front.2
  139.4 0.9 collective-permute-start
  140.2 2.8 collective-permute-start.1
  143.0 0.0 copy-start
  143.0 0.0 copy-start.1
  143.0 3.1 sort_rows.1
  146.1 4.9 %collective-permute-done.other0 = bf16[384,384]{1,0:T(8,128)(2,1)S(1)} collective-permute-done((bf16[384,384]{1,0:T(8,128)(2,1)S(1)}, bf16[384,384]{1,0:T(8,128)(2,1)S(1)}, u32[]{:S(2)}, u32[]{:S(2)}) %collective-permute-start) | collective-permute-done | bytes 294944 | tf_op jit(solution)/shard_map/ppermute | solution.py:502
  150.9 4.8 %collective-permute-done.1.other1 = bf16[384,384]{1,0:T(8,128)(2,1)S(1)} collective-permute-done((bf16[384,384]{1,0:T(8,128)(2,1)S(1)}, bf16[384,384]{1,0:T(8,128)(2,1)S(1)}, u32[]{:S(2)}, u32[]{:S(2)}) %collective-permute-start.1) | collective-permute-done | bytes 294944 | tf_op jit(solution)/shard_map/ppermute | solution.py:502
  155.7 0.0 copy-done
  155.7 0.0 copy-done.1
  155.7 12.1 %expert_rear.1 = bf16[128,7,24,384]{3,2,1,0:T(8,128)(2,1)S(1)} custom-call(s32[1]{0:T(128)} %bitcast.2.rank_ref, bf16[2,768,1536]{2,1,0:T(8,128)(2,1)S(1)} %get-tuple-element.36.x_ref, bf16[2,768,1536]{2,1,0:T(8,128)(2,1)S(1)} %get-tuple-element.37.c_ref, f32[384,384]{1,0:T(8,128)S(1)} %get-tuple-element.38.own0, f32[384,384]{1,0:T(8,128)S(1)} %get-tuple-element.39.own1, ...), custom_call_target="tpu_custom_call" | custom-call | flops 7000000000 | bytes 37748736 | tf_op jit(solution)/shard_map/expert_rear/pallas_call | solution.py:329
  167.8 0.0 copy-start.2
  167.9 0.0 copy-start.3
  167.9 195.5 %all_to_all.31 = bf16[128,168,384]{2,1,0:T(8,128)(2,1)S(1)} all-to-all(bf16[128,168,384]{2,1,0:T(8,128)(2,1)S(1)} %bitcast.18), channel_id=1, replica_groups=mesh['expert'=64,'dp'=2] {'expert','dp'}, dimensions={0} | all-to-all | bytes 33030144 | tf_op jit(solution)/shard_map/all_to_all | solution.py:447
  363.3 0.0 copy-done.2
  363.3 0.0 copy-done.3
  363.3 10.8 %combine.1 = (bf16[128,6144]{1,0:T(8,128)(2,1)}, bf16[128,6144]{1,0:T(8,128)(2,1)}) custom-call(s32[2,128]{1,0:T(2,128)S(1)} %bitcast.31, f32[2,128]{1,0:T(2,128)S(1)} %bitcast.33, bf16[128,7,24,384]{3,2,1,0:T(8,128)(2,1)S(1)} %bitcast.19), custom_call_target="tpu_custom_call" | custom-call | flops 6000000000 | bytes 13631488 | tf_op jit(solution)/shard_map/combine/pallas_call | solution.py:404
  374.1 1.7 reorder.1
  375.8 90.7 %all_to_all.32 = bf16[128,72,384]{2,1,0:T(8,128)(2,1)S(1)} all-to-all(bf16[128,72,384]{2,1,0:T(8,128)(2,1)S(1)} %bitcast.27), channel_id=1, replica_groups=mesh['expert'=64,'dp'=2] {'expert','dp'}, dimensions={0} | all-to-all | bytes 14155776 | tf_op jit(solution)/shard_map/all_to_all | solution.py:447
  466.5 3.0 split.1
  (2 shorter events, 0.0 us)
Async XLA Ops:
  1.4 131.7 %slice-start = ((s8[4718592]{0:T(1024)(128)(4,1)}), s8[524288]{0:T(1024)(128)(4,1)S(1)}, s32[]{:S(2)}) async-start(s8[4718592]{0:T(1024)(128)(4,1)} %bitcast.21), calls=%async_computation.3 | async-start | bytes 1048576
  12.7 120.4 %slice-start.1 = ((s8[4718592]{0:T(1024)(128)(4,1)}), s8[4194304]{0:T(1024)(128)(4,1)S(1)}, s32[]{:S(2)}) async-start(s8[4718592]{0:T(1024)(128)(4,1)} %bitcast.21), calls=%async_computation.4 | async-start | bytes 8388608
  139.4 11.5 %collective-permute-start = (bf16[384,384]{1,0:T(8,128)(2,1)S(1)}, bf16[384,384]{1,0:T(8,128)(2,1)S(1)}, u32[]{:S(2)}, u32[]{:S(2)}) collective-permute-start(bf16[384,384]{1,0:T(8,128)(2,1)S(1)} %get-tuple-element.40), channel_id=1, source_target_pairs={{0,1},{1,0},{2,3},{3,2},{4,5},{5,4},{6,7},{7,6},{8,9},{9,8},{10,11... | collective-permute-start | bytes 884744 | tf_op jit(solution)/shard_map/ppermute | solution.py:502
  140.2 15.5 %collective-permute-start.1 = (bf16[384,384]{1,0:T(8,128)(2,1)S(1)}, bf16[384,384]{1,0:T(8,128)(2,1)S(1)}, u32[]{:S(2)}, u32[]{:S(2)}) collective-permute-start(bf16[384,384]{1,0:T(8,128)(2,1)S(1)} %get-tuple-element.41), channel_id=1, source_target_pairs={{0,1},{1,0},{2,3},{3,2},{4,5},{5,4},{6,7},{7,6},{8,9},{9,8},{10,11... | collective-permute-start | bytes 884744 | tf_op jit(solution)/shard_map/ppermute | solution.py:502
  143.0 12.7 %copy-start = (bf16[1,3072,384]{2,1,0:T(8,128)(2,1)S(1)}, bf16[1,3072,384]{2,1,0:T(8,128)(2,1)}, u32[]{:S(2)}) copy-start(bf16[1,3072,384]{2,1,0:T(8,128)(2,1)} %param.14) | copy-start | bytes 7077892
  143.0 12.7 %copy-start.1 = (bf16[1,3072,384]{2,1,0:T(8,128)(2,1)S(1)}, bf16[1,3072,384]{2,1,0:T(8,128)(2,1)}, u32[]{:S(2)}) copy-start(bf16[1,3072,384]{2,1,0:T(8,128)(2,1)} %param.15) | copy-start | bytes 7077892
  167.8 195.5 %copy-start.2 = (s32[128,2]{0,1:T(2,128)S(1)}, s32[128,2]{0,1:T(2,128)}, u32[]{:S(2)}) copy-start(s32[128,2]{0,1:T(2,128)} %param.11) | copy-start | bytes 3076
  167.9 195.5 %copy-start.3 = (f32[128,2]{0,1:T(2,128)S(1)}, f32[128,2]{0,1:T(2,128)}, u32[]{:S(2)}) copy-start(f32[128,2]{0,1:T(2,128)} %param.10) | copy-start | bytes 3076

commit v6 on v5

--- a/solution.py
+++ b/solution.py
@@ -9,7 +9,7 @@
 BF = jnp.bfloat16
 F32 = jnp.float32
 MIB = 1024 * 1024
-DISPATCH_VMEM, FRONT_VMEM, SORT_VMEM = 60 * MIB, 12 * MIB, 12 * MIB
+DISPATCH_VMEM, FRONT_VMEM, SORT_VMEM = 20 * MIB, 12 * MIB, 12 * MIB
 REAR_VMEM, COMBINE_VMEM = 12 * MIB, 16 * MIB
 TILE = 512
 
@@ -34,7 +34,7 @@
 
 def dispatch_kernel(
     cap, experts, route_ref, prob_ref, token_ref, cot_ref, out_ref, rows_in, low, high, scale,
-    route, probs, stage, sem, out_sem
+    route, probs, sem
 ):
     tok, width = token_ref.shape
     per = 4 * cap
@@ -75,21 +75,18 @@
     half_width = width // 4
     lot = 16
 
-    tiles = half_width // TILE
-    sends = [
-        pltpu.make_async_copy(
-            stage.at[i], out_ref.at[:, :, :, pl.ds(i * TILE, TILE)], out_sem.at[i]
-        )
-        for i in range(tiles)
-    ]
-    for i in range(tiles):
+
+    def body(i, carry):
         for r in range(2):
             first, second = (
-                rows_in[:, (2 * r + h) * half_width + i * TILE :][:, :TILE] for h in range(2)
+                rows_in[
+                    :, pl.ds(pl.multiple_of((2 * r + h) * half_width + i * TILE, TILE), TILE)
+                ]
+                for h in range(2)
             )
-
-            def body(g, carry):
-                part = pl.ds(pl.multiple_of(g * lot * reach, lot * reach), lot * reach)
+            at = pl.ds(pl.multiple_of(i * TILE, TILE), TILE)
+            for g in range(experts // lot):
+                part = slice(g * lot * reach, (g + 1) * lot * reach)
                 y0 = jnp.dot(low[part, :], first, preferred_element_type=F32)
                 y1 = jnp.dot(high[part, :], second, preferred_element_type=F32)
                 y0 = y0 * scale[0, part, 0:1]
@@ -102,13 +99,10 @@
                         y0[base + mid : base + reach] + y1[base : base + mid],
                         y1[base + mid : base + reach],
                     ]
-                    stage[i, g * lot + j, r] = jnp.concatenate(made, axis=0).astype(BF)
-                return carry
-
-            lax.fori_loop(0, experts // lot, body, 0)
-        sends[i].start()
-    for send in sends:
-        send.wait()
+                    out_ref[g * lot + j, r, :, at] = jnp.concatenate(made, axis=0).astype(BF)
+        return carry
+
+    lax.fori_loop(0, half_width // TILE, body, 0)
 
 
 def dispatch(routes, probs, tokens, cotangent, experts, cap):
@@ -116,11 +110,11 @@
     half = width // 4
     per = 4 * cap
     rows = experts * per * 2 // 3
-    anywhere = pl.BlockSpec(memory_space=pltpu.HBM)
+    anywhere = pl.BlockSpec(memory_space=pl.ANY)
     return pl.pallas_call(
         functools.partial(dispatch_kernel, cap, experts),
         in_specs=[anywhere] * 4,
-        out_specs=anywhere,
+        out_specs=held(),
         out_shape=jax.ShapeDtypeStruct((experts, 2, per, half), BF),
         scratch_shapes=[
             pltpu.VMEM((2 * tok, width), BF),
@@ -129,9 +123,7 @@
             pltpu.VMEM((2, rows, 128), F32),
             pltpu.VMEM((2, tok), jnp.int32),
             pltpu.VMEM((2, tok), F32),
-            pltpu.VMEM((half // TILE, experts, 2, per, TILE), BF),
             pltpu.SemaphoreType.DMA((4,)),
-            pltpu.SemaphoreType.DMA((half // TILE,)),
         ],
         compiler_params=pltpu.CompilerParams(vmem_limit_bytes=DISPATCH_VMEM),
         cost_estimate=pl.CostEstimate(
@@ -141,7 +133,7 @@
     )(routes, probs, tokens, cotangent)
 
 
-def order_matrix(group, cap, inverse):
+def order_matrix(group, cap, inverse, paired=False):
     n = group * cap * 4
     i = lax.broadcasted_iota(jnp.int32, (n, n), 1 if inverse else 0)
     j = lax.broadcasted_iota(jnp.int32, (n, n), 0 if inverse else 1)
@@ -149,6 +141,9 @@
     rest = i - hk * (group * cap)
     src = rest // cap
     slot = rest - src * cap
+    if paired:
+        part = src // (group // 2)
+        src = 2 * (src - part * (group // 2)) + part
     return jnp.where(src * (4 * cap) + hk * cap + slot == j, 1.0, 0.0).astype(BF)
 
 
@@ -352,64 +347,69 @@
 
 
 def combine_kernel(
-    cap, group, experts, route_ref, prob_ref, back_ref, mixed_ref, grad_ref, stage, pick, both
+    cap, group, experts, route_ref, prob_ref, back_ref, mixed_ref, grad_ref, stage, pick, both,
+    mixed, grads, sem
 ):
     sources, _, per, tile = back_ref.shape
-    tok, width = mixed_ref.shape
+    tok, width = mixed.shape
     half = width // 4
-    n = group * cap
-    rows = sources * cap
-    fore = order_matrix(group, cap, False)
+    tiles = half // tile
+    m = group // 2 * cap
+    rows = experts * cap
+    fore = order_matrix(group, cap, False, True)
     slot0, slot1 = slots_of(route_ref[...], experts, cap)
     prob0, prob1 = column(prob_ref[0:1, :]), column(prob_ref[1:2, :])
-    r = lax.broadcasted_iota(jnp.int32, (tok, rows), 1)
-    source = r // cap
-    expert = source // 2
-    ident = expert * cap + r - source * cap
-    part = source - 2 * expert
+    ident = lax.broadcasted_iota(jnp.int32, (tok, rows), 1)
     hit0 = ident == column(slot0)
     hit1 = ident == column(slot1)
-    for k in range(2):
-        here = part == k
-        at = 2 * k * tok
-        pick[at : at + tok, :] = jnp.where(hit0 & here, 1.0, 0.0).astype(BF)
-        pick[at + tok : at + 2 * tok, :] = jnp.where(hit1 & here, 1.0, 0.0).astype(BF)
-        both[k * tok : (k + 1) * tok, :] = jnp.where((hit0 | hit1) & here, 1.0, 0.0).astype(BF)
-
-    def body(i, carry):
+    pick[:tok, :] = jnp.where(hit0, 1.0, 0.0).astype(BF)
+    pick[tok:, :] = jnp.where(hit1, 1.0, 0.0).astype(BF)
+    both[...] = jnp.where(hit0 | hit1, 1.0, 0.0).astype(BF)
+    sends = []
+    for i in range(tiles):
         for g in range(sources // group):
             block = back_ref[g * group : (g + 1) * group, i].reshape(group * per, tile)
-            got = jnp.dot(fore, block, preferred_element_type=F32).astype(BF)
+            got = jnp.dot(fore, block, preferred_element_type=F32)
             for k in range(4):
-                stage[k, g * n : (g + 1) * n, :] = got[k * n : (k + 1) * n]
-        for h in range(2):
-            out = jnp.dot(pick[...], stage[2 * h], preferred_element_type=F32)
-            grad = jnp.dot(both[...], stage[2 * h + 1], preferred_element_type=F32)
-            for k in range(2):
-                to = pl.ds(pl.multiple_of((2 * k + h) * half + i * tile, tile), tile)
-                one = out[2 * k * tok : (2 * k + 1) * tok]
-                two = out[(2 * k + 1) * tok : (2 * k + 2) * tok]
-                mixed_ref[:, to] = (one * prob0 + two * prob1).astype(BF)
-                grad_ref[:, to] = grad[k * tok : (k + 1) * tok].astype(BF)
-        return carry
-
-    lax.fori_loop(0, half // tile, body, 0)
+                for r in range(2):
+                    at = (2 * k + r) * m
+                    stage[k, r, g * m : (g + 1) * m, :] = got[at : at + m].astype(BF)
+        for r in range(2):
+            for h in range(2):
+                to = slice((2 * r + h) * half + i * tile, (2 * r + h) * half + (i + 1) * tile)
+                out = jnp.dot(pick[...], stage[2 * h, r], preferred_element_type=F32)
+                grad = jnp.dot(both[...], stage[2 * h + 1, r], preferred_element_type=F32)
+                mixed[:, to] = (out[:tok] * prob0 + out[tok:] * prob1).astype(BF)
+                grads[:, to] = grad.astype(BF)
+                for k, (source, target) in enumerate(((mixed, mixed_ref), (grads, grad_ref))):
+                    at = pl.ds(to.start, tile)
+                    send = pltpu.make_async_copy(
+                        source.at[:, at], target.at[:, at], sem.at[k, len(sends) // 2]
+                    )
+                    send.start()
+                    sends.append(send)
+    for send in sends:
+        send.wait()
 
 
 def combine(routes, probs, back, experts, cap):
     sources, slabs, _, tile = back.shape
-    rows = sources * cap
+    rows = experts * cap
     tok = routes.shape[1]
-    shape = jax.ShapeDtypeStruct((tok, 4 * (slabs - 3) * tile), BF)
+    width = 4 * (slabs - 3) * tile
+    shape = jax.ShapeDtypeStruct((tok, width), BF)
     return pl.pallas_call(
         functools.partial(combine_kernel, cap, GROUP, experts),
         in_specs=[held()] * 3,
-        out_specs=[held(), held()],
+        out_specs=[pl.BlockSpec(memory_space=pl.ANY)] * 2,
         out_shape=[shape, shape],
         scratch_shapes=[
-            pltpu.VMEM((4, rows, tile), BF),
-            pltpu.VMEM((4 * tok, rows), BF),
+            pltpu.VMEM((4, 2, rows, tile), BF),
             pltpu.VMEM((2 * tok, rows), BF),
+            pltpu.VMEM((tok, rows), BF),
+            pltpu.VMEM((tok, width), BF),
+            pltpu.VMEM((tok, width), BF),
+            pltpu.SemaphoreType.DMA((2, width // tile)),
         ],
         compiler_params=pltpu.CompilerParams(vmem_limit_bytes=COMBINE_VMEM),
         cost_estimate=pl.CostEstimate(
@@ -419,16 +419,16 @@
     )(routes, probs, back)
 
 
-def reorder_kernel(order_ref, source, out):
-    def body(j, carry):
+def reorder_kernel(place_ref, source, out):
+    def body(e, carry):
         for r in range(2):
-            out[2 * j + r] = source[2 * order_ref[j] + r, -3:]
+            out[2 * place_ref[e] + r] = source[2 * e + r, -3:]
         return carry
 
     lax.fori_loop(0, out.shape[0] // 2, body, 0)
 
 
-def reorder(array, inverse):
+def reorder(array, placement):
     sources, _, piece, columns = array.shape
     return pl.pallas_call(
         reorder_kernel,
@@ -440,7 +440,7 @@
             flops=0, bytes_accessed=12 * sources * piece * columns, transcendentals=0
         ),
         name="reorder",
-    )(inverse, array)
+    )(placement, array)
 
 
 def swap(array, axes):
@@ -487,16 +487,11 @@
     together = lax.optimization_barrier
 
     place = rank.reshape(1).astype(jnp.int32)
-    labels = jnp.arange(experts, dtype=jnp.int32)
-    inverse = jnp.sum(
-        labels[None, :] * (placement[None, :] == labels[:, None]).astype(jnp.int32), axis=1
-    )
-    inverse = jnp.minimum(inverse, experts - 1)
     send = dispatch(routes.T, gate_probs.T, tokens, cotangent, experts, cap)
-    send, inverse, place = together((send, inverse, place))
+    send, place = together((send, place))
     recv = swap(send.reshape(-1, width // 4), both)
     weight = weight.reshape(2, 2, rows // 2, columns)
-    recv, inverse, place = together((recv, inverse, place))
+    recv, place = together((recv, place))
     own0, out0 = front_call(place, recv, weight, cap, 0)
     own1, out1 = front_call(place, recv, weight, cap, 1)
     other = [lax.ppermute(out, "dp", [(0, 1), (1, 0)]) for out in (out0, out1)]
@@ -505,9 +500,8 @@
     sent = rear_call(
         place, x, c, [own0, own1], other, weight, first_moment[0], second_moment[0], cap, piece
     )
-    sent, inverse = together((sent, inverse))
     back = swap(sent.reshape(-1, columns), both).reshape(sent.shape)
-    ready = reorder(back, inverse)
+    ready = reorder(back, placement)
     mixed, token_grad = combine(routes.T, gate_probs.T, back, experts, cap)
     ready, mixed, token_grad = together((ready, mixed, token_grad))
     moved = swap(ready.reshape(-1, columns), both).reshape(ready.shape)

time: 471 us -> 465 us (0.987)
  Pallas kernels: 48.1 us -> 38.2 us
    pallas_call x1, Pallas kernels: 11.2 us -> 4.76 us  [dispatch(): pl.pallas_call(functools.partial(dispatch_kernel, cap, experts), in_specs...]
where the time goes in v6:
time: 465 us; the launch traced here: 463 us
  blocking collectives  406 us (87%)
  Pallas kernels  38.2 us (8%)
  waiting for transfers between devices  9.64 us (2%)
    all_to_all x3, blocking collectives, swap(): return lax.all_to_all(array, axes, split_axis=0, concat_axis=0, tiled=True)  406 us
    pallas_call x1, Pallas kernels, rear_call(): pl.pallas_call(functools.partial(rear_kernel, cap, GROUP, piece), in_spec...  12.1 us
    ppermute x2, waiting for transfers between devices, local(): other = [lax.ppermute(out, 'dp', [(0, 1), (1, 0)]) for out in (out0, out1)]  9.64 us
  transfers between devices with their start and end apart: 2, of which 2 were waited for; matrix products, arithmetic and copies ran while one was open for 0% of the time, Pallas kernels for 1%

profile of v6, /device:TPU:6, one launch (start us, length us, event | category | flops | bytes accessed | tf_op | source)
XLA Modules:
  0.0 462.9 jit_solution(5795709731112868749)
XLA Ops:
  0.6 0.0 copy-start.2
  0.6 1.4 copy-done.2
  2.0 0.0 copy-start.3
  2.0 1.4 copy-done.3
  3.5 0.0 copy-start.4
  3.5 0.7 copy-done.4
  4.1 0.7 copy-done.6
  4.8 4.8 %dispatch.1 = bf16[64,2,24,1536]{3,2,1,0:T(8,128)(2,1)S(1)} custom-call(s32[2,128]{1,0:T(2,128)S(1)} %bitcast.31, f32[2,128]{1,0:T(2,128)S(1)} %bitcast.33, bf16[128,6144]{1,0:T(8,128)(2,1)S(1)} %copy-done.2, bf16[128,6144]{1,0:T(8,128)(2,1)S(1)} %copy-done.3), custom_call_target="tpu_custom_call" | custom-call | flops 3000000000 | bytes 13631488 | tf_op jit(solution)/shard_map/dispatch/pallas_call | solution.py:114
  9.6 0.0 slice-start.1
  9.6 120.2 %all_to_all.30 = bf16[128,24,1536]{2,1,0:T(8,128)(2,1)S(1)} all-to-all(bf16[128,24,1536]{2,1,0:T(8,128)(2,1)S(1)} %bitcast.26), channel_id=1, replica_groups=mesh['expert'=64,'dp'=2] {'expert','dp'}, dimensions={0} | all-to-all | bytes 18874368 | tf_op jit(solution)/shard_map/all_to_all | solution.py:447
  129.8 0.0 slice-done
  129.8 0.0 slice-done.1
  129.8 3.2 expert_front.3
  133.0 3.2 expert_front.2
  136.2 0.8 collective-permute-start
  137.0 2.8 collective-permute-start.1
  139.8 3.1 sort_rows.1
  142.8 4.9 %collective-permute-done.other0 = bf16[384,384]{1,0:T(8,128)(2,1)S(1)} collective-permute-done((bf16[384,384]{1,0:T(8,128)(2,1)S(1)}, bf16[384,384]{1,0:T(8,128)(2,1)S(1)}, u32[]{:S(2)}, u32[]{:S(2)}) %collective-permute-start) | collective-permute-done | bytes 294944 | tf_op jit(solution)/shard_map/ppermute | solution.py:497
  147.7 4.8 %collective-permute-done.1.other1 = bf16[384,384]{1,0:T(8,128)(2,1)S(1)} collective-permute-done((bf16[384,384]{1,0:T(8,128)(2,1)S(1)}, bf16[384,384]{1,0:T(8,128)(2,1)S(1)}, u32[]{:S(2)}, u32[]{:S(2)}) %collective-permute-start.1) | collective-permute-done | bytes 294944 | tf_op jit(solution)/shard_map/ppermute | solution.py:497
  152.5 0.0 copy-done
  152.5 0.0 copy-done.1
  152.5 12.1 %expert_rear.1 = bf16[128,7,24,384]{3,2,1,0:T(8,128)(2,1)S(1)} custom-call(s32[1]{0:T(128)} %bitcast.2.rank_ref, bf16[2,768,1536]{2,1,0:T(8,128)(2,1)S(1)} %get-tuple-element.31.x_ref, bf16[2,768,1536]{2,1,0:T(8,128)(2,1)S(1)} %get-tuple-element.32.c_ref, f32[384,384]{1,0:T(8,128)S(1)} %get-tuple-element.33.own0, f32[384,384]{1,0:T(8,128)S(1)} %get-tuple-element.34.own1, ...), custom_call_target="tpu_custom_call" | custom-call | flops 7000000000 | bytes 37748736 | tf_op jit(solution)/shard_map/expert_rear/pallas_call | solution.py:324
  164.6 0.0 copy-start.5
  164.6 0.0 copy-start.7
  164.6 195.5 %all_to_all.31 = bf16[128,168,384]{2,1,0:T(8,128)(2,1)S(1)} all-to-all(bf16[128,168,384]{2,1,0:T(8,128)(2,1)S(1)} %bitcast.18), channel_id=1, replica_groups=mesh['expert'=64,'dp'=2] {'expert','dp'}, dimensions={0} | all-to-all | bytes 33030144 | tf_op jit(solution)/shard_map/all_to_all | solution.py:447
  360.1 0.0 copy-done.5
  360.1 0.0 copy-done.7
  360.1 7.5 %combine.1 = (bf16[128,6144]{1,0:T(8,128)(2,1)}, bf16[128,6144]{1,0:T(8,128)(2,1)}) custom-call(s32[2,128]{1,0:T(2,128)S(1)} %bitcast.32, f32[2,128]{1,0:T(2,128)S(1)} %bitcast.34, bf16[128,7,24,384]{3,2,1,0:T(8,128)(2,1)S(1)} %bitcast.19), custom_call_target="tpu_custom_call" | custom-call | flops 6000000000 | bytes 13631488 | tf_op jit(solution)/shard_map/combine/pallas_call | solution.py:401
  367.6 0.0 copy-done.8
  367.6 1.5 reorder.1
  369.1 90.7 %all_to_all.32 = bf16[128,72,384]{2,1,0:T(8,128)(2,1)S(1)} all-to-all(bf16[128,72,384]{2,1,0:T(8,128)(2,1)S(1)} %bitcast.28), channel_id=1, replica_groups=mesh['expert'=64,'dp'=2] {'expert','dp'}, dimensions={0} | all-to-all | bytes 14155776 | tf_op jit(solution)/shard_map/all_to_all | solution.py:447
  459.7 3.0 split.1
  (6 shorter events, 0.0 us)
Async XLA Ops:
  0.6 1.4 copy-start.2
  2.0 1.4 copy-start.3
  3.5 0.7 copy-start.4
  4.1 0.7 copy-start.6
  4.8 125.0 %slice-start = ((s8[4718592]{0:T(1024)(128)(4,1)}), s8[4194304]{0:T(1024)(128)(4,1)S(1)}, s32[]{:S(2)}) async-start(s8[4718592]{0:T(1024)(128)(4,1)} %bitcast.21), calls=%async_computation.3 | async-start | bytes 8388608
  9.6 120.2 %slice-start.1 = ((s8[4718592]{0:T(1024)(128)(4,1)}), s8[524288]{0:T(1024)(128)(4,1)S(1)}, s32[]{:S(2)}) async-start(s8[4718592]{0:T(1024)(128)(4,1)} %bitcast.21), calls=%async_computation.4 | async-start | bytes 1048576
  136.2 11.5 %collective-permute-start = (bf16[384,384]{1,0:T(8,128)(2,1)S(1)}, bf16[384,384]{1,0:T(8,128)(2,1)S(1)}, u32[]{:S(2)}, u32[]{:S(2)}) collective-permute-start(bf16[384,384]{1,0:T(8,128)(2,1)S(1)} %get-tuple-element.35), channel_id=1, source_target_pairs={{0,1},{1,0},{2,3},{3,2},{4,5},{5,4},{6,7},{7,6},{8,9},{9,8},{10,11... | collective-permute-start | bytes 884744 | tf_op jit(solution)/shard_map/ppermute | solution.py:497
  137.0 15.5 %collective-permute-start.1 = (bf16[384,384]{1,0:T(8,128)(2,1)S(1)}, bf16[384,384]{1,0:T(8,128)(2,1)S(1)}, u32[]{:S(2)}, u32[]{:S(2)}) collective-permute-start(bf16[384,384]{1,0:T(8,128)(2,1)S(1)} %get-tuple-element.36), channel_id=1, source_target_pairs={{0,1},{1,0},{2,3},{3,2},{4,5},{5,4},{6,7},{7,6},{8,9},{9,8},{10,11... | collective-permute-start | bytes 884744 | tf_op jit(solution)/shard_map/ppermute | solution.py:497
  139.8 12.7 %copy-start = (bf16[1,3072,384]{2,1,0:T(8,128)(2,1)S(1)}, bf16[1,3072,384]{2,1,0:T(8,128)(2,1)}, u32[]{:S(2)}) copy-start(bf16[1,3072,384]{2,1,0:T(8,128)(2,1)} %param.14) | copy-start | bytes 7077892
  139.8 12.7 %copy-start.1 = (bf16[1,3072,384]{2,1,0:T(8,128)(2,1)S(1)}, bf16[1,3072,384]{2,1,0:T(8,128)(2,1)}, u32[]{:S(2)}) copy-start(bf16[1,3072,384]{2,1,0:T(8,128)(2,1)} %param.15) | copy-start | bytes 7077892
  164.6 195.5 %copy-start.5 = (s32[128,2]{0,1:T(2,128)S(1)}, s32[128,2]{0,1:T(2,128)}, u32[]{:S(2)}) copy-start(s32[128,2]{0,1:T(2,128)} %param.11) | copy-start | bytes 3076
  164.6 195.5 %copy-start.7 = (f32[128,2]{0,1:T(2,128)S(1)}, f32[128,2]{0,1:T(2,128)}, u32[]{:S(2)}) copy-start(f32[128,2]{0,1:T(2,128)} %param.10) | copy-start | bytes 3076
  360.1 7.5 %copy-start.8 = (s32[64]{0:T(128)S(1)}, s32[64]{0:T(128)}, u32[]{:S(2)}) copy-start(s32[64]{0:T(128)} %place_ref.1) | copy-start | bytes 772

commit v7 on v6

--- a/solution.py
+++ b/solution.py
@@ -303,7 +303,8 @@
                 )
                 m = 0.9 * first_ref[h, cols, at].astype(F32) + 0.1 * grad
                 v = 0.95 * second_ref[h, cols, at].astype(F32) + 0.05 * grad * grad
-                step = m / (jnp.sqrt(v) + 1e-08) + 0.1 * w_ref[rank, h, cols, at].astype(F32)
+                scale = pl.reciprocal(v * lax.rsqrt(v) + 1e-08)
+                step = m * scale + 0.1 * w_ref[rank, h, cols, at].astype(F32)
                 count = tile // piece
                 for k, value in enumerate((m, v, step)):
                     for j in range(count):
@@ -493,10 +494,11 @@
     weight = weight.reshape(2, 2, rows // 2, columns)
     recv, place = together((recv, place))
     own0, out0 = front_call(place, recv, weight, cap, 0)
+    recv, own0 = together((recv, own0))
+    x, c = sort_call(recv, cap)
+    recv, x = together((recv, x))
     own1, out1 = front_call(place, recv, weight, cap, 1)
     other = [lax.ppermute(out, "dp", [(0, 1), (1, 0)]) for out in (out0, out1)]
-    recv, own1 = together((recv, own1))
-    x, c = sort_call(recv, cap)
     sent = rear_call(
         place, x, c, [own0, own1], other, weight, first_moment[0], second_moment[0], cap, piece
     )

time: 465 us -> 464 us (level)
  transfers between devices with their start and end apart: 2 -> 2, of which waited for: 2 -> 1; matrix products, arithmetic and copies ran while one was open for 0% -> 0% of each run, Pallas kernels for 1% -> 1%
where the time goes in v7:
time: 464 us; the launch traced here: 462 us
  blocking collectives  408 us (88%)
  Pallas kernels  37.5 us (8%)
  waiting for transfers between devices  7.65 us (2%)
    all_to_all x3, blocking collectives, swap(): return lax.all_to_all(array, axes, split_axis=0, concat_axis=0, tiled=True)  408 us
    pallas_call x1, Pallas kernels, rear_call(): pl.pallas_call(functools.partial(rear_kernel, cap, GROUP, piece), in_spec...  11.4 us
  transfers between devices with their start and end apart: 2, of which 1 were waited for; matrix products, arithmetic and copies ran while one was open for 0% of the time, Pallas kernels for 1%

profile of v7, /device:TPU:6, one launch (start us, length us, event | category | flops | bytes accessed | tf_op | source)
XLA Modules:
  0.0 461.6 jit_solution(12186328778945272607)
XLA Ops:
  0.6 0.0 copy-start.2
  0.6 1.4 copy-done.2
  2.0 1.4 copy-done.3
  3.5 0.7 copy-done.4
  4.1 0.7 copy-done.6
  4.8 4.8 %dispatch.1 = bf16[64,2,24,1536]{3,2,1,0:T(8,128)(2,1)S(1)} custom-call(s32[2,128]{1,0:T(2,128)S(1)} %bitcast.31, f32[2,128]{1,0:T(2,128)S(1)} %bitcast.33, bf16[128,6144]{1,0:T(8,128)(2,1)S(1)} %copy-done.2, bf16[128,6144]{1,0:T(8,128)(2,1)S(1)} %copy-done.3), custom_call_target="tpu_custom_call" | custom-call | flops 3000000000 | bytes 13631488 | tf_op jit(solution)/shard_map/dispatch/pallas_call | solution.py:114
  9.6 0.0 slice-start.1
  9.6 120.2 %all_to_all.30 = bf16[128,24,1536]{2,1,0:T(8,128)(2,1)S(1)} all-to-all(bf16[128,24,1536]{2,1,0:T(8,128)(2,1)S(1)} %bitcast.26), channel_id=1, replica_groups=mesh['expert'=64,'dp'=2] {'expert','dp'}, dimensions={0} | all-to-all | bytes 18874368 | tf_op jit(solution)/shard_map/all_to_all | solution.py:448
  129.8 0.0 slice-done
  129.8 0.0 slice-done.1
  129.8 3.2 expert_front.2
  133.0 0.8 collective-permute-start
  133.8 3.1 sort_rows.1
  136.9 0.0 copy-start
  136.9 0.0 copy-start.1
  136.9 3.2 expert_front.3
  140.1 2.9 collective-permute-start.1
  142.9 0.0 collective-permute-done.other0
  143.0 7.6 %collective-permute-done.1.other1 = bf16[384,384]{1,0:T(8,128)(2,1)S(1)} collective-permute-done((bf16[384,384]{1,0:T(8,128)(2,1)S(1)}, bf16[384,384]{1,0:T(8,128)(2,1)S(1)}, u32[]{:S(2)}, u32[]{:S(2)}) %collective-permute-start.1) | collective-permute-done | bytes 294944 | tf_op jit(solution)/shard_map/ppermute | solution.py:501
  150.6 0.0 copy-done
  150.6 0.0 copy-done.1
  150.6 11.4 %expert_rear.1 = bf16[128,7,24,384]{3,2,1,0:T(8,128)(2,1)S(1)} custom-call(s32[1]{0:T(128)} %bitcast.2.rank_ref, bf16[2,768,1536]{2,1,0:T(8,128)(2,1)S(1)} %get-tuple-element.34.x_ref, bf16[2,768,1536]{2,1,0:T(8,128)(2,1)S(1)} %get-tuple-element.35.c_ref, f32[384,384]{1,0:T(8,128)S(1)} %get-tuple-element.36.own0, f32[384,384]{1,0:T(8,128)S(1)} %get-tuple-element.38.own1, ...), custom_call_target="tpu_custom_call" | custom-call | flops 7000000000 | bytes 37748736 | tf_op jit(solution)/shard_map/expert_rear/pallas_call | solution.py:325
  162.0 0.0 copy-start.5
  162.0 0.0 copy-start.7
  162.0 196.9 %all_to_all.31 = bf16[128,168,384]{2,1,0:T(8,128)(2,1)S(1)} all-to-all(bf16[128,168,384]{2,1,0:T(8,128)(2,1)S(1)} %bitcast.18), channel_id=1, replica_groups=mesh['expert'=64,'dp'=2] {'expert','dp'}, dimensions={0} | all-to-all | bytes 33030144 | tf_op jit(solution)/shard_map/all_to_all | solution.py:448
  358.9 0.0 copy-done.5
  358.9 0.0 copy-done.7
  358.9 7.5 %combine.1 = (bf16[128,6144]{1,0:T(8,128)(2,1)}, bf16[128,6144]{1,0:T(8,128)(2,1)}) custom-call(s32[2,128]{1,0:T(2,128)S(1)} %bitcast.32, f32[2,128]{1,0:T(2,128)S(1)} %bitcast.34, bf16[128,7,24,384]{3,2,1,0:T(8,128)(2,1)S(1)} %bitcast.19), custom_call_target="tpu_custom_call" | custom-call | flops 6000000000 | bytes 13631488 | tf_op jit(solution)/shard_map/combine/pallas_call | solution.py:402
  366.4 0.0 copy-done.8
  366.4 1.5 reorder.1
  367.8 90.7 %all_to_all.32 = bf16[128,72,384]{2,1,0:T(8,128)(2,1)S(1)} all-to-all(bf16[128,72,384]{2,1,0:T(8,128)(2,1)S(1)} %bitcast.28), channel_id=1, replica_groups=mesh['expert'=64,'dp'=2] {'expert','dp'}, dimensions={0} | all-to-all | bytes 14155776 | tf_op jit(solution)/shard_map/all_to_all | solution.py:448
  458.5 3.0 split.1
  (6 shorter events, 0.0 us)
Async XLA Ops:
  0.6 1.4 copy-start.2
  2.0 1.4 copy-start.3
  3.5 0.7 copy-start.4
  4.1 0.7 copy-start.6
  4.8 125.0 %slice-start = ((s8[4718592]{0:T(1024)(128)(4,1)}), s8[4194304]{0:T(1024)(128)(4,1)S(1)}, s32[]{:S(2)}) async-start(s8[4718592]{0:T(1024)(128)(4,1)} %bitcast.21), calls=%async_computation.3 | async-start | bytes 8388608
  9.6 120.2 %slice-start.1 = ((s8[4718592]{0:T(1024)(128)(4,1)}), s8[524288]{0:T(1024)(128)(4,1)S(1)}, s32[]{:S(2)}) async-start(s8[4718592]{0:T(1024)(128)(4,1)} %bitcast.21), calls=%async_computation.4 | async-start | bytes 1048576
  133.0 10.0 %collective-permute-start = (bf16[384,384]{1,0:T(8,128)(2,1)S(1)}, bf16[384,384]{1,0:T(8,128)(2,1)S(1)}, u32[]{:S(2)}, u32[]{:S(2)}) collective-permute-start(bf16[384,384]{1,0:T(8,128)(2,1)S(1)} %get-tuple-element.39), channel_id=1, source_target_pairs={{0,1},{1,0},{2,3},{3,2},{4,5},{5,4},{6,7},{7,6},{8,9},{9,8},{10,11... | collective-permute-start | bytes 884744 | tf_op jit(solution)/shard_map/ppermute | solution.py:501
  136.9 13.7 %copy-start = (bf16[1,3072,384]{2,1,0:T(8,128)(2,1)S(1)}, bf16[1,3072,384]{2,1,0:T(8,128)(2,1)}, u32[]{:S(2)}) copy-start(bf16[1,3072,384]{2,1,0:T(8,128)(2,1)} %param.14) | copy-start | bytes 7077892
  136.9 13.7 %copy-start.1 = (bf16[1,3072,384]{2,1,0:T(8,128)(2,1)S(1)}, bf16[1,3072,384]{2,1,0:T(8,128)(2,1)}, u32[]{:S(2)}) copy-start(bf16[1,3072,384]{2,1,0:T(8,128)(2,1)} %param.15) | copy-start | bytes 7077892
  140.1 10.5 %collective-permute-start.1 = (bf16[384,384]{1,0:T(8,128)(2,1)S(1)}, bf16[384,384]{1,0:T(8,128)(2,1)S(1)}, u32[]{:S(2)}, u32[]{:S(2)}) collective-permute-start(bf16[384,384]{1,0:T(8,128)(2,1)S(1)} %get-tuple-element.40), channel_id=1, source_target_pairs={{0,1},{1,0},{2,3},{3,2},{4,5},{5,4},{6,7},{7,6},{8,9},{9,8},{10,11... | collective-permute-start | bytes 884744 | tf_op jit(solution)/shard_map/ppermute | solution.py:501
  162.0 196.9 %copy-start.5 = (s32[128,2]{0,1:T(2,128)S(1)}, s32[128,2]{0,1:T(2,128)}, u32[]{:S(2)}) copy-start(s32[128,2]{0,1:T(2,128)} %param.11) | copy-start | bytes 3076
  162.0 196.9 %copy-start.7 = (f32[128,2]{0,1:T(2,128)S(1)}, f32[128,2]{0,1:T(2,128)}, u32[]{:S(2)}) copy-start(f32[128,2]{0,1:T(2,128)} %param.10) | copy-start | bytes 3076
  358.9 7.5 %copy-start.8 = (s32[64]{0:T(128)S(1)}, s32[64]{0:T(128)}, u32[]{:S(2)}) copy-start(s32[64]{0:T(128)} %place_ref.1) | copy-start | bytes 772

commit v8 on v7

--- a/solution.py
+++ b/solution.py
@@ -11,7 +11,7 @@
 MIB = 1024 * 1024
 DISPATCH_VMEM, FRONT_VMEM, SORT_VMEM = 20 * MIB, 12 * MIB, 12 * MIB
 REAR_VMEM, COMBINE_VMEM = 12 * MIB, 16 * MIB
-TILE = 512
+TILE = 768
 
 
 def slots_of(route, experts, cap):

time: 464 us -> 463 us (level)
  transfers between devices with their start and end apart: 2 -> 2, of which waited for: 1 -> 2; matrix products, arithmetic and copies ran while one was open for 0% -> 0% of each run, Pallas kernels for 1% -> 1%
where the time goes in v8:
time: 463 us; the launch traced here: 461 us
  blocking collectives  408 us (88%)
  Pallas kernels  36.9 us (8%)
  waiting for transfers between devices  7.64 us (2%)
    all_to_all x3, blocking collectives, swap(): return lax.all_to_all(array, axes, split_axis=0, concat_axis=0, tiled=True)  408 us
    pallas_call x1, Pallas kernels, rear_call(): pl.pallas_call(functools.partial(rear_kernel, cap, GROUP, piece), in_spec...  11.4 us
  transfers between devices with their start and end apart: 2, of which 2 were waited for; matrix products, arithmetic and copies ran while one was open for 0% of the time, Pallas kernels for 1%

profile of v8, /device:TPU:6, one launch (start us, length us, event | category | flops | bytes accessed | tf_op | source)
XLA Modules:
  0.0 461.1 jit_solution(7772340353414178657)
XLA Ops:
  0.6 0.0 copy-start.2
  0.6 1.4 copy-done.2
  2.0 1.4 copy-done.3
  3.5 0.7 copy-done.4
  4.1 0.7 copy-done.6
  4.8 4.6 %dispatch.1 = bf16[64,2,24,1536]{3,2,1,0:T(8,128)(2,1)S(1)} custom-call(s32[2,128]{1,0:T(2,128)S(1)} %bitcast.31, f32[2,128]{1,0:T(2,128)S(1)} %bitcast.33, bf16[128,6144]{1,0:T(8,128)(2,1)S(1)} %copy-done.2, bf16[128,6144]{1,0:T(8,128)(2,1)S(1)} %copy-done.3), custom_call_target="tpu_custom_call" | custom-call | flops 3000000000 | bytes 13631488 | tf_op jit(solution)/shard_map/dispatch/pallas_call | solution.py:114
  9.5 0.0 slice-start.1
  9.5 120.2 %all_to_all.30 = bf16[128,24,1536]{2,1,0:T(8,128)(2,1)S(1)} all-to-all(bf16[128,24,1536]{2,1,0:T(8,128)(2,1)S(1)} %bitcast.26), channel_id=1, replica_groups=mesh['expert'=64,'dp'=2] {'expert','dp'}, dimensions={0} | all-to-all | bytes 18874368 | tf_op jit(solution)/shard_map/all_to_all | solution.py:448
  129.7 0.0 slice-done
  129.7 0.0 slice-done.1
  129.7 3.0 expert_front.2
  132.7 0.8 collective-permute-start
  133.6 2.9 sort_rows.1
  136.5 0.0 copy-start
  136.5 0.0 copy-start.1
  136.5 3.0 expert_front.3
  139.5 2.9 collective-permute-start.1
  142.4 0.3 collective-permute-done.other0
  142.7 7.3 %collective-permute-done.1.other1 = bf16[384,384]{1,0:T(8,128)(2,1)S(1)} collective-permute-done((bf16[384,384]{1,0:T(8,128)(2,1)S(1)}, bf16[384,384]{1,0:T(8,128)(2,1)S(1)}, u32[]{:S(2)}, u32[]{:S(2)}) %collective-permute-start.1) | collective-permute-done | bytes 294944 | tf_op jit(solution)/shard_map/ppermute | solution.py:501
  150.0 0.0 copy-done
  150.0 0.0 copy-done.1
  150.0 11.4 %expert_rear.1 = bf16[128,7,24,384]{3,2,1,0:T(8,128)(2,1)S(1)} custom-call(s32[1]{0:T(128)} %bitcast.2.rank_ref, bf16[2,768,1536]{2,1,0:T(8,128)(2,1)S(1)} %get-tuple-element.34.x_ref, bf16[2,768,1536]{2,1,0:T(8,128)(2,1)S(1)} %get-tuple-element.35.c_ref, f32[384,384]{1,0:T(8,128)S(1)} %get-tuple-element.36.own0, f32[384,384]{1,0:T(8,128)S(1)} %get-tuple-element.38.own1, ...), custom_call_target="tpu_custom_call" | custom-call | flops 7000000000 | bytes 37748736 | tf_op jit(solution)/shard_map/expert_rear/pallas_call | solution.py:325
  161.4 0.0 copy-start.5
  161.4 0.0 copy-start.7
  161.4 196.9 %all_to_all.31 = bf16[128,168,384]{2,1,0:T(8,128)(2,1)S(1)} all-to-all(bf16[128,168,384]{2,1,0:T(8,128)(2,1)S(1)} %bitcast.18), channel_id=1, replica_groups=mesh['expert'=64,'dp'=2] {'expert','dp'}, dimensions={0} | all-to-all | bytes 33030144 | tf_op jit(solution)/shard_map/all_to_all | solution.py:448
  358.3 0.0 copy-done.5
  358.3 0.0 copy-done.7
  358.3 7.5 %combine.1 = (bf16[128,6144]{1,0:T(8,128)(2,1)}, bf16[128,6144]{1,0:T(8,128)(2,1)}) custom-call(s32[2,128]{1,0:T(2,128)S(1)} %bitcast.32, f32[2,128]{1,0:T(2,128)S(1)} %bitcast.34, bf16[128,7,24,384]{3,2,1,0:T(8,128)(2,1)S(1)} %bitcast.19), custom_call_target="tpu_custom_call" | custom-call | flops 6000000000 | bytes 13631488 | tf_op jit(solution)/shard_map/combine/pallas_call | solution.py:402
  365.8 0.0 copy-done.8
  365.8 1.5 reorder.1
  367.3 90.7 %all_to_all.32 = bf16[128,72,384]{2,1,0:T(8,128)(2,1)S(1)} all-to-all(bf16[128,72,384]{2,1,0:T(8,128)(2,1)S(1)} %bitcast.28), channel_id=1, replica_groups=mesh['expert'=64,'dp'=2] {'expert','dp'}, dimensions={0} | all-to-all | bytes 14155776 | tf_op jit(solution)/shard_map/all_to_all | solution.py:448
  457.9 3.0 split.1
  (6 shorter events, 0.0 us)
Async XLA Ops:
  0.6 1.4 copy-start.2
  2.0 1.4 copy-start.3
  3.5 0.7 copy-start.4
  4.1 0.7 copy-start.6
  4.8 124.9 %slice-start = ((s8[4718592]{0:T(1024)(128)(4,1)}), s8[4194304]{0:T(1024)(128)(4,1)S(1)}, s32[]{:S(2)}) async-start(s8[4718592]{0:T(1024)(128)(4,1)} %bitcast.21), calls=%async_computation.3 | async-start | bytes 8388608
  9.5 120.2 %slice-start.1 = ((s8[4718592]{0:T(1024)(128)(4,1)}), s8[524288]{0:T(1024)(128)(4,1)S(1)}, s32[]{:S(2)}) async-start(s8[4718592]{0:T(1024)(128)(4,1)} %bitcast.21), calls=%async_computation.4 | async-start | bytes 1048576
  132.7 10.0 %collective-permute-start = (bf16[384,384]{1,0:T(8,128)(2,1)S(1)}, bf16[384,384]{1,0:T(8,128)(2,1)S(1)}, u32[]{:S(2)}, u32[]{:S(2)}) collective-permute-start(bf16[384,384]{1,0:T(8,128)(2,1)S(1)} %get-tuple-element.39), channel_id=1, source_target_pairs={{0,1},{1,0},{2,3},{3,2},{4,5},{5,4},{6,7},{7,6},{8,9},{9,8},{10,11... | collective-permute-start | bytes 884744 | tf_op jit(solution)/shard_map/ppermute | solution.py:501
  136.5 13.6 %copy-start = (bf16[1,3072,384]{2,1,0:T(8,128)(2,1)S(1)}, bf16[1,3072,384]{2,1,0:T(8,128)(2,1)}, u32[]{:S(2)}) copy-start(bf16[1,3072,384]{2,1,0:T(8,128)(2,1)} %param.14) | copy-start | bytes 7077892
  136.5 13.6 %copy-start.1 = (bf16[1,3072,384]{2,1,0:T(8,128)(2,1)S(1)}, bf16[1,3072,384]{2,1,0:T(8,128)(2,1)}, u32[]{:S(2)}) copy-start(bf16[1,3072,384]{2,1,0:T(8,128)(2,1)} %param.15) | copy-start | bytes 7077892
  139.5 10.5 %collective-permute-start.1 = (bf16[384,384]{1,0:T(8,128)(2,1)S(1)}, bf16[384,384]{1,0:T(8,128)(2,1)S(1)}, u32[]{:S(2)}, u32[]{:S(2)}) collective-permute-start(bf16[384,384]{1,0:T(8,128)(2,1)S(1)} %get-tuple-element.40), channel_id=1, source_target_pairs={{0,1},{1,0},{2,3},{3,2},{4,5},{5,4},{6,7},{7,6},{8,9},{9,8},{10,11... | collective-permute-start | bytes 884744 | tf_op jit(solution)/shard_map/ppermute | solution.py:501
  161.4 196.9 %copy-start.5 = (s32[128,2]{0,1:T(2,128)S(1)}, s32[128,2]{0,1:T(2,128)}, u32[]{:S(2)}) copy-start(s32[128,2]{0,1:T(2,128)} %param.11) | copy-start | bytes 3076
  161.4 196.9 %copy-start.7 = (f32[128,2]{0,1:T(2,128)S(1)}, f32[128,2]{0,1:T(2,128)}, u32[]{:S(2)}) copy-start(f32[128,2]{0,1:T(2,128)} %param.10) | copy-start | bytes 3076
  358.3 7.5 %copy-start.8 = (s32[64]{0:T(128)S(1)}, s32[64]{0:T(128)}, u32[]{:S(2)}) copy-start(s32[64]{0:T(128)} %place_ref.1) | copy-start | bytes 772
